TPU v7x, 32 devices: a whole 2x2x4 slice. The times are simulated.
32 devices in a mesh: shots: 4 (over y, x), space: 8 (over z, core).
Axes of the slice: x: 2, y: 2, z: 4, core: 2. Of those that a mesh axis runs over, the one named last changes fastest.
Arguments:
- probes: bfloat16 [8, 64, 2, 128, 8, 128], P('shots', None, None, 'space'), may hold values from -6 to 6
- sources: bfloat16 [8, 2, 128, 8, 128], P('shots', None, 'space'), may hold values from -6 to 6
- sketch: bfloat16 [32, 64, 64], P('space'), may hold values from -6 to 6
- pairing: int32 [8], replicated, may hold values from 0 to 7, each once
Outputs:
- basis: bfloat16 [32, 64, 64], P('space', 'shots')
Inputs may be any that keep to these rules, and one draw needn't show every extreme that they name: `pairing`: a permutation of the 8 shot groups.
All inputs are finite; a program needn't handle non-finite values.
Results may differ from a plain program's by a relative error of at most 0.013.
Values may be sent and summed in bfloat16 or wider, within the bound.
No kernel may reach another device: no remote copies, remote signals or barrier semaphores. Data moves between devices by JAX's collectives and lax.ppermute only.
A program may use at most 64 MiB of HBM per device.

v0:
```python
import math

import jax
import jax.numpy as jnp
from jax import lax
from jax.sharding import PartitionSpec as P


def from_behind(x, axis, by):
    count = lax.axis_size(axis)
    pairs = [(i, i + by) for i in range(count) if 0 <= i + by < count]
    return lax.ppermute(x, axis, pairs)


def from_partner(value, axis, distance):
    mask = 2**distance
    pairs = [(source, source ^ mask) for source in range(lax.axis_size(axis))]
    return lax.ppermute(value, axis, pairs)


def spline_table(fine_count, coarse_count, fine_start, coarse_start):
    fine_pos = jnp.arange(fine_count, dtype=jnp.float32) + fine_start
    coarse_pos = jnp.arange(coarse_count, dtype=jnp.float32) + coarse_start
    distance = jnp.abs((fine_pos[:, None] + 0.5 - 4.0 * coarse_pos[None, :] - 2.0) / 4.0)
    inner_part = 2.0 / 3.0 - distance**2 + 0.5 * distance**3
    outer_part = jnp.maximum(2.0 - distance, 0.0) ** 3 / 6.0
    return jnp.where(distance < 1.0, inner_part, outer_part) / 4.0


def solve_coef(gram_mats, cross_mats):
    rank_size = gram_mats.shape[-1]
    trace_sum = jnp.trace(gram_mats, axis1=1, axis2=2)
    ridge_term = 0.01 * trace_sum / rank_size + 1e-06
    identity = jnp.eye(rank_size, dtype=jnp.float32)
    factor = jnp.linalg.cholesky(gram_mats + ridge_term[:, None, None] * identity)
    halfway = lax.linalg.triangular_solve(factor, cross_mats, left_side=True, lower=True)
    return lax.linalg.triangular_solve(
        factor, halfway, left_side=True, lower=True, transpose_a=True
    )


def merge_level(pieces, sketch, scaling):
    gram_mats = jnp.einsum("pxay,pxby->pab", pieces, pieces, preferred_element_type=jnp.float32)
    cross_mats = jnp.einsum("pxay,xby->pab", pieces, sketch, preferred_element_type=jnp.float32)
    gram_mats, cross_mats = lax.psum((gram_mats, cross_mats), "space")
    coefficients = solve_coef(gram_mats, cross_mats).astype(jnp.bfloat16)
    term_sums = jnp.einsum(
        "pxay,pab->pxby", pieces, coefficients, preferred_element_type=jnp.float32
    )
    pair_count = pieces.shape[0] // 2
    term_sums = term_sums.reshape((pair_count, 2) + term_sums.shape[1:])
    return (scaling * (term_sums[:, 0] + term_sums[:, 1])).astype(jnp.bfloat16)


def body(probes, sources, sketch, pairing):
    hi = lax.Precision.HIGHEST
    groups, rank_size, steps_t, fine_x, fine_y, fine_z = probes.shape
    coarse_x = fine_x // 4
    coarse_y = fine_y // 4
    coarse_z = fine_z // 4
    images = jnp.einsum("gatxyz,gtxyz->gaxyz", probes, sources, preferred_element_type=jnp.float32)
    images = jnp.einsum(
        "gaxyz,zc->gaxyc", images, spline_table(fine_z, coarse_z, 0, 0), precision=hi
    )
    images = jnp.einsum(
        "gaxyc,yd->gaxdc", images, spline_table(fine_y, coarse_y, 0, 0), precision=hi
    )
    images = images.reshape(groups, rank_size, fine_x, coarse_y * coarse_z)
    table_x = spline_table(fine_x, coarse_x + 4, 0, -2)
    partial_sums = jnp.einsum("gaxc,xe->gaec", images, table_x, precision=hi)
    from_above = from_behind(partial_sums[:, :, :2], "space", -1)
    from_below = from_behind(partial_sums[:, :, coarse_x + 2 :], "space", 1)
    coarse = partial_sums[:, :, 2 : coarse_x + 2]
    coarse = coarse + jnp.pad(from_below, ((0, 0), (0, 0), (0, coarse_x - 2), (0, 0)))
    coarse = coarse + jnp.pad(from_above, ((0, 0), (0, 0), (coarse_x - 2, 0), (0, 0)))
    leaves = jnp.transpose(coarse, (0, 2, 1, 3)).astype(jnp.bfloat16)
    gathered = lax.all_gather(leaves, "shots", axis=0, tiled=True)
    cell_count = coarse_x * lax.axis_size("space") * coarse_y * coarse_z
    scaling = math.sqrt(cell_count / rank_size)
    shot_index = lax.axis_index("shots")
    first_slot = shot_index * groups
    chosen_ids = lax.dynamic_slice_in_dim(pairing, first_slot, groups)
    chosen = jnp.take(gathered, chosen_ids, axis=0)
    merged = merge_level(chosen, sketch, scaling)[0]
    for bit_number in range(lax.axis_size("shots").bit_length() - 1):
        partner_piece = from_partner(merged, "shots", bit_number)
        upper_bit = shot_index // (1 << bit_number) % 2
        low_piece = jnp.where(upper_bit == 1, partner_piece, merged)
        high_piece = jnp.where(upper_bit == 1, merged, partner_piece)
        merged = merge_level(jnp.stack([low_piece, high_piece]), sketch, scaling)[0]
    column_count = rank_size // lax.axis_size("shots")
    column_start = shot_index * column_count
    return lax.dynamic_slice_in_dim(merged, column_start, column_count, 1)


def solution(mesh):
    in_specs = (
        P("shots", None, None, "space", None, None),
        P("shots", None, "space", None, None),
        P("space", None, None),
        P(),
    )
    out_specs = P("space", "shots", None)
    return jax.shard_map(body, mesh=mesh, in_specs=in_specs, out_specs=out_specs, check_vma=False)
```

profile of v0, /device:TPU:0, one launch (start us, length us, event | category | flops | bytes accessed | tf_op | source)
XLA Modules:
  0.0 335.7 jit_solution(8425603574013189461)
XLA Ops:
  6.6 0.9 bitcast_convert_fusion
  7.5 10.0 %multiply_reduce_fusion = f32[2,16,8,128,64]{3,2,1,4,0:T(8,128)} fusion(f32[2,16,8,128,2]{3,2,1,4,0:T(8,128)S(1)} %bitcast_convert_fusion, bf16[2,64,2,16,8,128]{5,4,3,2,1,0:T(8,128)(2,1)} %param.9), kind=kLoop, calls=%fused_computation.1 | loop fusion | flops 10485760 | bytes 17039360
  17.6 28.1 %fusion = f32[2,64,16,8,32]{1,4,3,2,0:T(8,128)S(1)} fusion(f32[2,16,8,128,64]{3,2,1,4,0:T(8,128)} %multiply_reduce_fusion, f32[32]{0:T(128)S(1)} %iota_multiply_fusion, f32[128]{0:T(128)S(1)} %iota_add_fusion), kind=kOutput, calls=%fused_computation.2 | convolution fusion | flops 805376000 | bytes 10486400 | tf_op jit(solution)/shard_map/gaxyz,zc->gaxyc/dot_general | solution.py:62
  45.6 5.5 %fusion.5 = f32[2,64,16,2,32]{1,3,4,2,0:T(2,128)S(1)} fusion(f32[2,64,16,8,32]{1,4,3,2,0:T(8,128)S(1)} %fusion, f32[8]{0:T(128)S(1)} %iota_add_fusion.1, f32[2]{0:T(128)S(1)} %iota_multiply_fusion.1), kind=kOutput, calls=%fused_computation.7 | convolution fusion | flops 12583184 | bytes 2621480 | tf_op jit(solution)/shard_map/gaxyc,yd->gaxdc/dot_general | solution.py:65
  51.1 0.1 copy.51
  51.3 0.5 copy.52
  51.8 0.6 convolution_bitcast_fusion
  52.4 0.1 fusion.144
  52.5 1.3 collective-permute-start.1
  53.8 3.0 collective-permute-start
  56.9 0.1 compare_and_fusion
  57.0 0.8 collective-permute-done
  57.8 0.2 fusion.17
  58.0 12.6 %all_gather.3 = bf16[8,4,64,64]{3,2,1,0:T(8,128)(2,1)S(1)} all-gather(bf16[2,4,64,64]{3,2,1,0:T(8,128)(2,1)S(1)} %copy.53), channel_id=1, replica_groups=mesh['shots'=4,'space'=8] {'shots'}, dimensions={0}, use_global_device_ids=true | all-gather | bytes 327680 | tf_op jit(solution)/shard_map/all_gather | solution.py:77
  70.6 0.6 gather_fusion
  71.2 0.9 convolution_bitcast_fusion.9
  72.1 0.8 convolution_bitcast_fusion.8
  72.9 0.0 all-reduce.11.cloned.1.call-start
  73.0 57.2 %all-reduce.13.cloned.1.call-done = (f32[2,64,64]{2,1,0:T(8,128)}, f32[2,64,64]{1,2,0:T(8,128)}) async-done(((f32[2,64,64]{2,1,0:T(8,128)}, f32[2,64,64]{1,2,0:T(8,128)}), (f32[2,64,64]{2,1,0:T(8,128)}, f32[2,64,64]{1,2,0:T(8,128)})) %all-reduce.13.cloned.1.call-update) | async-done | bytes 65552 | tf_op jit(solution)/shard_map/psum | solution.py:45
  130.2 0.9 select_reduce_fusion.5
  131.2 0.9 multiply_add_fusion.2
  132.1 0.1 copy.55
  132.2 0.9 fusion.34
  133.1 11.7 %custom-call.15 = f32[2,64,64]{2,1,0:T(8,128)S(1)} custom-call(f32[2,64,64]{2,1,0:T(8,128)S(1)} %fusion.34), custom_call_target="Cholesky" | custom-call | tf_op jit(solution)/shard_map/jit(cholesky)/cholesky | solution.py:35
  144.9 0.1 compare_reduce_fusion.2
  145.0 0.1 select_bitcast_fusion.2
  145.1 9.8 %custom-call.17 = f32[2,1,64,64]{2,3,1,0:T(8,128)S(1)} custom-call(f32[2,1,64,64]{3,2,1,0:T(8,128)S(1)} %select_bitcast_fusion.2), custom_call_target="InvertDiagBlocksLowerTriangular" | custom-call | tf_op jit(solution)/shard_map/triangular_solve/custom-call.2 | solution.py:37
  154.9 1.1 fusion.31
  156.1 0.2 fusion.8
  156.3 0.2 convolution_bitcast_fusion.3
  156.5 1.5 collective-permute-start.2
  158.1 2.8 collective-permute-done.2
  160.9 0.8 convolution_bitcast_fusion.6
  161.7 0.8 convolution_bitcast_fusion.7
  162.5 0.0 all-reduce.9.cloned.1.call-start
  162.6 53.5 %all-reduce.11.cloned.1.call-done = (f32[2,64,64]{2,1,0:T(8,128)}, f32[2,64,64]{1,2,0:T(8,128)}) async-done(((f32[2,64,64]{2,1,0:T(8,128)}, f32[2,64,64]{1,2,0:T(8,128)}), (f32[2,64,64]{2,1,0:T(8,128)}, f32[2,64,64]{1,2,0:T(8,128)})) %all-reduce.11.cloned.1.call-update) | async-done | bytes 65552 | tf_op jit(solution)/shard_map/psum | solution.py:45
  216.1 0.9 select_reduce_fusion.4
  217.1 0.9 multiply_add_fusion.1
  218.0 0.1 copy.60
  218.1 0.9 fusion.27
  219.0 12.0 %custom-call.18 = f32[2,64,64]{2,1,0:T(8,128)S(1)} custom-call(f32[2,64,64]{2,1,0:T(8,128)S(1)} %fusion.27), custom_call_target="Cholesky" | custom-call | tf_op jit(solution)/shard_map/jit(cholesky)/cholesky | solution.py:35
  231.0 0.1 compare_reduce_fusion.1
  231.1 0.1 select_bitcast_fusion.1
  231.2 9.8 %custom-call.20 = f32[2,1,64,64]{2,3,1,0:T(8,128)S(1)} custom-call(f32[2,1,64,64]{3,2,1,0:T(8,128)S(1)} %select_bitcast_fusion.1), custom_call_target="InvertDiagBlocksLowerTriangular" | custom-call | tf_op jit(solution)/shard_map/triangular_solve/custom-call.2 | solution.py:37
  241.0 1.1 fusion.24
  242.2 0.2 fusion.9
  242.4 0.2 convolution_bitcast_fusion.2
  242.7 1.5 collective-permute-start.3
  244.2 2.8 collective-permute-done.3
  247.0 0.8 convolution_bitcast_fusion.4
  247.8 0.8 convolution_bitcast_fusion.5
  248.6 53.6 %all-reduce.9.cloned.1.call-done = (f32[2,64,64]{2,1,0:T(8,128)}, f32[2,64,64]{1,2,0:T(8,128)}) async-done(((f32[2,64,64]{2,1,0:T(8,128)}, f32[2,64,64]{1,2,0:T(8,128)}), (f32[2,64,64]{2,1,0:T(8,128)}, f32[2,64,64]{1,2,0:T(8,128)})) %all-reduce.9.cloned.1.call-update) | async-done | bytes 65552 | tf_op jit(solution)/shard_map/psum | solution.py:45
  302.2 0.9 select_reduce_fusion.3
  303.2 0.9 multiply_add_fusion
  304.1 0.1 copy.65
  304.2 0.9 fusion.23
  305.1 11.7 %custom-call.21 = f32[2,64,64]{2,1,0:T(8,128)S(1)} custom-call(f32[2,64,64]{2,1,0:T(8,128)S(1)} %fusion.23), custom_call_target="Cholesky" | custom-call | tf_op jit(solution)/shard_map/jit(cholesky)/cholesky | solution.py:35
  316.9 0.1 compare_reduce_fusion
  317.0 0.1 select_bitcast_fusion
  317.1 9.8 %custom-call.23 = f32[2,1,64,64]{2,3,1,0:T(8,128)S(1)} custom-call(f32[2,1,64,64]{3,2,1,0:T(8,128)S(1)} %select_bitcast_fusion), custom_call_target="InvertDiagBlocksLowerTriangular" | custom-call | tf_op jit(solution)/shard_map/triangular_solve/custom-call.2 | solution.py:37
  326.9 1.1 fusion.20
  328.1 0.2 fusion.10
  328.3 0.2 convolution_bitcast_fusion.1
  328.5 0.6 fusion.42
  (32 shorter events, 0.4 us)
Async XLA Ops:
  6.5 65.5 %copy-start = (bf16[4,64,64]{2,1,0:T(8,128)(2,1)S(1)}, bf16[4,64,64]{2,1,0:T(8,128)(2,1)}, u32[]{:S(2)}) copy-start(bf16[4,64,64]{2,1,0:T(8,128)(2,1)} %param.11) | copy-start | bytes 98308
  6.5 123.7 %all-reduce.13.cloned.1.call-start = ((), (), s32[]{:S(2)}) async-start(), calls=%async_computation.2 | async-start | bytes 262144 | tf_op jit(solution)/shard_map/psum | solution.py:45
  45.6 11.3 %copy-start.1 = (s32[8]{0:T(128)S(1)}, s32[8]{0:T(128)}, u32[]{:S(2)}) copy-start(s32[8]{0:T(128)} %param.12) | copy-start | bytes 100
  52.5 4.5 %collective-permute-start.1 = (f32[2,64,2,64]{3,2,1,0:T(2,128)S(1)}, f32[2,64,2,64]{3,2,1,0:T(2,128)S(1)}, u32[]{:S(2)}, u32[]{:S(2)}) collective-permute-start(f32[2,64,2,64]{3,2,1,0:T(2,128)S(1)} %get-tuple-element.17), channel_id=1, source_target_pairs={{1,0},{2,1},{3,2},{4,3},{5,4},{6,5},{7,6},{9,8},{10,9},{11,10},{12... | collective-permute-start | bytes 196616 | tf_op jit(solution)/shard_map/ppermute | solution.py:12
  53.8 4.0 %collective-permute-start = (f32[2,64,2,64]{3,2,1,0:T(2,128)S(1)}, f32[2,64,2,64]{3,2,1,0:T(2,128)S(1)}, u32[]{:S(2)}, u32[]{:S(2)}) collective-permute-start(f32[2,64,2,64]{3,2,1,0:T(2,128)S(1)} %get-tuple-element.16), channel_id=1, source_target_pairs={{0,1},{1,2},{2,3},{3,4},{4,5},{5,6},{6,7},{8,9},{9,10},{10,11},{11... | collective-permute-start | bytes 196616 | tf_op jit(solution)/shard_map/ppermute | solution.py:12
  72.9 143.2 %all-reduce.11.cloned.1.call-start = ((), (), s32[]{:S(2)}) async-start(), calls=%async_computation.1 | async-start | bytes 262144 | tf_op jit(solution)/shard_map/psum | solution.py:45
  156.5 4.3 %collective-permute-start.2 = (bf16[4,64,64]{2,1,0:T(8,128)(2,1)S(1)}, bf16[4,64,64]{2,1,0:T(8,128)(2,1)S(1)}, u32[]{:S(2)}, u32[]{:S(2)}) collective-permute-start(bf16[4,64,64]{2,1,0:T(8,128)(2,1)S(1)} %fusion.18), channel_id=1, source_target_pairs={{0,8},{8,0},{16,24},{24,16},{1,9},{9,1},{17,25},{25,17},{2,10},{10... | collective-permute-start | bytes 98312 | tf_op jit(solution)/shard_map/ppermute | solution.py:18
  162.5 139.7 %all-reduce.9.cloned.1.call-start = ((), (), s32[]{:S(2)}) async-start(), calls=%async_computation | async-start | bytes 262144 | tf_op jit(solution)/shard_map/psum | solution.py:45
  242.7 4.3 %collective-permute-start.3 = (bf16[4,64,64]{2,1,0:T(8,128)(2,1)S(1)}, bf16[4,64,64]{2,1,0:T(8,128)(2,1)S(1)}, u32[]{:S(2)}, u32[]{:S(2)}) collective-permute-start(bf16[4,64,64]{2,1,0:T(8,128)(2,1)S(1)} %fusion.19), channel_id=1, source_target_pairs={{0,16},{8,24},{16,0},{24,8},{1,17},{9,25},{17,1},{25,9},{2,18},{10... | collective-permute-start | bytes 98312 | tf_op jit(solution)/shard_map/ppermute | solution.py:18
Sparse Core Ops, SparseCore 0:
  73.0 57.1 all-reduce.12
  162.7 53.4 all-reduce.10
  248.8 53.4 all-reduce.8
where the time goes:
time: 336 us
  waiting for transfers between devices  171 us (51%)
  other arithmetic  86 us (26%)
  matrix products  43.8 us (13%)
  between operations  13.4 us (4%)
  blocking collectives  12.6 us (4%)
  starting transfers between devices  7.49 us (2%)
    psum x3, waiting for transfers between devices, merge_level(): gram_mats, cross_mats = lax.psum((gram_mats, cross_mats), 'space')  164 us
    another operation x10, other arithmetic, solve_coef(): jnp.linalg.cholesky(gram_mats + ridge_term[:, None, None] * identity)  35.9 us
    another operation x7, other arithmetic, solve_coef(): lax.linalg.triangular_solve(factor, halfway, left_side=True, lower=True,...  29.8 us
    dot_general x1, matrix products, body(): jnp.einsum('gaxyz,zc->gaxyc', images, spline_table(fine_z, coarse_z, 0, 0...  28.1 us
    all_gather x1, blocking collectives, body(): gathered = lax.all_gather(leaves, 'shots', axis=0, tiled=True)  12.6 us
    unnamed x2, other arithmetic  10.9 us
  transfers between devices with their start and end apart: 7, of which 6 were waited for; matrix products, arithmetic and copies ran while one was open for 0% of the time, Pallas kernels for 0%

commit v1 on v0

v1 whole, which is shorter than its diff:
```python
import math

import jax
import jax.numpy as jnp
import numpy as np
from jax import lax
from jax.experimental import pallas as pl
from jax.experimental.pallas import tpu as pltpu
from jax.sharding import PartitionSpec as P

F32 = jnp.float32
BF16 = jnp.bfloat16
VMEM_BYTES = 48 << 20


def spline_weights(fine_count, coarse_count, coarse_start):
    fine = np.arange(fine_count, dtype=np.float64)
    coarse = np.arange(coarse_count, dtype=np.float64) + coarse_start
    s = np.abs((fine[:, None] + 0.5 - 4.0 * coarse[None, :] - 2.0) / 4.0)
    inner = 2.0 / 3.0 - s**2 + 0.5 * s**3
    outer = np.maximum(2.0 - s, 0.0) ** 3 / 6.0
    return np.where(s < 1.0, inner, outer) / 4.0


def two_terms(table):
    table = jnp.asarray(table, F32)
    high = table.astype(BF16)
    return high, (table - high.astype(F32)).astype(BF16)


def halves(x):
    high = x.astype(BF16)
    return high, (x - high.astype(F32)).astype(BF16)


def thirds(x):
    high = x.astype(BF16)
    rest = x - high.astype(F32)
    mid = rest.astype(BF16)
    return high, mid, (rest - mid.astype(F32)).astype(BF16)


def dot(a, b):
    return jnp.dot(a, b, preferred_element_type=F32)


def dot_nt(a, b):
    return lax.dot_general(a, b, (((1,), (1,)), ((), ())), preferred_element_type=F32)


def wide_dot(wide, exact):
    return sum(dot(part, exact) for part in thirds(wide))


def dot_wide(exact, wide):
    return sum(dot(exact, part) for part in thirds(wide))


def restrict_kernel(ranks, probes, sources, table_xy, table_z, below, own, above, rows):
    groups, _, fine_z = rows.shape[1] // ranks, None, rows.shape[2]
    cells = sources.shape[1] // 2
    block_ranks = probes.shape[1] // (2 * cells)
    step = pl.program_id(0)
    edges = rows.shape[0]
    for g in range(groups):
        base = g * ranks + step * block_ranks

        def some_ranks(i, _, g=g, base=base):
            parts = []
            for k in range(2):
                at = (2 * i + k) * 2 * cells
                first = probes[g, pl.ds(pl.multiple_of(at, cells), cells)].astype(F32)
                second = probes[g, pl.ds(pl.multiple_of(at + cells, cells), cells)].astype(F32)
                image = first * sources[g, :cells].astype(F32)
                image = image + second * sources[g, cells:].astype(F32)
                parts.append(jnp.concatenate(halves(image), axis=0))
            both = dot(table_xy[...], jnp.concatenate(parts, axis=1))
            both = both[:edges] + both[edges:]
            for k in range(2):
                rows[:, base + 2 * i + k, :] = both[:, k * fine_z : (k + 1) * fine_z]
            return 0

        lax.fori_loop(0, block_ranks // 2, some_ranks, 0, unroll=2)

    @pl.when(step == pl.num_programs(0) - 1)
    def _():
        per = table_z.shape[0] // fine_z
        lanes = table_z.shape[1] // 2
        chunks = []
        for j in range(edges // per):
            total = 0.0
            for r in range(per):
                weights = table_z[r * fine_z : (r + 1) * fine_z]
                for part in halves(rows[j * per + r]):
                    total = total + dot(part, weights)
            chunks.append(total[:, :lanes] + total[:, lanes:])
        below[...] = chunks[0]
        own[...] = jnp.concatenate(chunks[1:-1], axis=1)
        above[...] = chunks[-1]


def restrict(probes, sources):
    groups, ranks, steps_t, fine_x, fine_y, fine_z = probes.shape
    cells = fine_x * fine_y
    coarse_x, coarse_y, coarse_z = fine_x // 4, fine_y // 4, fine_z // 4
    edges_x = coarse_x + 4
    weights_x = spline_weights(fine_x, edges_x, -2)
    weights_y = spline_weights(fine_y, coarse_y, 0)
    weights_z = spline_weights(fine_z, coarse_z, 0)
    table_xy = np.einsum("xe,yd->edxy", weights_x, weights_y).reshape(edges_x * coarse_y, cells)
    high, low = two_terms(table_xy)
    table_xy = jnp.concatenate(
        [jnp.concatenate([high, high], axis=1), jnp.concatenate([low, low], axis=1)], axis=0
    )
    per = 128 // coarse_z
    table_z = np.einsum("zc,rs->rzsc", weights_z, np.eye(per)).reshape(per * fine_z, 128)
    table_z = jnp.concatenate(two_terms(table_z), axis=1)
    block_ranks = 8
    grid = ranks // block_ranks
    block_rows = block_ranks * steps_t * cells
    all_rows = groups * ranks
    lanes = edges_x * coarse_y * coarse_z
    whole = lambda *shape: pl.BlockSpec(shape, lambda i: (0,) * len(shape))
    return pl.pallas_call(
        lambda *refs: restrict_kernel(ranks, *refs),
        grid=(grid,),
        in_specs=[
            pl.BlockSpec((groups, block_rows, fine_z), lambda i: (0, i, 0)),
            whole(groups, steps_t * cells, fine_z),
            whole(*table_xy.shape),
            whole(*table_z.shape),
        ],
        out_specs=[whole(all_rows, 128), whole(all_rows, lanes - 256), whole(all_rows, 128)],
        out_shape=[
            jax.ShapeDtypeStruct((all_rows, 128), F32),
            jax.ShapeDtypeStruct((all_rows, lanes - 256), F32),
            jax.ShapeDtypeStruct((all_rows, 128), F32),
        ],
        scratch_shapes=[pltpu.VMEM((edges_x * coarse_y, all_rows, fine_z), F32)],
        compiler_params=pltpu.CompilerParams(vmem_limit_bytes=VMEM_BYTES),
        name="restrict",
    )(
        probes.reshape(groups, ranks * steps_t * cells, fine_z),
        sources.reshape(groups, steps_t * cells, fine_z),
        table_xy,
        table_z,
    )


def products_kernel(ranks, place, *refs):
    *leaves, sketch, chosen, keep, send, table = refs
    rows = leaves[0].shape[0]
    for i, leaf in enumerate(leaves):
        table[i * rows : (i + 1) * rows, :] = leaf[...]
    picked = chosen.shape[0] // ranks
    for i in range(picked):
        at = pl.multiple_of(place[i] * ranks, ranks)
        chosen[i * ranks : (i + 1) * ranks, :] = table[pl.ds(at, ranks), :]
    pieces = chosen[...]
    gram = dot_nt(pieces, pieces)
    cross = dot_nt(pieces, sketch[...])
    block = lambda i, j: gram[i * ranks : (i + 1) * ranks, j * ranks : (j + 1) * ranks]
    pairs = [(block(i, i), cross[i * ranks : (i + 1) * ranks]) for i in range(picked)]
    pairs += [(block(0, 1), block(2, 3)), (block(0, 2), block(0, 3)), (block(1, 2), block(1, 3))]
    side = place[picked]
    half = ranks // 2
    for n, pair in enumerate(pairs):
        both = jnp.concatenate(pair, axis=1)
        top, bottom = both[:half], both[half:]
        keep[n * half : (n + 1) * half, :] = jnp.where(side == 0, top, bottom)
        send[n * half : (n + 1) * half, :] = jnp.where(side == 0, bottom, top)


def products(leaves, sketch, place, ranks):
    rows, lanes = leaves[0].shape
    count = len(leaves)
    half = (count * rows // ranks // 2) * ranks
    vmem = pl.BlockSpec(memory_space=pltpu.VMEM)
    out_rows = 7 * ranks // 2
    return pl.pallas_call(
        lambda *refs: products_kernel(ranks, *refs),
        in_specs=[pl.BlockSpec(memory_space=pltpu.SMEM)] + [vmem] * (count + 1),
        out_specs=[vmem] * 3,
        out_shape=[
            jax.ShapeDtypeStruct((half, lanes), BF16),
            jax.ShapeDtypeStruct((out_rows, 2 * ranks), F32),
            jax.ShapeDtypeStruct((out_rows, 2 * ranks), F32),
        ],
        scratch_shapes=[pltpu.VMEM((count * rows, lanes), BF16)],
        compiler_params=pltpu.CompilerParams(vmem_limit_bytes=VMEM_BYTES),
        name="products",
    )(place, *leaves, sketch)


def ridge_solve(grams, crosses):
    size = grams[0].shape[0]
    count = len(grams)
    eye = lax.broadcasted_iota(jnp.int32, (size, size), 0) == lax.broadcasted_iota(
        jnp.int32, (size, size), 1
    )
    blocks = size // 8
    whole = []
    for gram, cross in zip(grams, crosses):
        trace = jnp.sum(jnp.where(eye, gram, 0.0))
        gram = gram + jnp.where(eye, 0.01 * trace / size + 1e-06, 0.0)
        whole.append(jnp.concatenate([gram, cross], axis=1))
    start = tuple(
        tuple(m[8 * i : 8 * i + 8] for i in range(blocks)) for m in whole
    )
    sub = lax.broadcasted_iota(jnp.int32, (8, 2 * size), 0)

    def eliminate(_, mats):
        done = []
        for mat in mats:
            head = mat[0]
            columns = [jnp.broadcast_to(head[:, j : j + 1], head.shape) for j in range(8)]
            for j in range(8):
                inverse = 1.0 / columns[j][j : j + 1]
                here = sub == j
                row = head[j : j + 1] * inverse
                head = jnp.where(here, row, head - columns[j] * row)
                for m in range(j + 1, 8):
                    entry = columns[m][j : j + 1] * inverse
                    columns[m] = jnp.where(here, entry, columns[m] - columns[j] * entry)
            rest = []
            for block in mat[1:]:
                new = block
                for j in range(8):
                    new = new - block[:, j : j + 1] * head[j : j + 1]
                rest.append(new)
            done.append(tuple(pltpu.roll(x, 2 * size - 8, 1) for x in rest + [head]))
        return tuple(done)

    mats = lax.fori_loop(0, blocks, eliminate, start)
    return [jnp.concatenate(mat, axis=0)[:, :size].astype(BF16) for mat in mats]


def two_blocks(first, second):
    zero = jnp.zeros_like(first)
    return jnp.concatenate(
        [jnp.concatenate([first, zero], axis=1), jnp.concatenate([zero, second], axis=1)], axis=0
    )


def tree_kernel(ranks, scaling, place, mine, other, pieces, own, send, table):
    half = ranks // 2
    side = place[0]
    for n in range(7):
        a, b = mine[n * half : (n + 1) * half, :], other[n * half : (n + 1) * half, :]
        table[n * ranks : n * ranks + half, :] = jnp.where(side == 0, a, b)
        table[n * ranks + half : (n + 1) * ranks, :] = jnp.where(side == 0, b, a)
    unit = lambda n: table[n * ranks : (n + 1) * ranks, :]
    left = lambda n: unit(n)[:, :ranks]
    right = lambda n: unit(n)[:, ranks:]
    grams = [left(n) for n in range(4)]
    crosses = [right(n) for n in range(4)]
    g01, g23 = left(4), right(4)
    row = lambda *xs: jnp.concatenate(xs, axis=1)
    column = lambda *xs: jnp.concatenate(xs, axis=0)
    corner = column(unit(5), unit(6))
    top = column(row(grams[0], g01), row(g01.T, grams[1]))
    low = column(row(grams[2], g23), row(g23.T, grams[3]))
    joint = column(row(top, corner), row(corner.T, low))
    c = ridge_solve(grams, crosses)
    first = two_blocks(column(c[0], c[1]), column(c[2], c[3]))
    first_t = first.astype(F32).T.astype(BF16)
    square = scaling * scaling
    gram_m = square * dot_wide(first_t, wide_dot(joint, first))
    cross_m = scaling * dot_wide(first_t, column(*crosses))
    d = ridge_solve(
        [gram_m[:ranks, :ranks], gram_m[ranks:, ranks:]], [cross_m[:ranks], cross_m[ranks:]]
    )
    second = column(*d)
    second_t = second.astype(F32).T.astype(BF16)
    gram_n = square * dot_wide(second_t, wide_dot(gram_m, second))
    cross_n = scaling * dot_wide(second_t, cross_m)
    (e,) = ridge_solve([gram_n], [cross_n])
    e_t = e.astype(F32).T.astype(BF16)
    total_t = wide_dot(dot(e_t, second_t), first_t)
    result = (scaling * scaling * scaling) * sum(dot(part, pieces[...]) for part in halves(total_t))
    table[: result.shape[0], :] = result[:, : 2 * ranks]
    table[result.shape[0] : 2 * result.shape[0], :] = result[:, 2 * ranks :]
    count = own.shape[0]
    for out, at in ((own, place[1]), (send, place[2])):
        at = pl.multiple_of(at * count, count)
        for i in range(2):
            out[:, i * 2 * ranks : (i + 1) * 2 * ranks] = table[
                pl.ds(at + i * ranks, count), :
            ]


def tree(mine, other, pieces, place, ranks, scaling, columns):
    vmem = pl.BlockSpec(memory_space=pltpu.VMEM)
    out = jax.ShapeDtypeStruct((columns, pieces.shape[1]), F32)
    return pl.pallas_call(
        lambda *refs: tree_kernel(ranks, scaling, *refs),
        in_specs=[pl.BlockSpec(memory_space=pltpu.SMEM)] + [vmem] * 3,
        out_specs=[vmem] * 2,
        out_shape=[out, out],
        scratch_shapes=[pltpu.VMEM((7 * ranks, 2 * ranks), F32)],
        compiler_params=pltpu.CompilerParams(vmem_limit_bytes=VMEM_BYTES),
        name="tree",
    )(place, mine, other, pieces)


def swap(x, axis, mask):
    return lax.ppermute(x, axis, [(i, i ^ mask) for i in range(lax.axis_size(axis))])


def shift(x, axis, by):
    count = lax.axis_size(axis)
    return lax.ppermute(x, axis, [(i, i + by) for i in range(count) if 0 <= i + by < count])


def body(probes, sources, sketch, pairing):
    groups, ranks = probes.shape[:2]
    coarse_x = probes.shape[3] // 4
    layer = sketch.shape[2]
    shots, space = lax.axis_size("shots"), lax.axis_size("space")
    shot, place = lax.axis_index("shots"), lax.axis_index("space")
    scaling = math.sqrt(coarse_x * space * layer / ranks)

    below, own, above = restrict(probes, sources)
    from_above = shift(below, "space", -1)
    from_below = shift(above, "space", 1)
    leaf = (own + jnp.concatenate([from_below, from_above], axis=1)).astype(BF16)

    leaves = [leaf] + [swap(leaf, "shots", m) for m in range(1, shots)]
    picked = shots * groups // 2
    side = place % 2
    chosen = lax.dynamic_slice_in_dim(pairing, shot // (shots // 2) * picked, picked)
    slots = (chosen // groups ^ shot) * groups + chosen % groups
    sketch_t = jnp.transpose(sketch, (1, 0, 2)).reshape(ranks, coarse_x * layer)
    slots = jnp.concatenate([slots, side[None]]).astype(jnp.int32)
    pieces, mine, send = products(leaves, sketch_t, slots, ranks)

    mine = mine + swap(send, "space", 1)
    mask = 2
    while mask < space:
        mine = mine + swap(mine, "space", mask)
        mask *= 2
    other = swap(mine, "space", 1)

    columns = ranks // shots
    far = shots // 2
    spots = jnp.stack([side, shot, shot ^ far]).astype(jnp.int32)
    own_part, sent = tree(mine, other, pieces, spots, ranks, scaling, columns)
    total = (own_part + swap(sent, "shots", far)).astype(BF16)
    return jnp.transpose(total.reshape(columns, coarse_x, layer), (1, 0, 2))


def solution(mesh):
    in_specs = (
        P("shots", None, None, "space", None, None),
        P("shots", None, "space", None, None),
        P("space", None, None),
        P(),
    )
    out_specs = P("space", "shots", None)
    return jax.shard_map(body, mesh=mesh, in_specs=in_specs, out_specs=out_specs, check_vma=False)
```

time: 336 us -> 65.2 us (0.19)
  waiting for transfers between devices: 171 us -> 21.2 us
  other arithmetic: 86 us -> 0.3 us
  matrix products: 43.8 us -> 0 us
  Pallas kernels: 0 us -> 24.9 us
  between operations: 13.4 us -> 0.14 us
  blocking collectives: 12.6 us -> 0 us
  starting transfers between devices: 7.49 us -> 14.8 us
    psum x3 -> x0, waiting for transfers between devices: 164 us -> none  [merge_level(): gram_mats, cross_mats = lax.psum((gram_mats, cross_mats), 'space')]
    another operation x19 -> x1, other arithmetic: 65.7 us -> 0.08 us  [body(): spots = jnp.stack([side, shot, shot ^ far]).astype(jnp.int32)]
    dot_general x12 -> x0, matrix products: 39.8 us -> none  [the longest x1 28.1 us: body(): jnp.einsum('gaxyz,zc->gaxyc', images, spline_table(fine_z, coarse_z, 0, 0...]
    pallas_call x0 -> x3, Pallas kernels: none -> 24.9 us  [the longest x1 13.9 us: tree(): pl.pallas_call(lambda *refs: tree_kernel(ranks, scaling, *refs), in_specs...]
    ppermute x4 -> x10, waiting for transfers between devices: 6.38 us -> 21.2 us  [the longest x8 17.5 us: swap(): lax.ppermute(x, axis, [(i, i ^ mask) for i in range(lax.axis_size(axis))])]
    all_gather x1 -> x0, blocking collectives: 12.6 us -> none  [body(): gathered = lax.all_gather(leaves, 'shots', axis=0, tiled=True)]
    unnamed x2 -> x0, other arithmetic: 10.9 us -> none
    ppermute x4 -> x10, starting transfers between devices: 7.41 us -> 14.8 us  [the longest x8 11.1 us: swap(): lax.ppermute(x, axis, [(i, i ^ mask) for i in range(lax.axis_size(axis))])]
  transfers between devices with their start and end apart: 7 -> 10, of which waited for: 6 -> 9; matrix products, arithmetic and copies ran while one was open for 0% -> 1% of each run, Pallas kernels for 0% -> 0%
where the time goes in v1:
time: 65.2 us; the launch traced here: 64.8 us
  Pallas kernels  24.9 us (38%)
  waiting for transfers between devices  21.2 us (33%)
  starting transfers between devices  14.8 us (23%)
  local copies, waits for them, and re-layouts  3.46 us (5%)
    ppermute x8, waiting for transfers between devices, swap(): lax.ppermute(x, axis, [(i, i ^ mask) for i in range(lax.axis_size(axis))])  17.5 us
    pallas_call x1, Pallas kernels, tree(): pl.pallas_call(lambda *refs: tree_kernel(ranks, scaling, *refs), in_specs...  13.9 us
    ppermute x8, starting transfers between devices, swap(): lax.ppermute(x, axis, [(i, i ^ mask) for i in range(lax.axis_size(axis))])  11.1 us
    pallas_call x1, Pallas kernels, restrict(): pl.pallas_call(lambda *refs: restrict_kernel(ranks, *refs), grid=(grid,),...  10.2 us
    ppermute x2, waiting for transfers between devices, shift(): lax.ppermute(x, axis, [(i, i + by) for i in range(count) if 0 <= i + by <...  3.73 us
    ppermute x2, starting transfers between devices, shift(): lax.ppermute(x, axis, [(i, i + by) for i in range(count) if 0 <= i + by <...  3.65 us
    unnamed x10, local copies, waits for them, and re-layouts  2.59 us
  transfers between devices with their start and end apart: 10, of which 9 were waited for; matrix products, arithmetic and copies ran while one was open for 1% of the time, Pallas kernels for 0%

profile of v1, /device:TPU:0, one launch (start us, length us, event | category | flops | bytes accessed | tf_op | source)
XLA Modules:
  0.0 64.8 jit_solution(13850758973687300742)
XLA Ops:
  0.0 0.0 copy-start.4
  0.0 0.0 copy-start
  0.0 1.0 %copy-done = bf16[512,256]{1,0:T(8,128)(2,1)S(1)} copy-done((bf16[512,256]{1,0:T(8,128)(2,1)S(1)}, bf16[512,256]{1,0:T(8,128)(2,1)}, u32[]{:S(2)}) %copy-start) | copy-done | bytes 262168
  1.0 0.0 copy-start.1
  1.0 0.9 %copy-done.1 = bf16[2,2,16,8,128]{4,3,2,1,0:T(8,128)(2,1)S(1)} copy-done((bf16[2,2,16,8,128]{4,3,2,1,0:T(8,128)(2,1)S(1)}, bf16[2,2,16,8,128]{4,3,2,1,0:T(8,128)(2,1)}, u32[]{:S(2)}) %copy-start.1) | copy-done | bytes 131096
  1.9 0.0 copy-start.2
  1.9 0.7 %copy-done.2 = bf16[32,256]{1,0:T(8,128)(2,1)S(1)} copy-done((bf16[32,256]{1,0:T(8,128)(2,1)S(1)}, bf16[32,256]{1,0:T(8,128)(2,1)}, u32[]{:S(2)}) %copy-start.2) | copy-done | bytes 16408
  2.6 0.0 copy-start.3
  2.6 10.2 %restrict.1 = (f32[128,128]{1,0:T(8,128)S(1)}, f32[128,256]{1,0:T(8,128)S(1)}, f32[128,128]{1,0:T(8,128)S(1)}) custom-call(bf16[2,16384,128]{2,1,0:T(8,128)(2,1)} %bitcast.10, bf16[2,256,128]{2,1,0:T(8,128)(2,1)S(1)} %bitcast.9, bf16[32,256]{1,0:T(8,128)(2,1)S(1)} %copy-done.2, bf16[512,256]{1,0:T(8,128)(2,1)S(1)} %copy-done), custom_call_target="tpu_custom_call" | custom-call | tf_op jit(solution)/shard_map/restrict/pallas_call | solution.py:124
  12.8 2.4 %collective-permute-start = (f32[128,128]{1,0:T(8,128)S(1)}, f32[128,128]{1,0:T(8,128)S(1)}, u32[]{:S(2)}, u32[]{:S(2)}) collective-permute-start(f32[128,128]{1,0:T(8,128)S(1)} %get-tuple-element.14), channel_id=1, source_target_pairs={{0,1},{1,2},{2,3},{3,4},{4,5},{5,6},{6,7},{8,9},{9,10},{10,11},{11... | collective-permute-start | bytes 196616 | tf_op jit(solution)/shard_map/ppermute | solution.py:312
  15.1 1.3 %collective-permute-start.1 = (f32[128,128]{1,0:T(8,128)S(1)}, f32[128,128]{1,0:T(8,128)S(1)}, u32[]{:S(2)}, u32[]{:S(2)}) collective-permute-start(f32[128,128]{1,0:T(8,128)S(1)} %get-tuple-element.15), channel_id=1, source_target_pairs={{1,0},{2,1},{3,2},{4,3},{5,4},{6,5},{7,6},{9,8},{10,9},{11,10},{12... | collective-permute-start | bytes 196616 | tf_op jit(solution)/shard_map/ppermute | solution.py:312
  16.5 0.0 copy-done.3
  16.5 0.1 copy.7
  16.5 0.1 reshape.14.refs_5_
  16.7 0.0 copy-done.4
  16.7 0.1 fusion.1
  16.8 0.0 collective-permute-done
  16.8 3.7 %collective-permute-done.1 = f32[128,128]{1,0:T(8,128)S(1)} collective-permute-done((f32[128,128]{1,0:T(8,128)S(1)}, f32[128,128]{1,0:T(8,128)S(1)}, u32[]{:S(2)}, u32[]{:S(2)}) %collective-permute-start.1) | collective-permute-done | bytes 65568 | tf_op jit(solution)/shard_map/ppermute | solution.py:312
  20.5 2.5 %collective-permute-start.4 = (bf16[128,256]{1,0:T(8,128)(2,1)S(1)}, bf16[128,256]{1,0:T(8,128)(2,1)S(1)}, u32[]{:S(2)}, u32[]{:S(2)}) collective-permute-start(bf16[128,256]{1,0:T(8,128)(2,1)S(1)} %fusion.refs_1_), channel_id=1, source_target_pairs={{0,24},{8,16},{16,8},{24,0},{1,25},{9,17},{17,9},{25,1},{2,26},{10... | collective-permute-start | bytes 196616 | tf_op jit(solution)/shard_map/ppermute | solution.py:307
  23.0 0.5 collective-permute-start.3
  23.5 0.5 collective-permute-start.2
  24.1 0.1 pad_add_fusion.1.refs_0_
  24.1 1.6 %collective-permute-done.4.refs_4_ = bf16[128,256]{1,0:T(8,128)(2,1)S(1)} collective-permute-done((bf16[128,256]{1,0:T(8,128)(2,1)S(1)}, bf16[128,256]{1,0:T(8,128)(2,1)S(1)}, u32[]{:S(2)}, u32[]{:S(2)}) %collective-permute-start.4) | collective-permute-done | bytes 65568 | tf_op jit(solution)/shard_map/ppermute | solution.py:307
  25.7 2.2 %collective-permute-done.3.refs_3_ = bf16[128,256]{1,0:T(8,128)(2,1)S(1)} collective-permute-done((bf16[128,256]{1,0:T(8,128)(2,1)S(1)}, bf16[128,256]{1,0:T(8,128)(2,1)S(1)}, u32[]{:S(2)}, u32[]{:S(2)}) %collective-permute-start.3) | collective-permute-done | bytes 65568 | tf_op jit(solution)/shard_map/ppermute | solution.py:307
  28.0 0.5 collective-permute-done.2.refs_2_
  28.5 0.9 %products.1 = (bf16[256,256]{1,0:T(8,128)(2,1)S(1)}, f32[224,128]{1,0:T(8,128)S(1)}, f32[224,128]{1,0:T(8,128)S(1)}) custom-call(s32[5]{0:T(128)S(1)} %pad_add_fusion.1.refs_0_, bf16[128,256]{1,0:T(8,128)(2,1)S(1)} %fusion.refs_1_, bf16[128,256]{1,0:T(8,128)(2,1)S(1)} %collective-permute-done.2.refs_2_, bf16[128,256]{1,0:T(8,128)(2,1)S(1)} %collective-permute-done.3.refs_3_, ...), custom_call_target="tpu_custom_call" | custom-call | tf_op jit(solution)/shard_map/products/pallas_call | solution.py:180
  29.3 0.6 collective-permute-start.5
  30.0 1.0 %collective-permute-done.5 = f32[224,128]{1,0:T(8,128)S(1)} collective-permute-done((f32[224,128]{1,0:T(8,128)S(1)}, f32[224,128]{1,0:T(8,128)S(1)}, u32[]{:S(2)}, u32[]{:S(2)}) %collective-permute-start.5) | collective-permute-done | bytes 114720 | tf_op jit(solution)/shard_map/ppermute | solution.py:307
  30.9 2.5 %collective-permute-start.6 = (f32[224,128]{1,0:T(8,128)S(1)}, f32[224,128]{1,0:T(8,128)S(1)}, u32[]{:S(2)}, u32[]{:S(2)}) collective-permute-start(f32[224,128]{1,0:T(8,128)S(1)} %add.38), channel_id=1, source_target_pairs={{0,2},{1,3},{2,0},{3,1},{4,6},{5,7},{6,4},{7,5},{8,10},{9,11},{10,... | collective-permute-start | bytes 344072 | tf_op jit(solution)/shard_map/ppermute | solution.py:307
  33.4 3.5 %collective-permute-done.6 = f32[224,128]{1,0:T(8,128)S(1)} collective-permute-done((f32[224,128]{1,0:T(8,128)S(1)}, f32[224,128]{1,0:T(8,128)S(1)}, u32[]{:S(2)}, u32[]{:S(2)}) %collective-permute-start.6) | collective-permute-done | bytes 114720 | tf_op jit(solution)/shard_map/ppermute | solution.py:307
  36.9 2.8 %collective-permute-start.7 = (f32[224,128]{1,0:T(8,128)S(1)}, f32[224,128]{1,0:T(8,128)S(1)}, u32[]{:S(2)}, u32[]{:S(2)}) collective-permute-start(f32[224,128]{1,0:T(8,128)S(1)} %add.39), channel_id=1, source_target_pairs={{0,4},{1,5},{2,6},{3,7},{4,0},{5,1},{6,2},{7,3},{8,12},{9,13},{10,... | collective-permute-start | bytes 344072 | tf_op jit(solution)/shard_map/ppermute | solution.py:307
  39.7 5.3 %collective-permute-done.7 = f32[224,128]{1,0:T(8,128)S(1)} collective-permute-done((f32[224,128]{1,0:T(8,128)S(1)}, f32[224,128]{1,0:T(8,128)S(1)}, u32[]{:S(2)}, u32[]{:S(2)}) %collective-permute-start.7) | collective-permute-done | bytes 114720 | tf_op jit(solution)/shard_map/ppermute | solution.py:307
  45.0 0.1 collective-permute-start.8
  45.1 0.1 pad_add_fusion.refs_0_
  45.2 1.2 %collective-permute-done.8.refs_2_ = f32[224,128]{1,0:T(8,128)S(1)} collective-permute-done((f32[224,128]{1,0:T(8,128)S(1)}, f32[224,128]{1,0:T(8,128)S(1)}, u32[]{:S(2)}, u32[]{:S(2)}) %collective-permute-start.8) | collective-permute-done | bytes 114720 | tf_op jit(solution)/shard_map/ppermute | solution.py:307
  46.4 13.9 %tree.1 = (f32[16,256]{1,0:T(8,128)S(1)}, f32[16,256]{1,0:T(8,128)S(1)}) custom-call(s32[3]{0:T(128)S(1)} %pad_add_fusion.refs_0_, f32[224,128]{1,0:T(8,128)S(1)} %add.40.refs_1_, f32[224,128]{1,0:T(8,128)S(1)} %collective-permute-done.8.refs_2_, bf16[256,256]{1,0:T(8,128)(2,1)S(1)} %get-tuple-element.18.refs_3_), custom_call_target="tpu_custom_call" | custom-call | tf_op jit(solution)/shard_map/tree/pallas_call | solution.py:295
  60.3 1.6 %collective-permute-start.9 = (f32[16,256]{1,0:T(8,128)S(1)}, f32[16,256]{1,0:T(8,128)S(1)}, u32[]{:S(2)}, u32[]{:S(2)}) collective-permute-start(f32[16,256]{1,0:T(8,128)S(1)} %get-tuple-element.20), channel_id=1, source_target_pairs={{0,16},{8,24},{16,0},{24,8},{1,17},{9,25},{17,1},{25,9},{2,18},{10... | collective-permute-start | bytes 49160 | tf_op jit(solution)/shard_map/ppermute | solution.py:307
  61.9 2.2 %collective-permute-done.9 = f32[16,256]{1,0:T(8,128)S(1)} collective-permute-done((f32[16,256]{1,0:T(8,128)S(1)}, f32[16,256]{1,0:T(8,128)S(1)}, u32[]{:S(2)}, u32[]{:S(2)}) %collective-permute-start.9) | collective-permute-done | bytes 16416 | tf_op jit(solution)/shard_map/ppermute | solution.py:307
  64.1 0.1 reshape.15
  64.2 0.6 copy.10
  (5 shorter events, 0.1 us)
Async XLA Ops:
  0.0 16.7 %copy-start.4 = (s32[8]{0:T(128)S(1)}, s32[8]{0:T(128)}, u32[]{:S(2)}) copy-start(s32[8]{0:T(128)} %param.9) | copy-start | bytes 100
  0.0 1.0 %copy-start = (bf16[512,256]{1,0:T(8,128)(2,1)S(1)}, bf16[512,256]{1,0:T(8,128)(2,1)}, u32[]{:S(2)}) copy-start(bf16[512,256]{1,0:T(8,128)(2,1)} %constant.75.refs_3_) | copy-start | bytes 786436
  1.0 0.9 %copy-start.1 = (bf16[2,2,16,8,128]{4,3,2,1,0:T(8,128)(2,1)S(1)}, bf16[2,2,16,8,128]{4,3,2,1,0:T(8,128)(2,1)}, u32[]{:S(2)}) copy-start(bf16[2,2,16,8,128]{4,3,2,1,0:T(8,128)(2,1)} %param.7) | copy-start | bytes 393220
  1.9 0.7 %copy-start.2 = (bf16[32,256]{1,0:T(8,128)(2,1)S(1)}, bf16[32,256]{1,0:T(8,128)(2,1)}, u32[]{:S(2)}) copy-start(bf16[32,256]{1,0:T(8,128)(2,1)} %constant.70.refs_2_) | copy-start | bytes 49156
  2.6 13.9 %copy-start.3 = (bf16[4,64,64]{2,1,0:T(8,128)(2,1)S(1)}, bf16[4,64,64]{2,1,0:T(8,128)(2,1)}, u32[]{:S(2)}) copy-start(bf16[4,64,64]{2,1,0:T(8,128)(2,1)} %param.8) | copy-start | bytes 98308
  12.8 4.0 %collective-permute-start = (f32[128,128]{1,0:T(8,128)S(1)}, f32[128,128]{1,0:T(8,128)S(1)}, u32[]{:S(2)}, u32[]{:S(2)}) collective-permute-start(f32[128,128]{1,0:T(8,128)S(1)} %get-tuple-element.14), channel_id=1, source_target_pairs={{0,1},{1,2},{2,3},{3,4},{4,5},{5,6},{6,7},{8,9},{9,10},{10,11},{11... | collective-permute-start | bytes 196616 | tf_op jit(solution)/shard_map/ppermute | solution.py:312
  15.1 5.3 %collective-permute-start.1 = (f32[128,128]{1,0:T(8,128)S(1)}, f32[128,128]{1,0:T(8,128)S(1)}, u32[]{:S(2)}, u32[]{:S(2)}) collective-permute-start(f32[128,128]{1,0:T(8,128)S(1)} %get-tuple-element.15), channel_id=1, source_target_pairs={{1,0},{2,1},{3,2},{4,3},{5,4},{6,5},{7,6},{9,8},{10,9},{11,10},{12... | collective-permute-start | bytes 196616 | tf_op jit(solution)/shard_map/ppermute | solution.py:312
  20.5 5.2 %collective-permute-start.4 = (bf16[128,256]{1,0:T(8,128)(2,1)S(1)}, bf16[128,256]{1,0:T(8,128)(2,1)S(1)}, u32[]{:S(2)}, u32[]{:S(2)}) collective-permute-start(bf16[128,256]{1,0:T(8,128)(2,1)S(1)} %fusion.refs_1_), channel_id=1, source_target_pairs={{0,24},{8,16},{16,8},{24,0},{1,25},{9,17},{17,9},{25,1},{2,26},{10... | collective-permute-start | bytes 196616 | tf_op jit(solution)/shard_map/ppermute | solution.py:307
  23.0 5.0 %collective-permute-start.3 = (bf16[128,256]{1,0:T(8,128)(2,1)S(1)}, bf16[128,256]{1,0:T(8,128)(2,1)S(1)}, u32[]{:S(2)}, u32[]{:S(2)}) collective-permute-start(bf16[128,256]{1,0:T(8,128)(2,1)S(1)} %fusion.refs_1_), channel_id=1, source_target_pairs={{0,16},{8,24},{16,0},{24,8},{1,17},{9,25},{17,1},{25,9},{2,18},{10... | collective-permute-start | bytes 196616 | tf_op jit(solution)/shard_map/ppermute | solution.py:307
  23.5 4.9 %collective-permute-start.2 = (bf16[128,256]{1,0:T(8,128)(2,1)S(1)}, bf16[128,256]{1,0:T(8,128)(2,1)S(1)}, u32[]{:S(2)}, u32[]{:S(2)}) collective-permute-start(bf16[128,256]{1,0:T(8,128)(2,1)S(1)} %fusion.refs_1_), channel_id=1, source_target_pairs={{0,8},{8,0},{16,24},{24,16},{1,9},{9,1},{17,25},{25,17},{2,10},{10... | collective-permute-start | bytes 196616 | tf_op jit(solution)/shard_map/ppermute | solution.py:307
  29.3 1.6 %collective-permute-start.5 = (f32[224,128]{1,0:T(8,128)S(1)}, f32[224,128]{1,0:T(8,128)S(1)}, u32[]{:S(2)}, u32[]{:S(2)}) collective-permute-start(f32[224,128]{1,0:T(8,128)S(1)} %get-tuple-element.17), channel_id=1, source_target_pairs={{0,1},{1,0},{2,3},{3,2},{4,5},{5,4},{6,7},{7,6},{8,9},{9,8},{10,11... | collective-permute-start | bytes 344072 | tf_op jit(solution)/shard_map/ppermute | solution.py:307
  30.9 5.9 %collective-permute-start.6 = (f32[224,128]{1,0:T(8,128)S(1)}, f32[224,128]{1,0:T(8,128)S(1)}, u32[]{:S(2)}, u32[]{:S(2)}) collective-permute-start(f32[224,128]{1,0:T(8,128)S(1)} %add.38), channel_id=1, source_target_pairs={{0,2},{1,3},{2,0},{3,1},{4,6},{5,7},{6,4},{7,5},{8,10},{9,11},{10,... | collective-permute-start | bytes 344072 | tf_op jit(solution)/shard_map/ppermute | solution.py:307
  36.9 8.1 %collective-permute-start.7 = (f32[224,128]{1,0:T(8,128)S(1)}, f32[224,128]{1,0:T(8,128)S(1)}, u32[]{:S(2)}, u32[]{:S(2)}) collective-permute-start(f32[224,128]{1,0:T(8,128)S(1)} %add.39), channel_id=1, source_target_pairs={{0,4},{1,5},{2,6},{3,7},{4,0},{5,1},{6,2},{7,3},{8,12},{9,13},{10,... | collective-permute-start | bytes 344072 | tf_op jit(solution)/shard_map/ppermute | solution.py:307
  45.0 1.4 %collective-permute-start.8 = (f32[224,128]{1,0:T(8,128)S(1)}, f32[224,128]{1,0:T(8,128)S(1)}, u32[]{:S(2)}, u32[]{:S(2)}) collective-permute-start(f32[224,128]{1,0:T(8,128)S(1)} %add.40.refs_1_), channel_id=1, source_target_pairs={{0,1},{1,0},{2,3},{3,2},{4,5},{5,4},{6,7},{7,6},{8,9},{9,8},{10,11... | collective-permute-start | bytes 344072 | tf_op jit(solution)/shard_map/ppermute | solution.py:307
  60.3 3.8 %collective-permute-start.9 = (f32[16,256]{1,0:T(8,128)S(1)}, f32[16,256]{1,0:T(8,128)S(1)}, u32[]{:S(2)}, u32[]{:S(2)}) collective-permute-start(f32[16,256]{1,0:T(8,128)S(1)} %get-tuple-element.20), channel_id=1, source_target_pairs={{0,16},{8,24},{16,0},{24,8},{1,17},{9,25},{17,1},{25,9},{2,18},{10... | collective-permute-start | bytes 49160 | tf_op jit(solution)/shard_map/ppermute | solution.py:307

commit v2 on v1

v2 whole, which is shorter than its diff:
```python
import math

import jax
import jax.numpy as jnp
import numpy as np
from jax import lax
from jax.experimental import pallas as pl
from jax.experimental.pallas import tpu as pltpu
from jax.sharding import PartitionSpec as P

F32 = jnp.float32
BF16 = jnp.bfloat16
VMEM_BYTES = 48 << 20
FULL_VMEM = 60 << 20


def spline_weights(fine_count, coarse_count, coarse_start):
    fine = np.arange(fine_count, dtype=np.float64)
    coarse = np.arange(coarse_count, dtype=np.float64) + coarse_start
    s = np.abs((fine[:, None] + 0.5 - 4.0 * coarse[None, :] - 2.0) / 4.0)
    inner = 2.0 / 3.0 - s**2 + 0.5 * s**3
    outer = np.maximum(2.0 - s, 0.0) ** 3 / 6.0
    return np.where(s < 1.0, inner, outer) / 4.0


def two_terms(table):
    table = jnp.asarray(table, F32)
    high = table.astype(BF16)
    return high, (table - high.astype(F32)).astype(BF16)


def halves(x):
    high = x.astype(BF16)
    return high, (x - high.astype(F32)).astype(BF16)


def thirds(x):
    high = x.astype(BF16)
    rest = x - high.astype(F32)
    mid = rest.astype(BF16)
    return high, mid, (rest - mid.astype(F32)).astype(BF16)


def dot(a, b):
    return jnp.dot(a, b, preferred_element_type=F32)


def dot_nt(a, b):
    return lax.dot_general(a, b, (((1,), (1,)), ((), ())), preferred_element_type=F32)


def wide_dot(wide, exact):
    return sum(dot(part, exact) for part in thirds(wide))


def dot_wide(exact, wide):
    return sum(dot(exact, part) for part in thirds(wide))


def restrict_kernel(
    side, probes, sources, table_xy, table_z, own, to_core, to_chip,
    rows, held, raw, fields, weights_xy, weights_z, arrived, ready,
):
    edges, fine_z = weights_xy.shape[0] // 2, rows.shape[1]
    cells = weights_xy.shape[1] // 2
    all_rows = own.shape[0]
    chunks = arrived.shape[0]
    share = held.shape[0] // chunks
    ranks = share // (2 * cells)
    groups = sources.shape[0]

    def arrival(i):
        part = pl.ds(i * share, share)
        return pltpu.make_async_copy(probes.at[part], held.at[part], arrived.at[i])

    small = [
        pltpu.make_async_copy(source, target, ready.at[i])
        for i, (source, target) in enumerate(
            ((sources, raw), (table_xy, weights_xy), (table_z, weights_z))
        )
    ]
    small[0].start()
    small[1].start()
    for i in range(chunks):
        arrival(i).start()
    small[2].start()
    small[0].wait()
    small[1].wait()
    fields[...] = raw[...].astype(F32)
    for i in range(chunks):
        g = i * groups // chunks
        arrival(i).wait()
        for pair in range(ranks // 2):
            first, second = (i * ranks + 2 * pair + k for k in range(2))
            high, low = ([], []), ([], [])
            for c in range(0, cells, 16):
                field0, field1 = fields[g, c : c + 16], fields[g, cells + c : cells + c + 16]
                for k, rank in enumerate((first, second)):
                    at = rank * 2 * cells + c
                    image = held[at : at + 16].astype(F32) * field0
                    image = image + held[at + cells : at + cells + 16].astype(F32) * field1
                    parts = halves(image)
                    high[k].append(parts[0])
                    low[k].append(parts[1])
            both = jnp.concatenate(
                [jnp.concatenate(high[k] + low[k], axis=0) for k in range(2)], axis=1
            )
            both = dot(weights_xy[...], both)
            both = both[:edges] + both[edges:]
            for k, rank in enumerate((first, second)):
                rows[rank * edges : (rank + 1) * edges, :] = both[:, k * fine_z : (k + 1) * fine_z]
    small[2].wait()
    per = weights_z.shape[0] // fine_z
    lanes = weights_z.shape[1] // 2
    layers = []
    for j in range(edges // per):
        total = 0.0
        for r in range(per):
            weights = weights_z[r * fine_z : (r + 1) * fine_z]
            for part in halves(rows[pl.ds(j * per + r, all_rows, stride=edges), :]):
                total = total + dot(part, weights)
        layers.append(total[:, :lanes] + total[:, lanes:])
    own[...] = jnp.concatenate(layers[1:-1], axis=1)
    odd = side[0] == 1
    to_core[...] = jnp.where(odd, layers[0], layers[-1])
    to_chip[...] = jnp.where(odd, layers[-1], layers[0])


def restrict(probes, sources, side):
    groups, ranks, steps_t, fine_x, fine_y, fine_z = probes.shape
    cells = fine_x * fine_y
    coarse_x, coarse_y, coarse_z = fine_x // 4, fine_y // 4, fine_z // 4
    edges_x = coarse_x + 4
    weights_x = spline_weights(fine_x, edges_x, -2)
    weights_y = spline_weights(fine_y, coarse_y, 0)
    weights_z = spline_weights(fine_z, coarse_z, 0)
    table_xy = np.einsum("xe,yd->edxy", weights_x, weights_y).reshape(edges_x * coarse_y, cells)
    high, low = two_terms(table_xy)
    table_xy = jnp.concatenate(
        [jnp.concatenate([high, high], axis=1), jnp.concatenate([low, low], axis=1)], axis=0
    )
    per = 128 // coarse_z
    table_z = np.einsum("zc,rs->rzsc", weights_z, np.eye(per)).reshape(per * fine_z, 128)
    table_z = jnp.concatenate(two_terms(table_z), axis=1)
    all_rows = groups * ranks
    lanes = edges_x * coarse_y * coarse_z - 256
    chunks = 2 * groups
    anywhere = pl.BlockSpec(memory_space=pl.ANY)
    vmem = pl.BlockSpec(memory_space=pltpu.VMEM)
    series = steps_t * cells
    return pl.pallas_call(
        restrict_kernel,
        in_specs=[pl.BlockSpec(memory_space=pltpu.SMEM)] + [anywhere] * 4,
        out_specs=[vmem] * 3,
        out_shape=[jax.ShapeDtypeStruct((all_rows, n), F32) for n in (lanes, 128, 128)],
        scratch_shapes=[
            pltpu.VMEM((edges_x * coarse_y * all_rows, fine_z), F32),
            pltpu.VMEM((all_rows * series, fine_z), BF16),
            pltpu.VMEM((groups, series, fine_z), BF16),
            pltpu.VMEM((groups, series, fine_z), F32),
            pltpu.VMEM(table_xy.shape, BF16),
            pltpu.VMEM(table_z.shape, BF16),
            pltpu.SemaphoreType.DMA((chunks,)),
            pltpu.SemaphoreType.DMA((3,)),
        ],
        compiler_params=pltpu.CompilerParams(vmem_limit_bytes=FULL_VMEM),
        name="restrict",
    )(
        side,
        probes.reshape(all_rows * series, fine_z),
        sources.reshape(groups, series, fine_z),
        table_xy,
        table_z,
    )


def products_kernel(ranks, place, *refs):
    *leaves, sketch, chosen, keep, send, keep_far, send_far, table = refs
    rows = leaves[0].shape[0]
    for i, leaf in enumerate(leaves):
        table[i * rows : (i + 1) * rows, :] = leaf[...]
    picked = chosen.shape[0] // ranks
    for i in range(picked):
        at = pl.multiple_of(place[i] * ranks, ranks)
        chosen[i * ranks : (i + 1) * ranks, :] = table[pl.ds(at, ranks), :]
    pieces = chosen[...]
    gram = dot_nt(pieces, pieces)
    cross = dot_nt(pieces, sketch[...])
    block = lambda i, j: gram[i * ranks : (i + 1) * ranks, j * ranks : (j + 1) * ranks]
    row = lambda *xs: jnp.concatenate(xs, axis=1)
    column = lambda *xs: jnp.concatenate(xs, axis=0)
    solo = lambda i: row(block(i, i), cross[i * ranks : (i + 1) * ranks])
    half = ranks // 2
    fold = lambda x: row(x[:half], x[half:])
    near = [column(solo(0), solo(1)), column(solo(2), solo(3))]
    far = [
        column(row(block(0, 2), block(0, 3)), fold(block(0, 1))),
        column(row(block(1, 2), block(1, 3)), fold(block(2, 3))),
    ]
    low = place[picked] == 0
    keep[...] = jnp.where(low, near[0], near[1])
    send[...] = jnp.where(low, near[1], near[0])
    keep_far[...] = jnp.where(low, far[0], far[1])
    send_far[...] = jnp.where(low, far[1], far[0])


def products(leaves, sketch, place, ranks):
    rows, lanes = leaves[0].shape
    count = len(leaves)
    half = (count * rows // ranks // 2) * ranks
    vmem = pl.BlockSpec(memory_space=pltpu.VMEM)
    near = jax.ShapeDtypeStruct((2 * ranks, 2 * ranks), F32)
    far = jax.ShapeDtypeStruct((3 * ranks // 2, 2 * ranks), F32)
    return pl.pallas_call(
        lambda *refs: products_kernel(ranks, *refs),
        in_specs=[pl.BlockSpec(memory_space=pltpu.SMEM)] + [vmem] * (count + 1),
        out_specs=[vmem] * 5,
        out_shape=[jax.ShapeDtypeStruct((half, lanes), BF16), near, near, far, far],
        scratch_shapes=[pltpu.VMEM((count * rows, lanes), BF16)],
        compiler_params=pltpu.CompilerParams(vmem_limit_bytes=VMEM_BYTES),
        name="products",
    )(place, *leaves, sketch)


def ridge_solve(systems):
    size = systems[0].shape[0]
    blocks = size // 8
    shape = (size, 2 * size)
    eye = lax.broadcasted_iota(jnp.int32, shape, 0) == lax.broadcasted_iota(jnp.int32, shape, 1)
    start = []
    for system in systems:
        trace = jnp.sum(jnp.where(eye, system, 0.0))
        system = system + jnp.where(eye, 0.01 * trace / size + 1e-06, 0.0)
        start.append(tuple(system[8 * i : 8 * i + 8] for i in range(blocks)))
    sub = lax.broadcasted_iota(jnp.int32, (8, 2 * size), 0)

    def eliminate(_, mats):
        done = []
        for mat in mats:
            head = mat[0]
            columns = [jnp.broadcast_to(head[:, j : j + 1], head.shape) for j in range(8)]
            for j in range(8):
                inverse = 1.0 / columns[j][j : j + 1]
                here = sub == j
                row = head[j : j + 1] * inverse
                head = jnp.where(here, row, head - columns[j] * row)
                for m in range(j + 1, 8):
                    entry = columns[m][j : j + 1] * inverse
                    columns[m] = jnp.where(here, entry, columns[m] - columns[j] * entry)
            rest = []
            for block in mat[1:]:
                new = block
                for j in range(8):
                    new = new - block[:, j : j + 1] * head[j : j + 1]
                rest.append(new)
            done.append(tuple(pltpu.roll(x, 2 * size - 8, 1) for x in rest + [head]))
        return tuple(done)

    mats = lax.fori_loop(0, blocks, eliminate, tuple(start))
    return [jnp.concatenate(mat, axis=0)[:, :size].astype(BF16) for mat in mats]


def flip(x):
    return x.astype(F32).T.astype(BF16)


def leaf_kernel(near, coefs):
    size = near.shape[0] // 2
    a, b = ridge_solve([near[:size], near[size:]])
    coefs[:size, :] = a
    coefs[size:, :] = b


def pair_kernel(scaling, near, far, coefs, out):
    size = near.shape[0] // 2
    half = size // 2
    row = lambda *xs: jnp.concatenate(xs, axis=1)
    column = lambda *xs: jnp.concatenate(xs, axis=0)
    corner = column(far[size:, :size], far[size:, size:])
    joint = column(row(near[:size, :size], corner), row(corner.T, near[size:, :size]))
    cross = column(near[:size, size:], near[size:, size:])
    both = coefs[...]
    both_t = flip(both)
    gram = scaling * scaling * dot_wide(both_t, wide_dot(joint, both))
    system = row(gram, scaling * dot_wide(both_t, cross))
    (own,) = ridge_solve([system])
    out[:size, :] = system
    out[size : 2 * size, :] = far[:size, :]
    out[2 * size : 3 * size, :] = row(both[:size], both[size:]).astype(F32)
    out[3 * size :, :] = row(own[:half], own[half:]).astype(F32)


def root_kernel(scaling, place, mine, other, pieces, own, send, table):
    size = mine.shape[1] // 2
    half = size // 2
    row = lambda *xs: jnp.concatenate(xs, axis=1)
    column = lambda *xs: jnp.concatenate(xs, axis=0)
    low = place[0] == 0
    p = jnp.where(low, mine[...], other[...])
    q = jnp.where(low, other[...], mine[...])
    corner = column(p[size : 2 * size], q[size : 2 * size])
    coefs = [x[2 * size : 3 * size].astype(BF16) for x in (p, q)]
    coefs = [column(x[:, :size], x[:, size:]) for x in coefs]
    coefs_t = [flip(x) for x in coefs]
    tops = [x[3 * size :].astype(BF16) for x in (p, q)]
    tops = [column(x[:, :size], x[:, size:]) for x in tops]
    tops_t = [flip(x) for x in tops]
    square = scaling * scaling
    corner = square * dot_wide(coefs_t[0], wide_dot(corner, coefs[1]))
    joint = column(row(p[:size, :size], corner), row(corner.T, q[:size, :size]))
    both, both_t = column(*tops), row(*tops_t)
    gram = square * dot_wide(both_t, wide_dot(joint, both))
    cross = scaling * dot_wide(both_t, column(p[:size, size:], q[:size, size:]))
    (last,) = ridge_solve([row(gram, cross)])
    last_t = flip(last)
    total_t = row(*(wide_dot(dot(last_t, t), c) for t, c in zip(tops_t, coefs_t)))
    result = (square * scaling) * sum(dot(part, pieces[...]) for part in halves(total_t))
    table[:size, :] = result[:, : 2 * size]
    table[size:, :] = result[:, 2 * size :]
    count = own.shape[0]
    for out, at in ((own, place[1]), (send, place[2])):
        at = pl.multiple_of(at * count, count)
        for i in range(2):
            out[:, i * 2 * size : (i + 1) * 2 * size] = table[pl.ds(at + i * size, count), :]


def local_call(kernel, name, out, *args, scalars=(), scratch=(), flops=1 << 24):
    vmem = pl.BlockSpec(memory_space=pltpu.VMEM)
    smem = pl.BlockSpec(memory_space=pltpu.SMEM)
    return pl.pallas_call(
        kernel,
        in_specs=[smem] * len(scalars) + [vmem] * len(args),
        out_specs=jax.tree.map(lambda _: vmem, out),
        out_shape=out,
        scratch_shapes=scratch,
        compiler_params=pltpu.CompilerParams(vmem_limit_bytes=VMEM_BYTES),
        cost_estimate=pl.CostEstimate(flops=flops, bytes_accessed=1 << 17, transcendentals=0),
        name=name,
    )(*scalars, *args)


def swap(x, axis, mask):
    return lax.ppermute(x, axis, [(i, i ^ mask) for i in range(lax.axis_size(axis))])


def body(probes, sources, sketch, pairing):
    groups, ranks = probes.shape[:2]
    coarse_x = probes.shape[3] // 4
    layer = sketch.shape[2]
    shots, space = lax.axis_size("shots"), lax.axis_size("space")
    shot, place = lax.axis_index("shots"), lax.axis_index("space")
    scaling = math.sqrt(coarse_x * space * layer / ranks)
    side = place % 2

    own, to_core, to_chip = restrict(probes, sources, side[None].astype(jnp.int32))
    from_core = swap(to_core, "space", 1)
    across = [(i, i + 1 if i % 2 else i - 1) for i in range(space)]
    from_chip = lax.ppermute(to_chip, "space", [(i, j) for i, j in across if 0 <= j < space])
    from_below = jnp.where(side == 0, from_chip, from_core)
    from_above = jnp.where(side == 0, from_core, from_chip)
    leaf = (own + jnp.concatenate([from_below, from_above], axis=1)).astype(BF16)

    leaves = [leaf] + [swap(leaf, "shots", m) for m in range(1, shots)]
    picked = shots * groups // 2
    chosen = lax.dynamic_slice_in_dim(pairing, shot // (shots // 2) * picked, picked)
    slots = (chosen // groups ^ shot) * groups + chosen % groups
    sketch_t = jnp.transpose(sketch, (1, 0, 2)).reshape(ranks, coarse_x * layer)
    slots = jnp.concatenate([slots, side[None]]).astype(jnp.int32)
    pieces, near, send, far, send_far = products(leaves, sketch_t, slots, ranks)

    near = near + swap(send, "space", 1)
    far = far + swap(send_far, "space", 1)
    mask = 2
    while mask < space:
        near = near + swap(near, "space", mask)
        far = far + swap(far, "space", mask)
        mask *= 2
    coefs = local_call(
        leaf_kernel, "leaf_coefs", jax.ShapeDtypeStruct((2 * ranks, ranks), BF16), near,
        flops=1 << 32,
    )
    mine = local_call(
        lambda *refs: pair_kernel(scaling, *refs), "pair",
        jax.ShapeDtypeStruct((7 * ranks // 2, 2 * ranks), F32), near, far, coefs,
    )
    other = swap(mine, "space", 1)

    columns = ranks // shots
    across_tree = shots // 2
    spots = jnp.stack([side, shot, shot ^ across_tree]).astype(jnp.int32)
    part = jax.ShapeDtypeStruct((columns, pieces.shape[1]), F32)
    own_part, sent = local_call(
        lambda *refs: root_kernel(scaling, *refs), "root", [part, part], mine, other, pieces,
        scalars=(spots,), scratch=[pltpu.VMEM((2 * ranks, 2 * ranks), F32)],
    )
    total = (own_part + swap(sent, "shots", across_tree)).astype(BF16)
    return jnp.transpose(total.reshape(columns, coarse_x, layer), (1, 0, 2))


def solution(mesh):
    in_specs = (
        P("shots", None, None, "space", None, None),
        P("shots", None, "space", None, None),
        P("space", None, None),
        P(),
    )
    out_specs = P("space", "shots", None)
    return jax.shard_map(body, mesh=mesh, in_specs=in_specs, out_specs=out_specs, check_vma=False)
```

time: 65.2 us -> 52.2 us (0.80)
  Pallas kernels: 24.9 us -> 17.1 us
  waiting for transfers between devices: 21.2 us -> 15 us
  starting transfers between devices: 14.8 us -> 17.8 us
  local copies, waits for them, and re-layouts: 3.46 us -> 0.88 us
  other arithmetic: 0.3 us -> 1.23 us
    pallas_call x2 -> x4, Pallas kernels: 24.1 us -> 16.2 us  [the longest x3 9.76 us: local_call(): pl.pallas_call(kernel, in_specs=[smem] * len(scalars) + [vmem] * len(args...]
    ppermute x8 -> x12, starting transfers between devices: 11.1 us -> 17.2 us  [swap(): lax.ppermute(x, axis, [(i, i ^ mask) for i in range(lax.axis_size(axis))])]
    ppermute x2 -> x1, waiting for transfers between devices: 3.73 us -> 0.01 us  [body(): lax.ppermute(to_chip, 'space', [(i, j) for i, j in across if 0 <= j < spa...]
    ppermute x2 -> x1, starting transfers between devices: 3.65 us -> 0.66 us  [body(): lax.ppermute(to_chip, 'space', [(i, j) for i, j in across if 0 <= j < spa...]
    unnamed x10 -> x4, local copies, waits for them, and re-layouts: 2.59 us -> 0.01 us
    ppermute x8 -> x12, waiting for transfers between devices: 17.5 us -> 15 us  [swap(): lax.ppermute(x, axis, [(i, i ^ mask) for i in range(lax.axis_size(axis))])]
    convert_element_type x1, other arithmetic: 0.02 us -> 0.92 us  [body(): (own + jnp.concatenate([from_below, from_above], axis=1)).astype(BF16)]
  transfers between devices with their start and end apart: 10 -> 13, of which waited for: 9 -> 9; matrix products, arithmetic and copies ran while one was open for 1% -> 1% of each run, Pallas kernels for 0% -> 0%
where the time goes in v2:
time: 52.2 us; the launch traced here: 52.1 us
  starting transfers between devices  17.8 us (34%)
  Pallas kernels  17.1 us (33%)
  waiting for transfers between devices  15 us (29%)
  other arithmetic  1.23 us (2%)
  local copies, waits for them, and re-layouts  0.88 us (2%)
    ppermute x12, starting transfers between devices, swap(): lax.ppermute(x, axis, [(i, i ^ mask) for i in range(lax.axis_size(axis))])  17.2 us
    ppermute x12, waiting for transfers between devices, swap(): lax.ppermute(x, axis, [(i, i ^ mask) for i in range(lax.axis_size(axis))])  15 us
    pallas_call x3, Pallas kernels, local_call(): pl.pallas_call(kernel, in_specs=[smem] * len(scalars) + [vmem] * len(args...  9.76 us
    pallas_call x1, Pallas kernels, restrict(): pl.pallas_call(restrict_kernel, in_specs=[pl.BlockSpec(memory_space=pltpu...  6.43 us
  transfers between devices with their start and end apart: 13, of which 9 were waited for; matrix products, arithmetic and copies ran while one was open for 1% of the time, Pallas kernels for 0%

profile of v2, /device:TPU:0, one launch (start us, length us, event | category | flops | bytes accessed | tf_op | source)
XLA Modules:
  0.0 52.1 jit_solution(16829359510855262073)
XLA Ops:
  0.0 0.0 copy-start
  0.0 0.0 copy-start.1
  0.0 6.4 %restrict.1 = (f32[128,256]{1,0:T(8,128)}, f32[128,128]{1,0:T(8,128)}, f32[128,128]{1,0:T(8,128)}) custom-call(s32[1]{0:T(128)} %bitcast.side, bf16[32768,128]{1,0:T(8,128)(2,1)} %bitcast.9, bf16[2,256,128]{2,1,0:T(8,128)(2,1)} %bitcast.10, bf16[32,256]{1,0:T(8,128)(2,1)} %constant.70.table_xy, bf16[512,256]{1,0:T(8,128)(2,1)} %constant.75.table_z), custom_call_target="tpu_custom_call" | custom-call | tf_op jit(solution)/shard_map/restrict/pallas_call | solution.py:151
  6.4 0.7 %collective-permute-start = (f32[128,128]{1,0:T(8,128)}, f32[128,128]{1,0:T(8,128)S(1)}, u32[]{:S(2)}, u32[]{:S(2)}) collective-permute-start(f32[128,128]{1,0:T(8,128)} %get-tuple-element.16), channel_id=1, source_target_pairs={{1,2},{2,1},{3,4},{4,3},{5,6},{6,5},{9,10},{10,9},{11,12},{12,11},... | collective-permute-start | bytes 196616 | tf_op jit(solution)/shard_map/ppermute | solution.py:358
  7.1 4.5 %collective-permute-start.1 = (f32[128,128]{1,0:T(8,128)}, f32[128,128]{1,0:T(8,128)S(1)}, u32[]{:S(2)}, u32[]{:S(2)}) collective-permute-start(f32[128,128]{1,0:T(8,128)} %get-tuple-element.17), channel_id=1, source_target_pairs={{0,1},{1,0},{2,3},{3,2},{4,5},{5,4},{6,7},{7,6},{8,9},{9,8},{10,11... | collective-permute-start | bytes 196616 | tf_op jit(solution)/shard_map/ppermute | solution.py:343
  11.6 0.0 copy-done
  11.6 0.1 copy.7
  11.6 0.1 reshape.14.refs_5_
  11.8 0.0 copy-done.1
  11.8 0.1 fusion.1
  11.9 0.0 collective-permute-done
  11.9 0.8 %collective-permute-done.1 = f32[128,128]{1,0:T(8,128)S(1)} collective-permute-done((f32[128,128]{1,0:T(8,128)}, f32[128,128]{1,0:T(8,128)S(1)}, u32[]{:S(2)}, u32[]{:S(2)}) %collective-permute-start.1) | collective-permute-done | bytes 65568 | tf_op jit(solution)/shard_map/ppermute | solution.py:343
  12.7 0.9 %fusion.refs_1_ = bf16[128,256]{1,0:T(8,128)(2,1)S(1)} fusion(f32[128,256]{1,0:T(8,128)} %get-tuple-element.15, f32[128,128]{1,0:T(8,128)S(1)} %get-tuple-element.26, f32[128,128]{1,0:T(8,128)S(1)} %get-tuple-element.25), kind=kLoop, calls=%fused_computation.1 | loop fusion | flops 98304 | bytes 327680 | tf_op jit(solution)/shard_map/convert_element_type | solution.py:361
  13.6 2.5 %collective-permute-start.4 = (bf16[128,256]{1,0:T(8,128)(2,1)S(1)}, bf16[128,256]{1,0:T(8,128)(2,1)S(1)}, u32[]{:S(2)}, u32[]{:S(2)}) collective-permute-start(bf16[128,256]{1,0:T(8,128)(2,1)S(1)} %fusion.refs_1_), channel_id=1, source_target_pairs={{0,24},{8,16},{16,8},{24,0},{1,25},{9,17},{17,9},{25,1},{2,26},{10... | collective-permute-start | bytes 196616 | tf_op jit(solution)/shard_map/ppermute | solution.py:343
  16.1 0.5 collective-permute-start.3
  16.6 0.6 %collective-permute-start.2 = (bf16[128,256]{1,0:T(8,128)(2,1)S(1)}, bf16[128,256]{1,0:T(8,128)(2,1)S(1)}, u32[]{:S(2)}, u32[]{:S(2)}) collective-permute-start(bf16[128,256]{1,0:T(8,128)(2,1)S(1)} %fusion.refs_1_), channel_id=1, source_target_pairs={{0,8},{8,0},{16,24},{24,16},{1,9},{9,1},{17,25},{25,17},{2,10},{10... | collective-permute-start | bytes 196616 | tf_op jit(solution)/shard_map/ppermute | solution.py:343
  17.2 0.1 pad_add_fusion.1.refs_0_
  17.3 2.3 %collective-permute-done.4.refs_4_ = bf16[128,256]{1,0:T(8,128)(2,1)S(1)} collective-permute-done((bf16[128,256]{1,0:T(8,128)(2,1)S(1)}, bf16[128,256]{1,0:T(8,128)(2,1)S(1)}, u32[]{:S(2)}, u32[]{:S(2)}) %collective-permute-start.4) | collective-permute-done | bytes 65568 | tf_op jit(solution)/shard_map/ppermute | solution.py:343
  19.6 1.4 %collective-permute-done.3.refs_3_ = bf16[128,256]{1,0:T(8,128)(2,1)S(1)} collective-permute-done((bf16[128,256]{1,0:T(8,128)(2,1)S(1)}, bf16[128,256]{1,0:T(8,128)(2,1)S(1)}, u32[]{:S(2)}, u32[]{:S(2)}) %collective-permute-start.3) | collective-permute-done | bytes 65568 | tf_op jit(solution)/shard_map/ppermute | solution.py:343
  21.0 0.1 collective-permute-done.2.refs_2_
  21.1 0.9 %products.1 = (bf16[256,256]{1,0:T(8,128)(2,1)S(1)}, f32[128,128]{1,0:T(8,128)S(1)}, f32[128,128]{1,0:T(8,128)S(1)}, f32[96,128]{1,0:T(8,128)S(1)}, f32[96,128]{1,0:T(8,128)S(1)}) custom-call(s32[5]{0:T(128)S(1)} %pad_add_fusion.1.refs_0_, bf16[128,256]{1,0:T(8,128)(2,1)S(1)} %fusion.refs_1_, bf16[128,256]{1,0:T(8,128)(2,1)S(1)} %collective-permute-done.2.refs_2_, ...), custom_call_target="tpu_custom_call" | custom-call | tf_op jit(solution)/shard_map/products/pallas_call | solution.py:214
  22.0 0.1 collective-permute-start.5
  22.0 0.5 collective-permute-start.8
  22.5 0.7 %collective-permute-done.5 = f32[128,128]{1,0:T(8,128)S(1)} collective-permute-done((f32[128,128]{1,0:T(8,128)S(1)}, f32[128,128]{1,0:T(8,128)S(1)}, u32[]{:S(2)}, u32[]{:S(2)}) %collective-permute-start.5) | collective-permute-done | bytes 65568 | tf_op jit(solution)/shard_map/ppermute | solution.py:343
  23.3 2.5 %collective-permute-start.6 = (f32[128,128]{1,0:T(8,128)S(1)}, f32[128,128]{1,0:T(8,128)S(1)}, u32[]{:S(2)}, u32[]{:S(2)}) collective-permute-start(f32[128,128]{1,0:T(8,128)S(1)} %add.47), channel_id=1, source_target_pairs={{0,2},{1,3},{2,0},{3,1},{4,6},{5,7},{6,4},{7,5},{8,10},{9,11},{10,... | collective-permute-start | bytes 196616 | tf_op jit(solution)/shard_map/ppermute | solution.py:343
  25.8 0.0 collective-permute-done.8
  25.8 0.1 collective-permute-start.9
  25.9 2.3 %collective-permute-done.6 = f32[128,128]{1,0:T(8,128)S(1)} collective-permute-done((f32[128,128]{1,0:T(8,128)S(1)}, f32[128,128]{1,0:T(8,128)S(1)}, u32[]{:S(2)}, u32[]{:S(2)}) %collective-permute-start.6) | collective-permute-done | bytes 65568 | tf_op jit(solution)/shard_map/ppermute | solution.py:343
  28.2 3.2 %collective-permute-start.7 = (f32[128,128]{1,0:T(8,128)S(1)}, f32[128,128]{1,0:T(8,128)S(1)}, u32[]{:S(2)}, u32[]{:S(2)}) collective-permute-start(f32[128,128]{1,0:T(8,128)S(1)} %add.48), channel_id=1, source_target_pairs={{0,4},{1,5},{2,6},{3,7},{4,0},{5,1},{6,2},{7,3},{8,12},{9,13},{10,... | collective-permute-start | bytes 196616 | tf_op jit(solution)/shard_map/ppermute | solution.py:343
  31.4 0.0 collective-permute-done.9
  31.4 1.3 %collective-permute-start.10 = (f32[96,128]{1,0:T(8,128)S(1)}, f32[96,128]{1,0:T(8,128)S(1)}, u32[]{:S(2)}, u32[]{:S(2)}) collective-permute-start(f32[96,128]{1,0:T(8,128)S(1)} %add.51), channel_id=1, source_target_pairs={{0,4},{1,5},{2,6},{3,7},{4,0},{5,1},{6,2},{7,3},{8,12},{9,13},{10,... | collective-permute-start | bytes 147464 | tf_op jit(solution)/shard_map/ppermute | solution.py:343
  32.6 3.8 %collective-permute-done.10 = f32[96,128]{1,0:T(8,128)S(1)} collective-permute-done((f32[96,128]{1,0:T(8,128)S(1)}, f32[96,128]{1,0:T(8,128)S(1)}, u32[]{:S(2)}, u32[]{:S(2)}) %collective-permute-start.10) | collective-permute-done | bytes 49184 | tf_op jit(solution)/shard_map/ppermute | solution.py:343
  36.4 0.0 collective-permute-done.7
  36.5 3.0 %leaf_coefs.1.refs_2_ = bf16[128,64]{1,0:T(8,128)(2,1)S(1)} custom-call(f32[128,128]{1,0:T(8,128)S(1)} %add.49.near.refs_0_), custom_call_target="tpu_custom_call" | custom-call | flops 4294967296 | bytes 131072 | tf_op jit(solution)/shard_map/leaf_coefs/pallas_call | solution.py:330
  39.5 2.7 %pair.1.refs_1_ = f32[224,128]{1,0:T(8,128)S(1)} custom-call(f32[128,128]{1,0:T(8,128)S(1)} %add.49.near.refs_0_, f32[96,128]{1,0:T(8,128)S(1)} %add.52.refs_1_, bf16[128,64]{1,0:T(8,128)(2,1)S(1)} %leaf_coefs.1.refs_2_), custom_call_target="tpu_custom_call" | custom-call | flops 16777216 | bytes 131072 | tf_op jit(solution)/shard_map/pair/pallas_call | solution.py:330
  42.2 0.0 collective-permute-start.11
  42.2 0.1 pad_add_fusion.refs_0_
  42.3 1.2 %collective-permute-done.11.refs_2_ = f32[224,128]{1,0:T(8,128)S(1)} collective-permute-done((f32[224,128]{1,0:T(8,128)S(1)}, f32[224,128]{1,0:T(8,128)S(1)}, u32[]{:S(2)}, u32[]{:S(2)}) %collective-permute-start.11) | collective-permute-done | bytes 114720 | tf_op jit(solution)/shard_map/ppermute | solution.py:343
  43.5 4.1 %root.1 = (f32[16,256]{1,0:T(8,128)S(1)}, f32[16,256]{1,0:T(8,128)S(1)}) custom-call(s32[3]{0:T(128)S(1)} %pad_add_fusion.refs_0_, f32[224,128]{1,0:T(8,128)S(1)} %pair.1.refs_1_, f32[224,128]{1,0:T(8,128)S(1)} %collective-permute-done.11.refs_2_, bf16[256,256]{1,0:T(8,128)(2,1)S(1)} %get-tuple-element.22.refs_3_), custom_call_target="tpu_custom_call" | custom-call | flops 16777216 | bytes 131072 | tf_op jit(solution)/shard_map/root/pallas_call | solution.py:330
  47.6 1.5 %collective-permute-start.12 = (f32[16,256]{1,0:T(8,128)S(1)}, f32[16,256]{1,0:T(8,128)S(1)}, u32[]{:S(2)}, u32[]{:S(2)}) collective-permute-start(f32[16,256]{1,0:T(8,128)S(1)} %get-tuple-element.24), channel_id=1, source_target_pairs={{0,16},{8,24},{16,0},{24,8},{1,17},{9,25},{17,1},{25,9},{2,18},{10... | collective-permute-start | bytes 49160 | tf_op jit(solution)/shard_map/ppermute | solution.py:343
  49.1 2.3 %collective-permute-done.12 = f32[16,256]{1,0:T(8,128)S(1)} collective-permute-done((f32[16,256]{1,0:T(8,128)S(1)}, f32[16,256]{1,0:T(8,128)S(1)}, u32[]{:S(2)}, u32[]{:S(2)}) %collective-permute-start.12) | collective-permute-done | bytes 16416 | tf_op jit(solution)/shard_map/ppermute | solution.py:343
  51.4 0.1 reshape.15
  51.5 0.6 %copy.10 = bf16[16,4,64]{2,0,1:T(8,128)(2,1)} copy(bf16[16,4,64]{2,1,0:T(4,128)(2,1)S(1)} %reshape.15) | data formatting | bytes 16384 | tf_op jit(solution)/shard_map/reshape | solution.py:397
  (8 shorter events, 0.1 us)
Async XLA Ops:
  0.0 11.6 %copy-start = (bf16[4,64,64]{2,1,0:T(8,128)(2,1)S(1)}, bf16[4,64,64]{2,1,0:T(8,128)(2,1)}, u32[]{:S(2)}) copy-start(bf16[4,64,64]{2,1,0:T(8,128)(2,1)} %param.8) | copy-start | bytes 98308
  0.0 11.8 %copy-start.1 = (s32[8]{0:T(128)S(1)}, s32[8]{0:T(128)}, u32[]{:S(2)}) copy-start(s32[8]{0:T(128)} %param.9) | copy-start | bytes 100
  6.4 5.4 %collective-permute-start = (f32[128,128]{1,0:T(8,128)}, f32[128,128]{1,0:T(8,128)S(1)}, u32[]{:S(2)}, u32[]{:S(2)}) collective-permute-start(f32[128,128]{1,0:T(8,128)} %get-tuple-element.16), channel_id=1, source_target_pairs={{1,2},{2,1},{3,4},{4,3},{5,6},{6,5},{9,10},{10,9},{11,12},{12,11},... | collective-permute-start | bytes 196616 | tf_op jit(solution)/shard_map/ppermute | solution.py:358
  7.1 5.6 %collective-permute-start.1 = (f32[128,128]{1,0:T(8,128)}, f32[128,128]{1,0:T(8,128)S(1)}, u32[]{:S(2)}, u32[]{:S(2)}) collective-permute-start(f32[128,128]{1,0:T(8,128)} %get-tuple-element.17), channel_id=1, source_target_pairs={{0,1},{1,0},{2,3},{3,2},{4,5},{5,4},{6,7},{7,6},{8,9},{9,8},{10,11... | collective-permute-start | bytes 196616 | tf_op jit(solution)/shard_map/ppermute | solution.py:343
  13.6 5.9 %collective-permute-start.4 = (bf16[128,256]{1,0:T(8,128)(2,1)S(1)}, bf16[128,256]{1,0:T(8,128)(2,1)S(1)}, u32[]{:S(2)}, u32[]{:S(2)}) collective-permute-start(bf16[128,256]{1,0:T(8,128)(2,1)S(1)} %fusion.refs_1_), channel_id=1, source_target_pairs={{0,24},{8,16},{16,8},{24,0},{1,25},{9,17},{17,9},{25,1},{2,26},{10... | collective-permute-start | bytes 196616 | tf_op jit(solution)/shard_map/ppermute | solution.py:343
  16.1 4.8 %collective-permute-start.3 = (bf16[128,256]{1,0:T(8,128)(2,1)S(1)}, bf16[128,256]{1,0:T(8,128)(2,1)S(1)}, u32[]{:S(2)}, u32[]{:S(2)}) collective-permute-start(bf16[128,256]{1,0:T(8,128)(2,1)S(1)} %fusion.refs_1_), channel_id=1, source_target_pairs={{0,16},{8,24},{16,0},{24,8},{1,17},{9,25},{17,1},{25,9},{2,18},{10... | collective-permute-start | bytes 196616 | tf_op jit(solution)/shard_map/ppermute | solution.py:343
  16.6 4.4 %collective-permute-start.2 = (bf16[128,256]{1,0:T(8,128)(2,1)S(1)}, bf16[128,256]{1,0:T(8,128)(2,1)S(1)}, u32[]{:S(2)}, u32[]{:S(2)}) collective-permute-start(bf16[128,256]{1,0:T(8,128)(2,1)S(1)} %fusion.refs_1_), channel_id=1, source_target_pairs={{0,8},{8,0},{16,24},{24,16},{1,9},{9,1},{17,25},{25,17},{2,10},{10... | collective-permute-start | bytes 196616 | tf_op jit(solution)/shard_map/ppermute | solution.py:343
  22.0 1.3 %collective-permute-start.5 = (f32[128,128]{1,0:T(8,128)S(1)}, f32[128,128]{1,0:T(8,128)S(1)}, u32[]{:S(2)}, u32[]{:S(2)}) collective-permute-start(f32[128,128]{1,0:T(8,128)S(1)} %get-tuple-element.19), channel_id=1, source_target_pairs={{0,1},{1,0},{2,3},{3,2},{4,5},{5,4},{6,7},{7,6},{8,9},{9,8},{10,11... | collective-permute-start | bytes 196616 | tf_op jit(solution)/shard_map/ppermute | solution.py:343
  22.0 3.8 %collective-permute-start.8 = (f32[96,128]{1,0:T(8,128)S(1)}, f32[96,128]{1,0:T(8,128)S(1)}, u32[]{:S(2)}, u32[]{:S(2)}) collective-permute-start(f32[96,128]{1,0:T(8,128)S(1)} %get-tuple-element.21), channel_id=1, source_target_pairs={{0,1},{1,0},{2,3},{3,2},{4,5},{5,4},{6,7},{7,6},{8,9},{9,8},{10,11... | collective-permute-start | bytes 147464 | tf_op jit(solution)/shard_map/ppermute | solution.py:343
  23.3 4.9 %collective-permute-start.6 = (f32[128,128]{1,0:T(8,128)S(1)}, f32[128,128]{1,0:T(8,128)S(1)}, u32[]{:S(2)}, u32[]{:S(2)}) collective-permute-start(f32[128,128]{1,0:T(8,128)S(1)} %add.47), channel_id=1, source_target_pairs={{0,2},{1,3},{2,0},{3,1},{4,6},{5,7},{6,4},{7,5},{8,10},{9,11},{10,... | collective-permute-start | bytes 196616 | tf_op jit(solution)/shard_map/ppermute | solution.py:343
  25.8 5.6 %collective-permute-start.9 = (f32[96,128]{1,0:T(8,128)S(1)}, f32[96,128]{1,0:T(8,128)S(1)}, u32[]{:S(2)}, u32[]{:S(2)}) collective-permute-start(f32[96,128]{1,0:T(8,128)S(1)} %add.50), channel_id=1, source_target_pairs={{0,2},{1,3},{2,0},{3,1},{4,6},{5,7},{6,4},{7,5},{8,10},{9,11},{10,... | collective-permute-start | bytes 147464 | tf_op jit(solution)/shard_map/ppermute | solution.py:343
  28.2 8.2 %collective-permute-start.7 = (f32[128,128]{1,0:T(8,128)S(1)}, f32[128,128]{1,0:T(8,128)S(1)}, u32[]{:S(2)}, u32[]{:S(2)}) collective-permute-start(f32[128,128]{1,0:T(8,128)S(1)} %add.48), channel_id=1, source_target_pairs={{0,4},{1,5},{2,6},{3,7},{4,0},{5,1},{6,2},{7,3},{8,12},{9,13},{10,... | collective-permute-start | bytes 196616 | tf_op jit(solution)/shard_map/ppermute | solution.py:343
  31.4 5.1 %collective-permute-start.10 = (f32[96,128]{1,0:T(8,128)S(1)}, f32[96,128]{1,0:T(8,128)S(1)}, u32[]{:S(2)}, u32[]{:S(2)}) collective-permute-start(f32[96,128]{1,0:T(8,128)S(1)} %add.51), channel_id=1, source_target_pairs={{0,4},{1,5},{2,6},{3,7},{4,0},{5,1},{6,2},{7,3},{8,12},{9,13},{10,... | collective-permute-start | bytes 147464 | tf_op jit(solution)/shard_map/ppermute | solution.py:343
  42.2 1.3 %collective-permute-start.11 = (f32[224,128]{1,0:T(8,128)S(1)}, f32[224,128]{1,0:T(8,128)S(1)}, u32[]{:S(2)}, u32[]{:S(2)}) collective-permute-start(f32[224,128]{1,0:T(8,128)S(1)} %pair.1.refs_1_), channel_id=1, source_target_pairs={{0,1},{1,0},{2,3},{3,2},{4,5},{5,4},{6,7},{7,6},{8,9},{9,8},{10,11... | collective-permute-start | bytes 344072 | tf_op jit(solution)/shard_map/ppermute | solution.py:343
  47.6 3.8 %collective-permute-start.12 = (f32[16,256]{1,0:T(8,128)S(1)}, f32[16,256]{1,0:T(8,128)S(1)}, u32[]{:S(2)}, u32[]{:S(2)}) collective-permute-start(f32[16,256]{1,0:T(8,128)S(1)} %get-tuple-element.24), channel_id=1, source_target_pairs={{0,16},{8,24},{16,0},{24,8},{1,17},{9,25},{17,1},{25,9},{2,18},{10... | collective-permute-start | bytes 49160 | tf_op jit(solution)/shard_map/ppermute | solution.py:343

commit v3 on v2

--- a/solution.py
+++ b/solution.py
@@ -11,7 +11,7 @@
 F32 = jnp.float32
 BF16 = jnp.bfloat16
 VMEM_BYTES = 48 << 20
-FULL_VMEM = 60 << 20
+FRONT_VMEM = 24 << 20
 
 
 def spline_weights(fine_count, coarse_count, coarse_start):
@@ -145,14 +145,14 @@
     all_rows = groups * ranks
     lanes = edges_x * coarse_y * coarse_z - 256
     chunks = 2 * groups
-    anywhere = pl.BlockSpec(memory_space=pl.ANY)
+    outside = pl.BlockSpec(memory_space=pltpu.HBM)
     vmem = pl.BlockSpec(memory_space=pltpu.VMEM)
     series = steps_t * cells
     return pl.pallas_call(
         restrict_kernel,
-        in_specs=[pl.BlockSpec(memory_space=pltpu.SMEM)] + [anywhere] * 4,
+        in_specs=[pl.BlockSpec(memory_space=pltpu.SMEM)] + [outside] * 4,
         out_specs=[vmem] * 3,
-        out_shape=[jax.ShapeDtypeStruct((all_rows, n), F32) for n in (lanes, 128, 128)],
+        out_shape=[pltpu.VMEM((all_rows, n), F32) for n in (lanes, 128, 128)],
         scratch_shapes=[
             pltpu.VMEM((edges_x * coarse_y * all_rows, fine_z), F32),
             pltpu.VMEM((all_rows * series, fine_z), BF16),
@@ -163,14 +163,19 @@
             pltpu.SemaphoreType.DMA((chunks,)),
             pltpu.SemaphoreType.DMA((3,)),
         ],
-        compiler_params=pltpu.CompilerParams(vmem_limit_bytes=FULL_VMEM),
+        compiler_params=pltpu.CompilerParams(vmem_limit_bytes=FRONT_VMEM),
         name="restrict",
     )(
         side,
-        probes.reshape(all_rows * series, fine_z),
-        sources.reshape(groups, series, fine_z),
-        table_xy,
-        table_z,
+        *(
+            pltpu.with_memory_space_constraint(x, pltpu.HBM)
+            for x in (
+                probes.reshape(all_rows * series, fine_z),
+                sources.reshape(groups, series, fine_z),
+                table_xy,
+                table_z,
+            )
+        ),
     )
 
 
@@ -192,11 +197,8 @@
     solo = lambda i: row(block(i, i), cross[i * ranks : (i + 1) * ranks])
     half = ranks // 2
     fold = lambda x: row(x[:half], x[half:])
-    near = [column(solo(0), solo(1)), column(solo(2), solo(3))]
-    far = [
-        column(row(block(0, 2), block(0, 3)), fold(block(0, 1))),
-        column(row(block(1, 2), block(1, 3)), fold(block(2, 3))),
-    ]
+    near = [column(solo(i), solo(i + 1)) for i in (0, 2)]
+    far = [column(fold(block(2 * i, 2 * i + 1)), row(block(i, 2), block(i, 3))) for i in (0, 1)]
     low = place[picked] == 0
     keep[...] = jnp.where(low, near[0], near[1])
     send[...] = jnp.where(low, near[1], near[0])
@@ -227,93 +229,89 @@
     blocks = size // 8
     shape = (size, 2 * size)
     eye = lax.broadcasted_iota(jnp.int32, shape, 0) == lax.broadcasted_iota(jnp.int32, shape, 1)
-    start = []
+    mats = []
     for system in systems:
         trace = jnp.sum(jnp.where(eye, system, 0.0))
         system = system + jnp.where(eye, 0.01 * trace / size + 1e-06, 0.0)
-        start.append(tuple(system[8 * i : 8 * i + 8] for i in range(blocks)))
+        mats.append([system[8 * i : 8 * i + 8] for i in range(blocks)])
     sub = lax.broadcasted_iota(jnp.int32, (8, 2 * size), 0)
-
-    def eliminate(_, mats):
-        done = []
+    for k in range(blocks):
+        lane = 8 * k
         for mat in mats:
-            head = mat[0]
-            columns = [jnp.broadcast_to(head[:, j : j + 1], head.shape) for j in range(8)]
-            for j in range(8):
-                inverse = 1.0 / columns[j][j : j + 1]
-                here = sub == j
-                row = head[j : j + 1] * inverse
-                head = jnp.where(here, row, head - columns[j] * row)
-                for m in range(j + 1, 8):
-                    entry = columns[m][j : j + 1] * inverse
-                    columns[m] = jnp.where(here, entry, columns[m] - columns[j] * entry)
-            rest = []
-            for block in mat[1:]:
-                new = block
-                for j in range(8):
-                    new = new - block[:, j : j + 1] * head[j : j + 1]
-                rest.append(new)
-            done.append(tuple(pltpu.roll(x, 2 * size - 8, 1) for x in rest + [head]))
-        return tuple(done)
-
-    mats = lax.fori_loop(0, blocks, eliminate, tuple(start))
-    return [jnp.concatenate(mat, axis=0)[:, :size].astype(BF16) for mat in mats]
+            head = mat[k]
+            columns = [
+                jnp.broadcast_to(head[:, lane + j : lane + j + 1], head.shape) for j in range(8)
+            ]
+            for j in range(0, 8, 2):
+                left, right = columns[j], columns[j + 1]
+                a, b, c = left[j : j + 1], left[j + 1 : j + 2], right[j + 1 : j + 2]
+                inverse = 1.0 / (a * c - b * b)
+
+                def reduced(x):
+                    p, q = x[j : j + 1], x[j + 1 : j + 2]
+                    p, q = (c * p - b * q) * inverse, (a * q - b * p) * inverse
+                    rest = (x - left * p) - right * q
+                    return jnp.where(sub == j, p, jnp.where(sub == j + 1, q, rest))
+
+                head = reduced(head)
+                for m in range(j + 2, 8):
+                    columns[m] = reduced(columns[m])
+            for i in range(blocks):
+                if i != k:
+                    new = mat[i]
+                    for j in range(8):
+                        new = new - mat[i][:, lane + j : lane + j + 1] * head[j : j + 1]
+                    mat[i] = new
+            mat[k] = head
+    return [jnp.concatenate(mat, axis=0)[:, size:].astype(BF16) for mat in mats]
 
 
 def flip(x):
     return x.astype(F32).T.astype(BF16)
 
 
-def leaf_kernel(near, coefs):
-    size = near.shape[0] // 2
-    a, b = ridge_solve([near[:size], near[size:]])
-    coefs[:size, :] = a
-    coefs[size:, :] = b
-
-
-def pair_kernel(scaling, near, far, coefs, out):
-    size = near.shape[0] // 2
+def pair_kernel(scaling, near, far, out):
+    size = near.shape[1] // 2
     half = size // 2
     row = lambda *xs: jnp.concatenate(xs, axis=1)
     column = lambda *xs: jnp.concatenate(xs, axis=0)
-    corner = column(far[size:, :size], far[size:, size:])
+    corner = column(far[:half, :size], far[:half, size:])
     joint = column(row(near[:size, :size], corner), row(corner.T, near[size:, :size]))
     cross = column(near[:size, size:], near[size:, size:])
-    both = coefs[...]
+    both = column(*ridge_solve([near[:size], near[size:]]))
     both_t = flip(both)
     gram = scaling * scaling * dot_wide(both_t, wide_dot(joint, both))
     system = row(gram, scaling * dot_wide(both_t, cross))
     (own,) = ridge_solve([system])
     out[:size, :] = system
-    out[size : 2 * size, :] = far[:size, :]
-    out[2 * size : 3 * size, :] = row(both[:size], both[size:]).astype(F32)
-    out[3 * size :, :] = row(own[:half], own[half:]).astype(F32)
+    out[size : 2 * size, :] = dot(flip(own), both_t)
+    out[2 * size : 2 * size + half, :] = row(own[:half], own[half:]).astype(F32)
+    out[2 * size + half :, :] = far[half:, :]
 
 
 def root_kernel(scaling, place, mine, other, pieces, own, send, table):
     size = mine.shape[1] // 2
-    half = size // 2
     row = lambda *xs: jnp.concatenate(xs, axis=1)
     column = lambda *xs: jnp.concatenate(xs, axis=0)
     low = place[0] == 0
-    p = jnp.where(low, mine[...], other[...])
-    q = jnp.where(low, other[...], mine[...])
-    corner = column(p[size : 2 * size], q[size : 2 * size])
-    coefs = [x[2 * size : 3 * size].astype(BF16) for x in (p, q)]
-    coefs = [column(x[:, :size], x[:, size:]) for x in coefs]
-    coefs_t = [flip(x) for x in coefs]
-    tops = [x[3 * size :].astype(BF16) for x in (p, q)]
-    tops = [column(x[:, :size], x[:, size:]) for x in tops]
-    tops_t = [flip(x) for x in tops]
+    a, b = mine[size : 2 * size, :], other[size : 2 * size, :]
+    p, q = jnp.where(low, a, b), jnp.where(low, b, a)
+    last = 5 * size // 2
+    a, b = mine[last:, :], other[last:, :]
+    corner = column(jnp.where(low, a, b), jnp.where(low, b, a))
     square = scaling * scaling
-    corner = square * dot_wide(coefs_t[0], wide_dot(corner, coefs[1]))
-    joint = column(row(p[:size, :size], corner), row(corner.T, q[:size, :size]))
-    both, both_t = column(*tops), row(*tops_t)
-    gram = square * dot_wide(both_t, wide_dot(joint, both))
-    cross = scaling * dot_wide(both_t, column(p[:size, size:], q[:size, size:]))
+    exact = dict(precision=lax.Precision.HIGHEST, preferred_element_type=F32)
+    right = lax.dot_general(corner, q, (((1,), (1,)), ((), ())), **exact)
+    across = (square * square) * jnp.dot(p, right, **exact)
+    gram, cross = across + across.T, 0.0
+    for half in (mine, other):
+        coef = half[2 * size : last, :].astype(BF16)
+        coef = column(coef[:, :size], coef[:, size:])
+        coef_t = flip(coef)
+        gram = gram + square * dot_wide(coef_t, wide_dot(half[:size, :size], coef))
+        cross = cross + scaling * dot_wide(coef_t, half[:size, size:])
     (last,) = ridge_solve([row(gram, cross)])
-    last_t = flip(last)
-    total_t = row(*(wide_dot(dot(last_t, t), c) for t, c in zip(tops_t, coefs_t)))
+    total_t = dot_wide(flip(last), row(p, q))
     result = (square * scaling) * sum(dot(part, pieces[...]) for part in halves(total_t))
     table[:size, :] = result[:, : 2 * size]
     table[size:, :] = result[:, 2 * size :]
@@ -354,8 +352,9 @@
 
     own, to_core, to_chip = restrict(probes, sources, side[None].astype(jnp.int32))
     from_core = swap(to_core, "space", 1)
-    across = [(i, i + 1 if i % 2 else i - 1) for i in range(space)]
-    from_chip = lax.ppermute(to_chip, "space", [(i, j) for i, j in across if 0 <= j < space])
+    across = [(i, (i + 1 if i % 2 else i - 1) % space) for i in range(space)]
+    from_chip = lax.ppermute(to_chip, "space", across)
+    from_chip = jnp.where((place == 0) | (place == space - 1), 0.0, from_chip)
     from_below = jnp.where(side == 0, from_chip, from_core)
     from_above = jnp.where(side == 0, from_core, from_chip)
     leaf = (own + jnp.concatenate([from_below, from_above], axis=1)).astype(BF16)
@@ -372,16 +371,11 @@
     far = far + swap(send_far, "space", 1)
     mask = 2
     while mask < space:
-        near = near + swap(near, "space", mask)
-        far = far + swap(far, "space", mask)
+        near, far = near + swap(near, "space", mask), far + swap(far, "space", mask)
         mask *= 2
-    coefs = local_call(
-        leaf_kernel, "leaf_coefs", jax.ShapeDtypeStruct((2 * ranks, ranks), BF16), near,
-        flops=1 << 32,
-    )
     mine = local_call(
         lambda *refs: pair_kernel(scaling, *refs), "pair",
-        jax.ShapeDtypeStruct((7 * ranks // 2, 2 * ranks), F32), near, far, coefs,
+        jax.ShapeDtypeStruct((7 * ranks // 2, 2 * ranks), F32), near, far,
     )
     other = swap(mine, "space", 1)
 

time: 52.2 us -> 48 us (0.920)
  Pallas kernels: 17.1 us -> 14.5 us
  starting transfers between devices: 17.8 us -> 15.7 us
  waiting for transfers between devices: 15 us -> 16.2 us
  other arithmetic: 1.23 us -> 0.35 us
    ppermute x12, starting transfers between devices: 17.2 us -> 11.2 us  [swap(): lax.ppermute(x, axis, [(i, i ^ mask) for i in range(lax.axis_size(axis))])]
    ppermute x1, starting transfers between devices: 0.66 us -> 4.53 us  [body(): from_chip = lax.ppermute(to_chip, 'space', across)]
    pallas_call x3 -> x2, Pallas kernels: 9.76 us -> 7.92 us  [local_call(): pl.pallas_call(kernel, in_specs=[smem] * len(scalars) + [vmem] * len(args...]
    ppermute x1, waiting for transfers between devices: 0.01 us -> 1.78 us  [body(): from_chip = lax.ppermute(to_chip, 'space', across)]
    convert_element_type x1, other arithmetic: 0.92 us -> 0.02 us  [body(): (own + jnp.concatenate([from_below, from_above], axis=1)).astype(BF16)]
    pallas_call x1, Pallas kernels: 6.43 us -> 5.75 us  [restrict(): pl.pallas_call(restrict_kernel, in_specs=[pl.BlockSpec(memory_space=pltpu...]
  transfers between devices with their start and end apart: 13 -> 13, of which waited for: 9 -> 10; matrix products, arithmetic and copies ran while one was open for 1% -> 1% of each run, Pallas kernels for 0% -> 0%
where the time goes in v3:
time: 48 us; the launch traced here: 47.8 us
  waiting for transfers between devices  16.2 us (34%)
  starting transfers between devices  15.7 us (33%)
  Pallas kernels  14.5 us (30%)
  local copies, waits for them, and re-layouts  0.88 us (2%)
    ppermute x12, waiting for transfers between devices, swap(): lax.ppermute(x, axis, [(i, i ^ mask) for i in range(lax.axis_size(axis))])  14.5 us
    ppermute x12, starting transfers between devices, swap(): lax.ppermute(x, axis, [(i, i ^ mask) for i in range(lax.axis_size(axis))])  11.2 us
    pallas_call x2, Pallas kernels, local_call(): pl.pallas_call(kernel, in_specs=[smem] * len(scalars) + [vmem] * len(args...  7.92 us
    pallas_call x1, Pallas kernels, restrict(): pl.pallas_call(restrict_kernel, in_specs=[pl.BlockSpec(memory_space=pltpu...  5.75 us
    ppermute x1, starting transfers between devices, body(): from_chip = lax.ppermute(to_chip, 'space', across)  4.53 us
    ppermute x1, waiting for transfers between devices, body(): from_chip = lax.ppermute(to_chip, 'space', across)  1.78 us
  transfers between devices with their start and end apart: 13, of which 10 were waited for; matrix products, arithmetic and copies ran while one was open for 1% of the time, Pallas kernels for 0%

profile of v3, /device:TPU:0, one launch (start us, length us, event | category | flops | bytes accessed | tf_op | source)
XLA Modules:
  0.0 47.8 jit_solution(14683589640819562523)
XLA Ops:
  0.0 0.0 copy-start
  0.0 0.0 copy-start.1
  0.0 5.7 %restrict.1 = (f32[128,256]{1,0:T(8,128)S(1)}, f32[128,128]{1,0:T(8,128)S(1)}, f32[128,128]{1,0:T(8,128)S(1)}) custom-call(s32[1]{0:T(128)} %bitcast.side, bf16[32768,128]{1,0:T(8,128)(2,1)} %bitcast.9, bf16[2,256,128]{2,1,0:T(8,128)(2,1)} %bitcast.10, bf16[32,256]{1,0:T(8,128)(2,1)} %constant.74.table_xy, bf16[512,256]{1,0:T(8,128)(2,1)} %constant.79.table_z), custom_call_target="tpu_custom_call" | custom-call | tf_op jit(solution)/shard_map/restrict/pallas_call | solution.py:151
  5.8 4.5 %collective-permute-start = (f32[128,128]{1,0:T(8,128)S(1)}, f32[128,128]{1,0:T(8,128)S(1)}, u32[]{:S(2)}, u32[]{:S(2)}) collective-permute-start(f32[128,128]{1,0:T(8,128)S(1)} %get-tuple-element.16), channel_id=1, source_target_pairs={{0,7},{1,2},{2,1},{3,4},{4,3},{5,6},{6,5},{7,0},{8,15},{9,10},{10,... | collective-permute-start | bytes 196616 | tf_op jit(solution)/shard_map/ppermute | solution.py:356
  10.3 0.0 collective-permute-start.1
  10.3 0.0 copy-done
  10.3 0.1 copy.7
  10.4 0.1 reshape.14.refs_5_
  10.5 0.0 copy-done.1
  10.5 0.1 fusion.1
  10.6 1.8 %collective-permute-done = f32[128,128]{1,0:T(8,128)S(1)} collective-permute-done((f32[128,128]{1,0:T(8,128)S(1)}, f32[128,128]{1,0:T(8,128)S(1)}, u32[]{:S(2)}, u32[]{:S(2)}) %collective-permute-start) | collective-permute-done | bytes 65568 | tf_op jit(solution)/shard_map/ppermute | solution.py:356
  12.3 0.0 collective-permute-done.1
  12.4 3.3 %collective-permute-start.4 = (bf16[128,256]{1,0:T(8,128)(2,1)S(1)}, bf16[128,256]{1,0:T(8,128)(2,1)S(1)}, u32[]{:S(2)}, u32[]{:S(2)}) collective-permute-start(bf16[128,256]{1,0:T(8,128)(2,1)S(1)} %fusion.refs_1_), channel_id=1, source_target_pairs={{0,24},{8,16},{16,8},{24,0},{1,25},{9,17},{17,9},{25,1},{2,26},{10... | collective-permute-start | bytes 196616 | tf_op jit(solution)/shard_map/ppermute | solution.py:341
  15.7 0.5 %collective-permute-start.3 = (bf16[128,256]{1,0:T(8,128)(2,1)S(1)}, bf16[128,256]{1,0:T(8,128)(2,1)S(1)}, u32[]{:S(2)}, u32[]{:S(2)}) collective-permute-start(bf16[128,256]{1,0:T(8,128)(2,1)S(1)} %fusion.refs_1_), channel_id=1, source_target_pairs={{0,16},{8,24},{16,0},{24,8},{1,17},{9,25},{17,1},{25,9},{2,18},{10... | collective-permute-start | bytes 196616 | tf_op jit(solution)/shard_map/ppermute | solution.py:341
  16.2 0.1 collective-permute-start.2
  16.3 0.1 pad_add_fusion.1.refs_0_
  16.4 1.8 %collective-permute-done.4.refs_4_ = bf16[128,256]{1,0:T(8,128)(2,1)S(1)} collective-permute-done((bf16[128,256]{1,0:T(8,128)(2,1)S(1)}, bf16[128,256]{1,0:T(8,128)(2,1)S(1)}, u32[]{:S(2)}, u32[]{:S(2)}) %collective-permute-start.4) | collective-permute-done | bytes 65568 | tf_op jit(solution)/shard_map/ppermute | solution.py:341
  18.2 1.8 %collective-permute-done.3.refs_3_ = bf16[128,256]{1,0:T(8,128)(2,1)S(1)} collective-permute-done((bf16[128,256]{1,0:T(8,128)(2,1)S(1)}, bf16[128,256]{1,0:T(8,128)(2,1)S(1)}, u32[]{:S(2)}, u32[]{:S(2)}) %collective-permute-start.3) | collective-permute-done | bytes 65568 | tf_op jit(solution)/shard_map/ppermute | solution.py:341
  20.0 0.5 %collective-permute-done.2.refs_2_ = bf16[128,256]{1,0:T(8,128)(2,1)S(1)} collective-permute-done((bf16[128,256]{1,0:T(8,128)(2,1)S(1)}, bf16[128,256]{1,0:T(8,128)(2,1)S(1)}, u32[]{:S(2)}, u32[]{:S(2)}) %collective-permute-start.2) | collective-permute-done | bytes 65568 | tf_op jit(solution)/shard_map/ppermute | solution.py:341
  20.5 0.9 %products.1 = (bf16[256,256]{1,0:T(8,128)(2,1)S(1)}, f32[128,128]{1,0:T(8,128)S(1)}, f32[128,128]{1,0:T(8,128)S(1)}, f32[96,128]{1,0:T(8,128)S(1)}, f32[96,128]{1,0:T(8,128)S(1)}) custom-call(s32[5]{0:T(128)S(1)} %pad_add_fusion.1.refs_0_, bf16[128,256]{1,0:T(8,128)(2,1)S(1)} %fusion.refs_1_, bf16[128,256]{1,0:T(8,128)(2,1)S(1)} %collective-permute-done.2.refs_2_, ...), custom_call_target="tpu_custom_call" | custom-call | tf_op jit(solution)/shard_map/products/pallas_call | solution.py:216
  21.4 0.1 collective-permute-start.5
  21.4 0.5 %collective-permute-start.8 = (f32[96,128]{1,0:T(8,128)S(1)}, f32[96,128]{1,0:T(8,128)S(1)}, u32[]{:S(2)}, u32[]{:S(2)}) collective-permute-start(f32[96,128]{1,0:T(8,128)S(1)} %get-tuple-element.21), channel_id=1, source_target_pairs={{0,1},{1,0},{2,3},{3,2},{4,5},{5,4},{6,7},{7,6},{8,9},{9,8},{10,11... | collective-permute-start | bytes 147464 | tf_op jit(solution)/shard_map/ppermute | solution.py:341
  21.9 0.7 %collective-permute-done.5 = f32[128,128]{1,0:T(8,128)S(1)} collective-permute-done((f32[128,128]{1,0:T(8,128)S(1)}, f32[128,128]{1,0:T(8,128)S(1)}, u32[]{:S(2)}, u32[]{:S(2)}) %collective-permute-start.5) | collective-permute-done | bytes 65568 | tf_op jit(solution)/shard_map/ppermute | solution.py:341
  22.7 0.1 collective-permute-start.6
  22.8 0.0 collective-permute-done.8
  22.8 2.0 %collective-permute-start.9 = (f32[96,128]{1,0:T(8,128)S(1)}, f32[96,128]{1,0:T(8,128)S(1)}, u32[]{:S(2)}, u32[]{:S(2)}) collective-permute-start(f32[96,128]{1,0:T(8,128)S(1)} %add.50), channel_id=1, source_target_pairs={{0,2},{1,3},{2,0},{3,1},{4,6},{5,7},{6,4},{7,5},{8,10},{9,11},{10,... | collective-permute-start | bytes 147464 | tf_op jit(solution)/shard_map/ppermute | solution.py:341
  24.9 2.6 %collective-permute-done.6 = f32[128,128]{1,0:T(8,128)S(1)} collective-permute-done((f32[128,128]{1,0:T(8,128)S(1)}, f32[128,128]{1,0:T(8,128)S(1)}, u32[]{:S(2)}, u32[]{:S(2)}) %collective-permute-start.6) | collective-permute-done | bytes 65568 | tf_op jit(solution)/shard_map/ppermute | solution.py:341
  27.5 0.4 collective-permute-start.7
  27.9 0.1 collective-permute-done.9
  28.0 2.5 %collective-permute-start.10 = (f32[96,128]{1,0:T(8,128)S(1)}, f32[96,128]{1,0:T(8,128)S(1)}, u32[]{:S(2)}, u32[]{:S(2)}) collective-permute-start(f32[96,128]{1,0:T(8,128)S(1)} %add.51), channel_id=1, source_target_pairs={{0,4},{1,5},{2,6},{3,7},{4,0},{5,1},{6,2},{7,3},{8,12},{9,13},{10,... | collective-permute-start | bytes 147464 | tf_op jit(solution)/shard_map/ppermute | solution.py:341
  30.5 3.5 %collective-permute-done.10 = f32[96,128]{1,0:T(8,128)S(1)} collective-permute-done((f32[96,128]{1,0:T(8,128)S(1)}, f32[96,128]{1,0:T(8,128)S(1)}, u32[]{:S(2)}, u32[]{:S(2)}) %collective-permute-start.10) | collective-permute-done | bytes 49184 | tf_op jit(solution)/shard_map/ppermute | solution.py:341
  34.0 0.0 collective-permute-done.7
  34.0 4.2 %pair.1.refs_1_ = f32[224,128]{1,0:T(8,128)S(1)} custom-call(f32[128,128]{1,0:T(8,128)S(1)} %add.49.refs_0_, f32[96,128]{1,0:T(8,128)S(1)} %add.52.refs_1_), custom_call_target="tpu_custom_call" | custom-call | flops 16777216 | bytes 131072 | tf_op jit(solution)/shard_map/pair/pallas_call | solution.py:328
  38.2 0.0 collective-permute-start.11
  38.2 0.1 pad_add_fusion.refs_0_
  38.3 1.3 %collective-permute-done.11.refs_2_ = f32[224,128]{1,0:T(8,128)S(1)} collective-permute-done((f32[224,128]{1,0:T(8,128)S(1)}, f32[224,128]{1,0:T(8,128)S(1)}, u32[]{:S(2)}, u32[]{:S(2)}) %collective-permute-start.11) | collective-permute-done | bytes 114720 | tf_op jit(solution)/shard_map/ppermute | solution.py:341
  39.6 3.7 %root.1 = (f32[16,256]{1,0:T(8,128)S(1)}, f32[16,256]{1,0:T(8,128)S(1)}) custom-call(s32[3]{0:T(128)S(1)} %pad_add_fusion.refs_0_, f32[224,128]{1,0:T(8,128)S(1)} %pair.1.refs_1_, f32[224,128]{1,0:T(8,128)S(1)} %collective-permute-done.11.refs_2_, bf16[256,256]{1,0:T(8,128)(2,1)S(1)} %get-tuple-element.22.refs_3_), custom_call_target="tpu_custom_call" | custom-call | flops 16777216 | bytes 131072 | tf_op jit(solution)/shard_map/root/pallas_call | solution.py:328
  43.3 1.6 %collective-permute-start.12 = (f32[16,256]{1,0:T(8,128)S(1)}, f32[16,256]{1,0:T(8,128)S(1)}, u32[]{:S(2)}, u32[]{:S(2)}) collective-permute-start(f32[16,256]{1,0:T(8,128)S(1)} %get-tuple-element.24), channel_id=1, source_target_pairs={{0,16},{8,24},{16,0},{24,8},{1,17},{9,25},{17,1},{25,9},{2,18},{10... | collective-permute-start | bytes 49160 | tf_op jit(solution)/shard_map/ppermute | solution.py:341
  44.9 2.2 %collective-permute-done.12 = f32[16,256]{1,0:T(8,128)S(1)} collective-permute-done((f32[16,256]{1,0:T(8,128)S(1)}, f32[16,256]{1,0:T(8,128)S(1)}, u32[]{:S(2)}, u32[]{:S(2)}) %collective-permute-start.12) | collective-permute-done | bytes 16416 | tf_op jit(solution)/shard_map/ppermute | solution.py:341
  47.1 0.1 reshape.15
  47.2 0.6 %copy.10 = bf16[16,4,64]{2,0,1:T(8,128)(2,1)} copy(bf16[16,4,64]{2,1,0:T(4,128)(2,1)S(1)} %reshape.15) | data formatting | bytes 16384 | tf_op jit(solution)/shard_map/reshape | solution.py:391
  (9 shorter events, 0.1 us)
Async XLA Ops:
  0.0 10.3 %copy-start = (bf16[4,64,64]{2,1,0:T(8,128)(2,1)S(1)}, bf16[4,64,64]{2,1,0:T(8,128)(2,1)}, u32[]{:S(2)}) copy-start(bf16[4,64,64]{2,1,0:T(8,128)(2,1)} %param.8) | copy-start | bytes 98308
  0.0 10.5 %copy-start.1 = (s32[8]{0:T(128)S(1)}, s32[8]{0:T(128)}, u32[]{:S(2)}) copy-start(s32[8]{0:T(128)} %param.9) | copy-start | bytes 100
  5.8 6.6 %collective-permute-start = (f32[128,128]{1,0:T(8,128)S(1)}, f32[128,128]{1,0:T(8,128)S(1)}, u32[]{:S(2)}, u32[]{:S(2)}) collective-permute-start(f32[128,128]{1,0:T(8,128)S(1)} %get-tuple-element.16), channel_id=1, source_target_pairs={{0,7},{1,2},{2,1},{3,4},{4,3},{5,6},{6,5},{7,0},{8,15},{9,10},{10,... | collective-permute-start | bytes 196616 | tf_op jit(solution)/shard_map/ppermute | solution.py:356
  10.3 2.1 %collective-permute-start.1 = (f32[128,128]{1,0:T(8,128)S(1)}, f32[128,128]{1,0:T(8,128)S(1)}, u32[]{:S(2)}, u32[]{:S(2)}) collective-permute-start(f32[128,128]{1,0:T(8,128)S(1)} %get-tuple-element.17), channel_id=1, source_target_pairs={{0,1},{1,0},{2,3},{3,2},{4,5},{5,4},{6,7},{7,6},{8,9},{9,8},{10,11... | collective-permute-start | bytes 196616 | tf_op jit(solution)/shard_map/ppermute | solution.py:341
  12.4 5.8 %collective-permute-start.4 = (bf16[128,256]{1,0:T(8,128)(2,1)S(1)}, bf16[128,256]{1,0:T(8,128)(2,1)S(1)}, u32[]{:S(2)}, u32[]{:S(2)}) collective-permute-start(bf16[128,256]{1,0:T(8,128)(2,1)S(1)} %fusion.refs_1_), channel_id=1, source_target_pairs={{0,24},{8,16},{16,8},{24,0},{1,25},{9,17},{17,9},{25,1},{2,26},{10... | collective-permute-start | bytes 196616 | tf_op jit(solution)/shard_map/ppermute | solution.py:341
  15.7 4.3 %collective-permute-start.3 = (bf16[128,256]{1,0:T(8,128)(2,1)S(1)}, bf16[128,256]{1,0:T(8,128)(2,1)S(1)}, u32[]{:S(2)}, u32[]{:S(2)}) collective-permute-start(bf16[128,256]{1,0:T(8,128)(2,1)S(1)} %fusion.refs_1_), channel_id=1, source_target_pairs={{0,16},{8,24},{16,0},{24,8},{1,17},{9,25},{17,1},{25,9},{2,18},{10... | collective-permute-start | bytes 196616 | tf_op jit(solution)/shard_map/ppermute | solution.py:341
  16.2 4.3 %collective-permute-start.2 = (bf16[128,256]{1,0:T(8,128)(2,1)S(1)}, bf16[128,256]{1,0:T(8,128)(2,1)S(1)}, u32[]{:S(2)}, u32[]{:S(2)}) collective-permute-start(bf16[128,256]{1,0:T(8,128)(2,1)S(1)} %fusion.refs_1_), channel_id=1, source_target_pairs={{0,8},{8,0},{16,24},{24,16},{1,9},{9,1},{17,25},{25,17},{2,10},{10... | collective-permute-start | bytes 196616 | tf_op jit(solution)/shard_map/ppermute | solution.py:341
  21.4 1.3 %collective-permute-start.5 = (f32[128,128]{1,0:T(8,128)S(1)}, f32[128,128]{1,0:T(8,128)S(1)}, u32[]{:S(2)}, u32[]{:S(2)}) collective-permute-start(f32[128,128]{1,0:T(8,128)S(1)} %get-tuple-element.19), channel_id=1, source_target_pairs={{0,1},{1,0},{2,3},{3,2},{4,5},{5,4},{6,7},{7,6},{8,9},{9,8},{10,11... | collective-permute-start | bytes 196616 | tf_op jit(solution)/shard_map/ppermute | solution.py:341
  21.4 1.4 %collective-permute-start.8 = (f32[96,128]{1,0:T(8,128)S(1)}, f32[96,128]{1,0:T(8,128)S(1)}, u32[]{:S(2)}, u32[]{:S(2)}) collective-permute-start(f32[96,128]{1,0:T(8,128)S(1)} %get-tuple-element.21), channel_id=1, source_target_pairs={{0,1},{1,0},{2,3},{3,2},{4,5},{5,4},{6,7},{7,6},{8,9},{9,8},{10,11... | collective-permute-start | bytes 147464 | tf_op jit(solution)/shard_map/ppermute | solution.py:341
  22.7 4.7 %collective-permute-start.6 = (f32[128,128]{1,0:T(8,128)S(1)}, f32[128,128]{1,0:T(8,128)S(1)}, u32[]{:S(2)}, u32[]{:S(2)}) collective-permute-start(f32[128,128]{1,0:T(8,128)S(1)} %add.47), channel_id=1, source_target_pairs={{0,2},{1,3},{2,0},{3,1},{4,6},{5,7},{6,4},{7,5},{8,10},{9,11},{10,... | collective-permute-start | bytes 196616 | tf_op jit(solution)/shard_map/ppermute | solution.py:341
  22.8 5.1 %collective-permute-start.9 = (f32[96,128]{1,0:T(8,128)S(1)}, f32[96,128]{1,0:T(8,128)S(1)}, u32[]{:S(2)}, u32[]{:S(2)}) collective-permute-start(f32[96,128]{1,0:T(8,128)S(1)} %add.50), channel_id=1, source_target_pairs={{0,2},{1,3},{2,0},{3,1},{4,6},{5,7},{6,4},{7,5},{8,10},{9,11},{10,... | collective-permute-start | bytes 147464 | tf_op jit(solution)/shard_map/ppermute | solution.py:341
  27.5 6.5 %collective-permute-start.7 = (f32[128,128]{1,0:T(8,128)S(1)}, f32[128,128]{1,0:T(8,128)S(1)}, u32[]{:S(2)}, u32[]{:S(2)}) collective-permute-start(f32[128,128]{1,0:T(8,128)S(1)} %add.48), channel_id=1, source_target_pairs={{0,4},{1,5},{2,6},{3,7},{4,0},{5,1},{6,2},{7,3},{8,12},{9,13},{10,... | collective-permute-start | bytes 196616 | tf_op jit(solution)/shard_map/ppermute | solution.py:341
  28.0 6.0 %collective-permute-start.10 = (f32[96,128]{1,0:T(8,128)S(1)}, f32[96,128]{1,0:T(8,128)S(1)}, u32[]{:S(2)}, u32[]{:S(2)}) collective-permute-start(f32[96,128]{1,0:T(8,128)S(1)} %add.51), channel_id=1, source_target_pairs={{0,4},{1,5},{2,6},{3,7},{4,0},{5,1},{6,2},{7,3},{8,12},{9,13},{10,... | collective-permute-start | bytes 147464 | tf_op jit(solution)/shard_map/ppermute | solution.py:341
  38.2 1.4 %collective-permute-start.11 = (f32[224,128]{1,0:T(8,128)S(1)}, f32[224,128]{1,0:T(8,128)S(1)}, u32[]{:S(2)}, u32[]{:S(2)}) collective-permute-start(f32[224,128]{1,0:T(8,128)S(1)} %pair.1.refs_1_), channel_id=1, source_target_pairs={{0,1},{1,0},{2,3},{3,2},{4,5},{5,4},{6,7},{7,6},{8,9},{9,8},{10,11... | collective-permute-start | bytes 344072 | tf_op jit(solution)/shard_map/ppermute | solution.py:341
  43.3 3.8 %collective-permute-start.12 = (f32[16,256]{1,0:T(8,128)S(1)}, f32[16,256]{1,0:T(8,128)S(1)}, u32[]{:S(2)}, u32[]{:S(2)}) collective-permute-start(f32[16,256]{1,0:T(8,128)S(1)} %get-tuple-element.24), channel_id=1, source_target_pairs={{0,16},{8,24},{16,0},{24,8},{1,17},{9,25},{17,1},{25,9},{2,18},{10... | collective-permute-start | bytes 49160 | tf_op jit(solution)/shard_map/ppermute | solution.py:341

commit v4 on v3

--- a/solution.py
+++ b/solution.py
@@ -81,7 +81,8 @@
     ]
     small[0].start()
     small[1].start()
-    for i in range(chunks):
+    ahead = chunks - 1
+    for i in range(ahead):
         arrival(i).start()
     small[2].start()
     small[0].wait()
@@ -90,6 +91,8 @@
     for i in range(chunks):
         g = i * groups // chunks
         arrival(i).wait()
+        if i + ahead < chunks:
+            arrival(i + ahead).start()
         for pair in range(ranks // 2):
             first, second = (i * ranks + 2 * pair + k for k in range(2))
             high, low = ([], []), ([], [])
@@ -114,11 +117,8 @@
     lanes = weights_z.shape[1] // 2
     layers = []
     for j in range(edges // per):
-        total = 0.0
-        for r in range(per):
-            weights = weights_z[r * fine_z : (r + 1) * fine_z]
-            for part in halves(rows[pl.ds(j * per + r, all_rows, stride=edges), :]):
-                total = total + dot(part, weights)
+        parts = [halves(rows[pl.ds(j * per + r, all_rows, stride=edges), :]) for r in range(per)]
+        total = sum(dot(jnp.concatenate(x, axis=1), weights_z[...]) for x in zip(*parts))
         layers.append(total[:, :lanes] + total[:, lanes:])
     own[...] = jnp.concatenate(layers[1:-1], axis=1)
     odd = side[0] == 1
@@ -270,15 +270,24 @@
     return x.astype(F32).T.astype(BF16)
 
 
-def pair_kernel(scaling, near, far, out):
+def leaf_kernel(near, got, whole, coefs):
+    size = near.shape[1] // 2
+    whole[...] = near[...] + got[...]
+    a, b = ridge_solve([whole[:size], whole[size:]])
+    coefs[:size, :] = a
+    coefs[size:, :] = b
+
+
+def pair_kernel(scaling, near, coefs, far, far_got, out):
     size = near.shape[1] // 2
     half = size // 2
     row = lambda *xs: jnp.concatenate(xs, axis=1)
     column = lambda *xs: jnp.concatenate(xs, axis=0)
+    far = far[...] + far_got[...]
     corner = column(far[:half, :size], far[:half, size:])
     joint = column(row(near[:size, :size], corner), row(corner.T, near[size:, :size]))
     cross = column(near[:size, size:], near[size:, size:])
-    both = column(*ridge_solve([near[:size], near[size:]]))
+    both = coefs[...]
     both_t = flip(both)
     gram = scaling * scaling * dot_wide(both_t, wide_dot(joint, both))
     system = row(gram, scaling * dot_wide(both_t, cross))
@@ -370,12 +379,21 @@
     near = near + swap(send, "space", 1)
     far = far + swap(send_far, "space", 1)
     mask = 2
-    while mask < space:
+    while 2 * mask < space:
         near, far = near + swap(near, "space", mask), far + swap(far, "space", mask)
         mask *= 2
+    near_got, far_got = swap(near, "space", mask), swap(far, "space", mask)
+    near, coefs = local_call(
+        leaf_kernel, "leaf",
+        [
+            jax.ShapeDtypeStruct(near.shape, F32),
+            jax.ShapeDtypeStruct((2 * ranks, ranks), BF16),
+        ],
+        near, near_got, flops=1 << 24,
+    )
     mine = local_call(
         lambda *refs: pair_kernel(scaling, *refs), "pair",
-        jax.ShapeDtypeStruct((7 * ranks // 2, 2 * ranks), F32), near, far,
+        jax.ShapeDtypeStruct((7 * ranks // 2, 2 * ranks), F32), near, coefs, far, far_got,
     )
     other = swap(mine, "space", 1)
 

time: 48 us -> 47 us (0.979)
    pallas_call x1, Pallas kernels: 5.75 us -> 5.24 us  [restrict(): pl.pallas_call(restrict_kernel, in_specs=[pl.BlockSpec(memory_space=pltpu...]
    pallas_call x2 -> x3, Pallas kernels: 7.92 us -> 8.01 us  [local_call(): pl.pallas_call(kernel, in_specs=[smem] * len(scalars) + [vmem] * len(args...]
  transfers between devices with their start and end apart: 13 -> 13, of which waited for: 10 -> 10; matrix products, arithmetic and copies ran while one was open for 1% -> 1% of each run, Pallas kernels for 0% -> 4%
where the time goes in v4:
time: 47 us; the launch traced here: 46.9 us
  waiting for transfers between devices  15.8 us (34%)
  starting transfers between devices  15.7 us (33%)
  Pallas kernels  14.1 us (30%)
  local copies, waits for them, and re-layouts  0.88 us (2%)
    ppermute x12, waiting for transfers between devices, swap(): lax.ppermute(x, axis, [(i, i ^ mask) for i in range(lax.axis_size(axis))])  14 us
    ppermute x12, starting transfers between devices, swap(): lax.ppermute(x, axis, [(i, i ^ mask) for i in range(lax.axis_size(axis))])  11.1 us
    pallas_call x3, Pallas kernels, local_call(): pl.pallas_call(kernel, in_specs=[smem] * len(scalars) + [vmem] * len(args...  8.01 us
    pallas_call x1, Pallas kernels, restrict(): pl.pallas_call(restrict_kernel, in_specs=[pl.BlockSpec(memory_space=pltpu...  5.24 us
    ppermute x1, starting transfers between devices, body(): from_chip = lax.ppermute(to_chip, 'space', across)  4.55 us
    ppermute x1, waiting for transfers between devices, body(): from_chip = lax.ppermute(to_chip, 'space', across)  1.78 us
  transfers between devices with their start and end apart: 13, of which 10 were waited for; matrix products, arithmetic and copies ran while one was open for 1% of the time, Pallas kernels for 4%

profile of v4, /device:TPU:0, one launch (start us, length us, event | category | flops | bytes accessed | tf_op | source)
XLA Modules:
  0.0 46.9 jit_solution(2893699891359948030)
XLA Ops:
  0.0 0.0 copy-start
  0.0 0.0 copy-start.1
  0.0 5.2 %restrict.1 = (f32[128,256]{1,0:T(8,128)S(1)}, f32[128,128]{1,0:T(8,128)S(1)}, f32[128,128]{1,0:T(8,128)S(1)}) custom-call(s32[1]{0:T(128)} %bitcast.side, bf16[32768,128]{1,0:T(8,128)(2,1)} %bitcast.9, bf16[2,256,128]{2,1,0:T(8,128)(2,1)} %bitcast.10, bf16[32,256]{1,0:T(8,128)(2,1)} %constant.74.table_xy, bf16[512,256]{1,0:T(8,128)(2,1)} %constant.79.table_z), custom_call_target="tpu_custom_call" | custom-call | tf_op jit(solution)/shard_map/restrict/pallas_call | solution.py:151
  5.3 4.6 %collective-permute-start = (f32[128,128]{1,0:T(8,128)S(1)}, f32[128,128]{1,0:T(8,128)S(1)}, u32[]{:S(2)}, u32[]{:S(2)}) collective-permute-start(f32[128,128]{1,0:T(8,128)S(1)} %get-tuple-element.18), channel_id=1, source_target_pairs={{0,7},{1,2},{2,1},{3,4},{4,3},{5,6},{6,5},{7,0},{8,15},{9,10},{10,... | collective-permute-start | bytes 196616 | tf_op jit(solution)/shard_map/ppermute | solution.py:365
  9.8 0.0 collective-permute-start.1
  9.8 0.0 copy-done
  9.8 0.1 copy.7
  9.9 0.1 reshape.14.refs_5_
  10.0 0.0 copy-done.1
  10.0 0.1 fusion.1
  10.1 1.8 %collective-permute-done = f32[128,128]{1,0:T(8,128)S(1)} collective-permute-done((f32[128,128]{1,0:T(8,128)S(1)}, f32[128,128]{1,0:T(8,128)S(1)}, u32[]{:S(2)}, u32[]{:S(2)}) %collective-permute-start) | collective-permute-done | bytes 65568 | tf_op jit(solution)/shard_map/ppermute | solution.py:365
  11.9 0.0 collective-permute-done.1
  11.9 3.3 %collective-permute-start.4 = (bf16[128,256]{1,0:T(8,128)(2,1)S(1)}, bf16[128,256]{1,0:T(8,128)(2,1)S(1)}, u32[]{:S(2)}, u32[]{:S(2)}) collective-permute-start(bf16[128,256]{1,0:T(8,128)(2,1)S(1)} %fusion.refs_1_), channel_id=1, source_target_pairs={{0,24},{8,16},{16,8},{24,0},{1,25},{9,17},{17,9},{25,1},{2,26},{10... | collective-permute-start | bytes 196616 | tf_op jit(solution)/shard_map/ppermute | solution.py:350
  15.2 0.5 %collective-permute-start.3 = (bf16[128,256]{1,0:T(8,128)(2,1)S(1)}, bf16[128,256]{1,0:T(8,128)(2,1)S(1)}, u32[]{:S(2)}, u32[]{:S(2)}) collective-permute-start(bf16[128,256]{1,0:T(8,128)(2,1)S(1)} %fusion.refs_1_), channel_id=1, source_target_pairs={{0,16},{8,24},{16,0},{24,8},{1,17},{9,25},{17,1},{25,9},{2,18},{10... | collective-permute-start | bytes 196616 | tf_op jit(solution)/shard_map/ppermute | solution.py:350
  15.8 0.1 collective-permute-start.2
  15.9 0.1 pad_add_fusion.1.refs_0_
  16.0 1.8 %collective-permute-done.4.refs_4_ = bf16[128,256]{1,0:T(8,128)(2,1)S(1)} collective-permute-done((bf16[128,256]{1,0:T(8,128)(2,1)S(1)}, bf16[128,256]{1,0:T(8,128)(2,1)S(1)}, u32[]{:S(2)}, u32[]{:S(2)}) %collective-permute-start.4) | collective-permute-done | bytes 65568 | tf_op jit(solution)/shard_map/ppermute | solution.py:350
  17.8 1.7 %collective-permute-done.3.refs_3_ = bf16[128,256]{1,0:T(8,128)(2,1)S(1)} collective-permute-done((bf16[128,256]{1,0:T(8,128)(2,1)S(1)}, bf16[128,256]{1,0:T(8,128)(2,1)S(1)}, u32[]{:S(2)}, u32[]{:S(2)}) %collective-permute-start.3) | collective-permute-done | bytes 65568 | tf_op jit(solution)/shard_map/ppermute | solution.py:350
  19.5 0.5 %collective-permute-done.2.refs_2_ = bf16[128,256]{1,0:T(8,128)(2,1)S(1)} collective-permute-done((bf16[128,256]{1,0:T(8,128)(2,1)S(1)}, bf16[128,256]{1,0:T(8,128)(2,1)S(1)}, u32[]{:S(2)}, u32[]{:S(2)}) %collective-permute-start.2) | collective-permute-done | bytes 65568 | tf_op jit(solution)/shard_map/ppermute | solution.py:350
  20.0 0.9 %products.1 = (bf16[256,256]{1,0:T(8,128)(2,1)S(1)}, f32[128,128]{1,0:T(8,128)S(1)}, f32[128,128]{1,0:T(8,128)S(1)}, f32[96,128]{1,0:T(8,128)S(1)}, f32[96,128]{1,0:T(8,128)S(1)}) custom-call(s32[5]{0:T(128)S(1)} %pad_add_fusion.1.refs_0_, bf16[128,256]{1,0:T(8,128)(2,1)S(1)} %fusion.refs_1_, bf16[128,256]{1,0:T(8,128)(2,1)S(1)} %collective-permute-done.2.refs_2_, ...), custom_call_target="tpu_custom_call" | custom-call | tf_op jit(solution)/shard_map/products/pallas_call | solution.py:216
  20.9 0.1 collective-permute-start.5
  21.0 0.5 %collective-permute-start.8 = (f32[96,128]{1,0:T(8,128)S(1)}, f32[96,128]{1,0:T(8,128)S(1)}, u32[]{:S(2)}, u32[]{:S(2)}) collective-permute-start(f32[96,128]{1,0:T(8,128)S(1)} %get-tuple-element.25), channel_id=1, source_target_pairs={{0,1},{1,0},{2,3},{3,2},{4,5},{5,4},{6,7},{7,6},{8,9},{9,8},{10,11... | collective-permute-start | bytes 147464 | tf_op jit(solution)/shard_map/ppermute | solution.py:350
  21.5 0.7 %collective-permute-done.5 = f32[128,128]{1,0:T(8,128)S(1)} collective-permute-done((f32[128,128]{1,0:T(8,128)S(1)}, f32[128,128]{1,0:T(8,128)S(1)}, u32[]{:S(2)}, u32[]{:S(2)}) %collective-permute-start.5) | collective-permute-done | bytes 65568 | tf_op jit(solution)/shard_map/ppermute | solution.py:350
  22.2 0.1 collective-permute-start.6
  22.3 0.0 collective-permute-done.8
  22.4 2.0 %collective-permute-start.9 = (f32[96,128]{1,0:T(8,128)S(1)}, f32[96,128]{1,0:T(8,128)S(1)}, u32[]{:S(2)}, u32[]{:S(2)}) collective-permute-start(f32[96,128]{1,0:T(8,128)S(1)} %add.43), channel_id=1, source_target_pairs={{0,2},{1,3},{2,0},{3,1},{4,6},{5,7},{6,4},{7,5},{8,10},{9,11},{10,... | collective-permute-start | bytes 147464 | tf_op jit(solution)/shard_map/ppermute | solution.py:350
  24.4 2.6 %collective-permute-done.6 = f32[128,128]{1,0:T(8,128)S(1)} collective-permute-done((f32[128,128]{1,0:T(8,128)S(1)}, f32[128,128]{1,0:T(8,128)S(1)}, u32[]{:S(2)}, u32[]{:S(2)}) %collective-permute-start.6) | collective-permute-done | bytes 65568 | tf_op jit(solution)/shard_map/ppermute | solution.py:350
  27.0 0.3 collective-permute-start.7
  27.3 0.2 collective-permute-done.9
  27.5 2.5 %collective-permute-start.10 = (f32[96,128]{1,0:T(8,128)S(1)}, f32[96,128]{1,0:T(8,128)S(1)}, u32[]{:S(2)}, u32[]{:S(2)}) collective-permute-start(f32[96,128]{1,0:T(8,128)S(1)} %add.44.refs_2_), channel_id=1, source_target_pairs={{0,4},{1,5},{2,6},{3,7},{4,0},{5,1},{6,2},{7,3},{8,12},{9,13},{10,... | collective-permute-start | bytes 147464 | tf_op jit(solution)/shard_map/ppermute | solution.py:350
  30.1 2.9 %collective-permute-done.7.got = f32[128,128]{1,0:T(8,128)S(1)} collective-permute-done((f32[128,128]{1,0:T(8,128)S(1)}, f32[128,128]{1,0:T(8,128)S(1)}, u32[]{:S(2)}, u32[]{:S(2)}) %collective-permute-start.7) | collective-permute-done | bytes 65568 | tf_op jit(solution)/shard_map/ppermute | solution.py:350
  33.0 2.1 %leaf.1 = (f32[128,128]{1,0:T(8,128)S(1)}, bf16[128,64]{1,0:T(8,128)(2,1)S(1)}) custom-call(f32[128,128]{1,0:T(8,128)S(1)} %add.42.near, f32[128,128]{1,0:T(8,128)S(1)} %collective-permute-done.7.got), custom_call_target="tpu_custom_call" | custom-call | flops 16777216 | bytes 131072 | tf_op jit(solution)/shard_map/leaf/pallas_call | solution.py:337
  35.1 0.0 collective-permute-done.10.refs_3_
  35.1 2.2 %pair.1.refs_1_ = f32[224,128]{1,0:T(8,128)S(1)} custom-call(f32[128,128]{1,0:T(8,128)S(1)} %get-tuple-element.22.refs_0_, bf16[128,64]{1,0:T(8,128)(2,1)S(1)} %get-tuple-element.23.refs_1_, f32[96,128]{1,0:T(8,128)S(1)} %add.44.refs_2_, f32[96,128]{1,0:T(8,128)S(1)} %collective-permute-done.10.refs_3_), custom_call_target="tpu_custom_call" | custom-call | flops 16777216 | bytes 131072 | tf_op jit(solution)/shard_map/pair/pallas_call | solution.py:337
  37.3 0.0 collective-permute-start.11
  37.3 0.1 pad_add_fusion.refs_0_
  37.4 1.3 %collective-permute-done.11.refs_2_ = f32[224,128]{1,0:T(8,128)S(1)} collective-permute-done((f32[224,128]{1,0:T(8,128)S(1)}, f32[224,128]{1,0:T(8,128)S(1)}, u32[]{:S(2)}, u32[]{:S(2)}) %collective-permute-start.11) | collective-permute-done | bytes 114720 | tf_op jit(solution)/shard_map/ppermute | solution.py:350
  38.6 3.7 %root.1 = (f32[16,256]{1,0:T(8,128)S(1)}, f32[16,256]{1,0:T(8,128)S(1)}) custom-call(s32[3]{0:T(128)S(1)} %pad_add_fusion.refs_0_, f32[224,128]{1,0:T(8,128)S(1)} %pair.1.refs_1_, f32[224,128]{1,0:T(8,128)S(1)} %collective-permute-done.11.refs_2_, bf16[256,256]{1,0:T(8,128)(2,1)S(1)} %get-tuple-element.26.refs_3_), custom_call_target="tpu_custom_call" | custom-call | flops 16777216 | bytes 131072 | tf_op jit(solution)/shard_map/root/pallas_call | solution.py:337
  42.4 1.6 %collective-permute-start.12 = (f32[16,256]{1,0:T(8,128)S(1)}, f32[16,256]{1,0:T(8,128)S(1)}, u32[]{:S(2)}, u32[]{:S(2)}) collective-permute-start(f32[16,256]{1,0:T(8,128)S(1)} %get-tuple-element.28), channel_id=1, source_target_pairs={{0,16},{8,24},{16,0},{24,8},{1,17},{9,25},{17,1},{25,9},{2,18},{10... | collective-permute-start | bytes 49160 | tf_op jit(solution)/shard_map/ppermute | solution.py:350
  44.0 2.2 %collective-permute-done.12 = f32[16,256]{1,0:T(8,128)S(1)} collective-permute-done((f32[16,256]{1,0:T(8,128)S(1)}, f32[16,256]{1,0:T(8,128)S(1)}, u32[]{:S(2)}, u32[]{:S(2)}) %collective-permute-start.12) | collective-permute-done | bytes 16416 | tf_op jit(solution)/shard_map/ppermute | solution.py:350
  46.2 0.1 reshape.15
  46.3 0.6 %copy.10 = bf16[16,4,64]{2,0,1:T(8,128)(2,1)} copy(bf16[16,4,64]{2,1,0:T(4,128)(2,1)S(1)} %reshape.15) | data formatting | bytes 16384 | tf_op jit(solution)/shard_map/reshape | solution.py:409
  (7 shorter events, 0.1 us)
Async XLA Ops:
  0.0 9.8 %copy-start = (bf16[4,64,64]{2,1,0:T(8,128)(2,1)S(1)}, bf16[4,64,64]{2,1,0:T(8,128)(2,1)}, u32[]{:S(2)}) copy-start(bf16[4,64,64]{2,1,0:T(8,128)(2,1)} %param.8) | copy-start | bytes 98308
  0.0 10.0 %copy-start.1 = (s32[8]{0:T(128)S(1)}, s32[8]{0:T(128)}, u32[]{:S(2)}) copy-start(s32[8]{0:T(128)} %param.9) | copy-start | bytes 100
  5.3 6.6 %collective-permute-start = (f32[128,128]{1,0:T(8,128)S(1)}, f32[128,128]{1,0:T(8,128)S(1)}, u32[]{:S(2)}, u32[]{:S(2)}) collective-permute-start(f32[128,128]{1,0:T(8,128)S(1)} %get-tuple-element.18), channel_id=1, source_target_pairs={{0,7},{1,2},{2,1},{3,4},{4,3},{5,6},{6,5},{7,0},{8,15},{9,10},{10,... | collective-permute-start | bytes 196616 | tf_op jit(solution)/shard_map/ppermute | solution.py:365
  9.8 2.1 %collective-permute-start.1 = (f32[128,128]{1,0:T(8,128)S(1)}, f32[128,128]{1,0:T(8,128)S(1)}, u32[]{:S(2)}, u32[]{:S(2)}) collective-permute-start(f32[128,128]{1,0:T(8,128)S(1)} %get-tuple-element.19), channel_id=1, source_target_pairs={{0,1},{1,0},{2,3},{3,2},{4,5},{5,4},{6,7},{7,6},{8,9},{9,8},{10,11... | collective-permute-start | bytes 196616 | tf_op jit(solution)/shard_map/ppermute | solution.py:350
  11.9 5.9 %collective-permute-start.4 = (bf16[128,256]{1,0:T(8,128)(2,1)S(1)}, bf16[128,256]{1,0:T(8,128)(2,1)S(1)}, u32[]{:S(2)}, u32[]{:S(2)}) collective-permute-start(bf16[128,256]{1,0:T(8,128)(2,1)S(1)} %fusion.refs_1_), channel_id=1, source_target_pairs={{0,24},{8,16},{16,8},{24,0},{1,25},{9,17},{17,9},{25,1},{2,26},{10... | collective-permute-start | bytes 196616 | tf_op jit(solution)/shard_map/ppermute | solution.py:350
  15.2 4.3 %collective-permute-start.3 = (bf16[128,256]{1,0:T(8,128)(2,1)S(1)}, bf16[128,256]{1,0:T(8,128)(2,1)S(1)}, u32[]{:S(2)}, u32[]{:S(2)}) collective-permute-start(bf16[128,256]{1,0:T(8,128)(2,1)S(1)} %fusion.refs_1_), channel_id=1, source_target_pairs={{0,16},{8,24},{16,0},{24,8},{1,17},{9,25},{17,1},{25,9},{2,18},{10... | collective-permute-start | bytes 196616 | tf_op jit(solution)/shard_map/ppermute | solution.py:350
  15.8 4.3 %collective-permute-start.2 = (bf16[128,256]{1,0:T(8,128)(2,1)S(1)}, bf16[128,256]{1,0:T(8,128)(2,1)S(1)}, u32[]{:S(2)}, u32[]{:S(2)}) collective-permute-start(bf16[128,256]{1,0:T(8,128)(2,1)S(1)} %fusion.refs_1_), channel_id=1, source_target_pairs={{0,8},{8,0},{16,24},{24,16},{1,9},{9,1},{17,25},{25,17},{2,10},{10... | collective-permute-start | bytes 196616 | tf_op jit(solution)/shard_map/ppermute | solution.py:350
  20.9 1.3 %collective-permute-start.5 = (f32[128,128]{1,0:T(8,128)S(1)}, f32[128,128]{1,0:T(8,128)S(1)}, u32[]{:S(2)}, u32[]{:S(2)}) collective-permute-start(f32[128,128]{1,0:T(8,128)S(1)} %get-tuple-element.21), channel_id=1, source_target_pairs={{0,1},{1,0},{2,3},{3,2},{4,5},{5,4},{6,7},{7,6},{8,9},{9,8},{10,11... | collective-permute-start | bytes 196616 | tf_op jit(solution)/shard_map/ppermute | solution.py:350
  21.0 1.4 %collective-permute-start.8 = (f32[96,128]{1,0:T(8,128)S(1)}, f32[96,128]{1,0:T(8,128)S(1)}, u32[]{:S(2)}, u32[]{:S(2)}) collective-permute-start(f32[96,128]{1,0:T(8,128)S(1)} %get-tuple-element.25), channel_id=1, source_target_pairs={{0,1},{1,0},{2,3},{3,2},{4,5},{5,4},{6,7},{7,6},{8,9},{9,8},{10,11... | collective-permute-start | bytes 147464 | tf_op jit(solution)/shard_map/ppermute | solution.py:350
  22.2 4.7 %collective-permute-start.6 = (f32[128,128]{1,0:T(8,128)S(1)}, f32[128,128]{1,0:T(8,128)S(1)}, u32[]{:S(2)}, u32[]{:S(2)}) collective-permute-start(f32[128,128]{1,0:T(8,128)S(1)} %add.41), channel_id=1, source_target_pairs={{0,2},{1,3},{2,0},{3,1},{4,6},{5,7},{6,4},{7,5},{8,10},{9,11},{10,... | collective-permute-start | bytes 196616 | tf_op jit(solution)/shard_map/ppermute | solution.py:350
  22.4 5.1 %collective-permute-start.9 = (f32[96,128]{1,0:T(8,128)S(1)}, f32[96,128]{1,0:T(8,128)S(1)}, u32[]{:S(2)}, u32[]{:S(2)}) collective-permute-start(f32[96,128]{1,0:T(8,128)S(1)} %add.43), channel_id=1, source_target_pairs={{0,2},{1,3},{2,0},{3,1},{4,6},{5,7},{6,4},{7,5},{8,10},{9,11},{10,... | collective-permute-start | bytes 147464 | tf_op jit(solution)/shard_map/ppermute | solution.py:350
  27.0 6.0 %collective-permute-start.7 = (f32[128,128]{1,0:T(8,128)S(1)}, f32[128,128]{1,0:T(8,128)S(1)}, u32[]{:S(2)}, u32[]{:S(2)}) collective-permute-start(f32[128,128]{1,0:T(8,128)S(1)} %add.42.near), channel_id=1, source_target_pairs={{0,4},{1,5},{2,6},{3,7},{4,0},{5,1},{6,2},{7,3},{8,12},{9,13},{10,... | collective-permute-start | bytes 196616 | tf_op jit(solution)/shard_map/ppermute | solution.py:350
  27.5 7.6 %collective-permute-start.10 = (f32[96,128]{1,0:T(8,128)S(1)}, f32[96,128]{1,0:T(8,128)S(1)}, u32[]{:S(2)}, u32[]{:S(2)}) collective-permute-start(f32[96,128]{1,0:T(8,128)S(1)} %add.44.refs_2_), channel_id=1, source_target_pairs={{0,4},{1,5},{2,6},{3,7},{4,0},{5,1},{6,2},{7,3},{8,12},{9,13},{10,... | collective-permute-start | bytes 147464 | tf_op jit(solution)/shard_map/ppermute | solution.py:350
  37.3 1.3 %collective-permute-start.11 = (f32[224,128]{1,0:T(8,128)S(1)}, f32[224,128]{1,0:T(8,128)S(1)}, u32[]{:S(2)}, u32[]{:S(2)}) collective-permute-start(f32[224,128]{1,0:T(8,128)S(1)} %pair.1.refs_1_), channel_id=1, source_target_pairs={{0,1},{1,0},{2,3},{3,2},{4,5},{5,4},{6,7},{7,6},{8,9},{9,8},{10,11... | collective-permute-start | bytes 344072 | tf_op jit(solution)/shard_map/ppermute | solution.py:350
  42.4 3.8 %collective-permute-start.12 = (f32[16,256]{1,0:T(8,128)S(1)}, f32[16,256]{1,0:T(8,128)S(1)}, u32[]{:S(2)}, u32[]{:S(2)}) collective-permute-start(f32[16,256]{1,0:T(8,128)S(1)} %get-tuple-element.28), channel_id=1, source_target_pairs={{0,16},{8,24},{16,0},{24,8},{1,17},{9,25},{17,1},{25,9},{2,18},{10... | collective-permute-start | bytes 49160 | tf_op jit(solution)/shard_map/ppermute | solution.py:350

commit v5 on v4

--- a/solution.py
+++ b/solution.py
@@ -193,17 +193,16 @@
     cross = dot_nt(pieces, sketch[...])
     block = lambda i, j: gram[i * ranks : (i + 1) * ranks, j * ranks : (j + 1) * ranks]
     row = lambda *xs: jnp.concatenate(xs, axis=1)
-    column = lambda *xs: jnp.concatenate(xs, axis=0)
     solo = lambda i: row(block(i, i), cross[i * ranks : (i + 1) * ranks])
     half = ranks // 2
     fold = lambda x: row(x[:half], x[half:])
-    near = [column(solo(i), solo(i + 1)) for i in (0, 2)]
-    far = [column(fold(block(2 * i, 2 * i + 1)), row(block(i, 2), block(i, 3))) for i in (0, 1)]
     low = place[picked] == 0
-    keep[...] = jnp.where(low, near[0], near[1])
-    send[...] = jnp.where(low, near[1], near[0])
-    keep_far[...] = jnp.where(low, far[0], far[1])
-    send_far[...] = jnp.where(low, far[1], far[0])
+    keep[:ranks, :], keep[ranks:, :] = solo(0), solo(1)
+    send[:ranks, :], send[ranks:, :] = solo(2), solo(3)
+    keep_far[:half, :], send_far[:half, :] = fold(block(0, 1)), fold(block(2, 3))
+    across = lambda i, j: row(block(i, j), block(i, j + 1))
+    keep_far[half:, :] = jnp.where(low, across(0, 2), across(3, 0))
+    send_far[half:, :] = jnp.where(low, across(1, 2), across(2, 0))
 
 
 def products(leaves, sketch, place, ranks):
@@ -231,7 +230,8 @@
     eye = lax.broadcasted_iota(jnp.int32, shape, 0) == lax.broadcasted_iota(jnp.int32, shape, 1)
     mats = []
     for system in systems:
-        trace = jnp.sum(jnp.where(eye, system, 0.0))
+        trace = jnp.sum(jnp.where(eye, system, 0.0), axis=0, keepdims=True)
+        trace = jnp.sum(trace, axis=1, keepdims=True)
         system = system + jnp.where(eye, 0.01 * trace / size + 1e-06, 0.0)
         mats.append([system[8 * i : 8 * i + 8] for i in range(blocks)])
     sub = lax.broadcasted_iota(jnp.int32, (8, 2 * size), 0)
@@ -303,8 +303,8 @@
     row = lambda *xs: jnp.concatenate(xs, axis=1)
     column = lambda *xs: jnp.concatenate(xs, axis=0)
     low = place[0] == 0
-    a, b = mine[size : 2 * size, :], other[size : 2 * size, :]
-    p, q = jnp.where(low, a, b), jnp.where(low, b, a)
+    a_t, b_t = mine[size : 2 * size, :], other[size : 2 * size, :]
+    p, q = jnp.where(low, a_t, b_t), jnp.where(low, b_t, a_t)
     last = 5 * size // 2
     a, b = mine[last:, :], other[last:, :]
     corner = column(jnp.where(low, a, b), jnp.where(low, b, a))
@@ -320,15 +320,13 @@
         gram = gram + square * dot_wide(coef_t, wide_dot(half[:size, :size], coef))
         cross = cross + scaling * dot_wide(coef_t, half[:size, size:])
     (last,) = ridge_solve([row(gram, cross)])
-    total_t = dot_wide(flip(last), row(p, q))
+    table[:size, :size] = last.astype(F32).T
+    count = own.shape[0]
+    picks = [table[pl.ds(pl.multiple_of(place[i] * count, count), count), :size] for i in (1, 2)]
+    total_t = dot_wide(column(*picks).astype(BF16), row(a_t, b_t))
     result = (square * scaling) * sum(dot(part, pieces[...]) for part in halves(total_t))
-    table[:size, :] = result[:, : 2 * size]
-    table[size:, :] = result[:, 2 * size :]
-    count = own.shape[0]
-    for out, at in ((own, place[1]), (send, place[2])):
-        at = pl.multiple_of(at * count, count)
-        for i in range(2):
-            out[:, i * 2 * size : (i + 1) * 2 * size] = table[pl.ds(at + i * size, count), :]
+    own[...] = result[:count]
+    send[...] = result[count:]
 
 
 def local_call(kernel, name, out, *args, scalars=(), scratch=(), flops=1 << 24):
@@ -371,6 +369,7 @@
     leaves = [leaf] + [swap(leaf, "shots", m) for m in range(1, shots)]
     picked = shots * groups // 2
     chosen = lax.dynamic_slice_in_dim(pairing, shot // (shots // 2) * picked, picked)
+    chosen = lax.dynamic_slice_in_dim(jnp.concatenate([chosen, chosen]), side * (picked // 2), picked)
     slots = (chosen // groups ^ shot) * groups + chosen % groups
     sketch_t = jnp.transpose(sketch, (1, 0, 2)).reshape(ranks, coarse_x * layer)
     slots = jnp.concatenate([slots, side[None]]).astype(jnp.int32)
@@ -403,7 +402,7 @@
     part = jax.ShapeDtypeStruct((columns, pieces.shape[1]), F32)
     own_part, sent = local_call(
         lambda *refs: root_kernel(scaling, *refs), "root", [part, part], mine, other, pieces,
-        scalars=(spots,), scratch=[pltpu.VMEM((2 * ranks, 2 * ranks), F32)],
+        scalars=(spots,), scratch=[pltpu.VMEM((ranks, 2 * ranks), F32)],
     )
     total = (own_part + swap(sent, "shots", across_tree)).astype(BF16)
     return jnp.transpose(total.reshape(columns, coarse_x, layer), (1, 0, 2))

time: 47 us -> 46.8 us (level)
  no operation moved by 1% of the time
where the time goes in v5:
time: 46.8 us; the launch traced here: 46.7 us
  starting transfers between devices  15.6 us (33%)
  waiting for transfers between devices  15.6 us (33%)
  Pallas kernels  14 us (30%)
  local copies, waits for them, and re-layouts  0.95 us (2%)
    ppermute x12, waiting for transfers between devices, swap(): lax.ppermute(x, axis, [(i, i ^ mask) for i in range(lax.axis_size(axis))])  14 us
    ppermute x12, starting transfers between devices, swap(): lax.ppermute(x, axis, [(i, i ^ mask) for i in range(lax.axis_size(axis))])  11.1 us
    pallas_call x3, Pallas kernels, local_call(): pl.pallas_call(kernel, in_specs=[smem] * len(scalars) + [vmem] * len(args...  7.85 us
    pallas_call x1, Pallas kernels, restrict(): pl.pallas_call(restrict_kernel, in_specs=[pl.BlockSpec(memory_space=pltpu...  5.24 us
    ppermute x1, starting transfers between devices, body(): from_chip = lax.ppermute(to_chip, 'space', across)  4.55 us
    ppermute x1, waiting for transfers between devices, body(): from_chip = lax.ppermute(to_chip, 'space', across)  1.63 us
  transfers between devices with their start and end apart: 13, of which 10 were waited for; matrix products, arithmetic and copies ran while one was open for 1% of the time, Pallas kernels for 4%

profile of v5, /device:TPU:0, one launch (start us, length us, event | category | flops | bytes accessed | tf_op | source)
XLA Modules:
  0.0 46.7 jit_solution(3795196046125032262)
XLA Ops:
  0.0 0.0 copy-start.1
  0.0 0.0 copy-start
  0.0 5.2 %restrict.1 = (f32[128,256]{1,0:T(8,128)S(1)}, f32[128,128]{1,0:T(8,128)S(1)}, f32[128,128]{1,0:T(8,128)S(1)}) custom-call(s32[1]{0:T(128)} %bitcast.side, bf16[32768,128]{1,0:T(8,128)(2,1)} %bitcast.9, bf16[2,256,128]{2,1,0:T(8,128)(2,1)} %bitcast.10, bf16[32,256]{1,0:T(8,128)(2,1)} %constant.74.table_xy, bf16[512,256]{1,0:T(8,128)(2,1)} %constant.79.table_z), custom_call_target="tpu_custom_call" | custom-call | tf_op jit(solution)/shard_map/restrict/pallas_call | solution.py:151
  5.3 4.6 %collective-permute-start = (f32[128,128]{1,0:T(8,128)S(1)}, f32[128,128]{1,0:T(8,128)S(1)}, u32[]{:S(2)}, u32[]{:S(2)}) collective-permute-start(f32[128,128]{1,0:T(8,128)S(1)} %get-tuple-element.18), channel_id=1, source_target_pairs={{0,7},{1,2},{2,1},{3,4},{4,3},{5,6},{6,5},{7,0},{8,15},{9,10},{10,... | collective-permute-start | bytes 196616 | tf_op jit(solution)/shard_map/ppermute | solution.py:363
  9.8 0.0 collective-permute-start.1
  9.8 0.0 copy-done.1
  9.8 0.1 dynamic_slice.6
  9.9 0.1 pad_add_fusion.1
  10.0 0.0 copy-done
  10.0 0.1 copy.7
  10.0 0.1 reshape.14.refs_5_
  10.1 0.1 fusion.1
  10.2 1.6 %collective-permute-done = f32[128,128]{1,0:T(8,128)S(1)} collective-permute-done((f32[128,128]{1,0:T(8,128)S(1)}, f32[128,128]{1,0:T(8,128)S(1)}, u32[]{:S(2)}, u32[]{:S(2)}) %collective-permute-start) | collective-permute-done | bytes 65568 | tf_op jit(solution)/shard_map/ppermute | solution.py:363
  11.9 0.0 collective-permute-done.1
  11.9 3.3 %collective-permute-start.4 = (bf16[128,256]{1,0:T(8,128)(2,1)S(1)}, bf16[128,256]{1,0:T(8,128)(2,1)S(1)}, u32[]{:S(2)}, u32[]{:S(2)}) collective-permute-start(bf16[128,256]{1,0:T(8,128)(2,1)S(1)} %fusion.refs_1_), channel_id=1, source_target_pairs={{0,24},{8,16},{16,8},{24,0},{1,25},{9,17},{17,9},{25,1},{2,26},{10... | collective-permute-start | bytes 196616 | tf_op jit(solution)/shard_map/ppermute | solution.py:348
  15.2 0.5 %collective-permute-start.3 = (bf16[128,256]{1,0:T(8,128)(2,1)S(1)}, bf16[128,256]{1,0:T(8,128)(2,1)S(1)}, u32[]{:S(2)}, u32[]{:S(2)}) collective-permute-start(bf16[128,256]{1,0:T(8,128)(2,1)S(1)} %fusion.refs_1_), channel_id=1, source_target_pairs={{0,16},{8,24},{16,0},{24,8},{1,17},{9,25},{17,1},{25,9},{2,18},{10... | collective-permute-start | bytes 196616 | tf_op jit(solution)/shard_map/ppermute | solution.py:348
  15.8 0.1 collective-permute-start.2
  15.9 0.1 pad_add_fusion.2.refs_0_
  16.0 1.8 %collective-permute-done.4.refs_4_ = bf16[128,256]{1,0:T(8,128)(2,1)S(1)} collective-permute-done((bf16[128,256]{1,0:T(8,128)(2,1)S(1)}, bf16[128,256]{1,0:T(8,128)(2,1)S(1)}, u32[]{:S(2)}, u32[]{:S(2)}) %collective-permute-start.4) | collective-permute-done | bytes 65568 | tf_op jit(solution)/shard_map/ppermute | solution.py:348
  17.8 1.7 %collective-permute-done.3.refs_3_ = bf16[128,256]{1,0:T(8,128)(2,1)S(1)} collective-permute-done((bf16[128,256]{1,0:T(8,128)(2,1)S(1)}, bf16[128,256]{1,0:T(8,128)(2,1)S(1)}, u32[]{:S(2)}, u32[]{:S(2)}) %collective-permute-start.3) | collective-permute-done | bytes 65568 | tf_op jit(solution)/shard_map/ppermute | solution.py:348
  19.5 0.5 %collective-permute-done.2.refs_2_ = bf16[128,256]{1,0:T(8,128)(2,1)S(1)} collective-permute-done((bf16[128,256]{1,0:T(8,128)(2,1)S(1)}, bf16[128,256]{1,0:T(8,128)(2,1)S(1)}, u32[]{:S(2)}, u32[]{:S(2)}) %collective-permute-start.2) | collective-permute-done | bytes 65568 | tf_op jit(solution)/shard_map/ppermute | solution.py:348
  20.0 0.9 %products.1 = (bf16[256,256]{1,0:T(8,128)(2,1)S(1)}, f32[128,128]{1,0:T(8,128)S(1)}, f32[128,128]{1,0:T(8,128)S(1)}, f32[96,128]{1,0:T(8,128)S(1)}, f32[96,128]{1,0:T(8,128)S(1)}) custom-call(s32[5]{0:T(128)S(1)} %pad_add_fusion.2.refs_0_, bf16[128,256]{1,0:T(8,128)(2,1)S(1)} %fusion.refs_1_, bf16[128,256]{1,0:T(8,128)(2,1)S(1)} %collective-permute-done.2.refs_2_, ...), custom_call_target="tpu_custom_call" | custom-call | tf_op jit(solution)/shard_map/products/pallas_call | solution.py:215
  20.9 0.1 collective-permute-start.5
  21.0 0.5 %collective-permute-start.8 = (f32[96,128]{1,0:T(8,128)S(1)}, f32[96,128]{1,0:T(8,128)S(1)}, u32[]{:S(2)}, u32[]{:S(2)}) collective-permute-start(f32[96,128]{1,0:T(8,128)S(1)} %get-tuple-element.25), channel_id=1, source_target_pairs={{0,1},{1,0},{2,3},{3,2},{4,5},{5,4},{6,7},{7,6},{8,9},{9,8},{10,11... | collective-permute-start | bytes 147464 | tf_op jit(solution)/shard_map/ppermute | solution.py:348
  21.5 0.7 %collective-permute-done.5 = f32[128,128]{1,0:T(8,128)S(1)} collective-permute-done((f32[128,128]{1,0:T(8,128)S(1)}, f32[128,128]{1,0:T(8,128)S(1)}, u32[]{:S(2)}, u32[]{:S(2)}) %collective-permute-start.5) | collective-permute-done | bytes 65568 | tf_op jit(solution)/shard_map/ppermute | solution.py:348
  22.2 0.1 collective-permute-start.6
  22.3 0.0 collective-permute-done.8
  22.4 2.0 %collective-permute-start.9 = (f32[96,128]{1,0:T(8,128)S(1)}, f32[96,128]{1,0:T(8,128)S(1)}, u32[]{:S(2)}, u32[]{:S(2)}) collective-permute-start(f32[96,128]{1,0:T(8,128)S(1)} %add.47), channel_id=1, source_target_pairs={{0,2},{1,3},{2,0},{3,1},{4,6},{5,7},{6,4},{7,5},{8,10},{9,11},{10,... | collective-permute-start | bytes 147464 | tf_op jit(solution)/shard_map/ppermute | solution.py:348
  24.4 2.6 %collective-permute-done.6 = f32[128,128]{1,0:T(8,128)S(1)} collective-permute-done((f32[128,128]{1,0:T(8,128)S(1)}, f32[128,128]{1,0:T(8,128)S(1)}, u32[]{:S(2)}, u32[]{:S(2)}) %collective-permute-start.6) | collective-permute-done | bytes 65568 | tf_op jit(solution)/shard_map/ppermute | solution.py:348
  27.0 0.3 collective-permute-start.7
  27.3 0.2 collective-permute-done.9
  27.5 2.5 %collective-permute-start.10 = (f32[96,128]{1,0:T(8,128)S(1)}, f32[96,128]{1,0:T(8,128)S(1)}, u32[]{:S(2)}, u32[]{:S(2)}) collective-permute-start(f32[96,128]{1,0:T(8,128)S(1)} %add.48.refs_2_), channel_id=1, source_target_pairs={{0,4},{1,5},{2,6},{3,7},{4,0},{5,1},{6,2},{7,3},{8,12},{9,13},{10,... | collective-permute-start | bytes 147464 | tf_op jit(solution)/shard_map/ppermute | solution.py:348
  30.1 2.9 %collective-permute-done.7.got = f32[128,128]{1,0:T(8,128)S(1)} collective-permute-done((f32[128,128]{1,0:T(8,128)S(1)}, f32[128,128]{1,0:T(8,128)S(1)}, u32[]{:S(2)}, u32[]{:S(2)}) %collective-permute-start.7) | collective-permute-done | bytes 65568 | tf_op jit(solution)/shard_map/ppermute | solution.py:348
  33.0 2.0 %leaf.1 = (f32[128,128]{1,0:T(8,128)S(1)}, bf16[128,64]{1,0:T(8,128)(2,1)S(1)}) custom-call(f32[128,128]{1,0:T(8,128)S(1)} %add.46.near, f32[128,128]{1,0:T(8,128)S(1)} %collective-permute-done.7.got), custom_call_target="tpu_custom_call" | custom-call | flops 16777216 | bytes 131072 | tf_op jit(solution)/shard_map/leaf/pallas_call | solution.py:335
  35.0 0.0 collective-permute-done.10.refs_3_
  35.1 2.1 %pair.1.refs_1_ = f32[224,128]{1,0:T(8,128)S(1)} custom-call(f32[128,128]{1,0:T(8,128)S(1)} %get-tuple-element.22.refs_0_, bf16[128,64]{1,0:T(8,128)(2,1)S(1)} %get-tuple-element.23.refs_1_, f32[96,128]{1,0:T(8,128)S(1)} %add.48.refs_2_, f32[96,128]{1,0:T(8,128)S(1)} %collective-permute-done.10.refs_3_), custom_call_target="tpu_custom_call" | custom-call | flops 16777216 | bytes 131072 | tf_op jit(solution)/shard_map/pair/pallas_call | solution.py:335
  37.2 0.0 collective-permute-start.11
  37.2 0.1 pad_add_fusion.refs_0_
  37.3 1.3 %collective-permute-done.11.refs_2_ = f32[224,128]{1,0:T(8,128)S(1)} collective-permute-done((f32[224,128]{1,0:T(8,128)S(1)}, f32[224,128]{1,0:T(8,128)S(1)}, u32[]{:S(2)}, u32[]{:S(2)}) %collective-permute-start.11) | collective-permute-done | bytes 114720 | tf_op jit(solution)/shard_map/ppermute | solution.py:348
  38.5 3.7 %root.1 = (f32[16,256]{1,0:T(8,128)S(1)}, f32[16,256]{1,0:T(8,128)S(1)}) custom-call(s32[3]{0:T(128)S(1)} %pad_add_fusion.refs_0_, f32[224,128]{1,0:T(8,128)S(1)} %pair.1.refs_1_, f32[224,128]{1,0:T(8,128)S(1)} %collective-permute-done.11.refs_2_, bf16[256,256]{1,0:T(8,128)(2,1)S(1)} %get-tuple-element.26.refs_3_), custom_call_target="tpu_custom_call" | custom-call | flops 16777216 | bytes 131072 | tf_op jit(solution)/shard_map/root/pallas_call | solution.py:335
  42.2 1.5 %collective-permute-start.12 = (f32[16,256]{1,0:T(8,128)S(1)}, f32[16,256]{1,0:T(8,128)S(1)}, u32[]{:S(2)}, u32[]{:S(2)}) collective-permute-start(f32[16,256]{1,0:T(8,128)S(1)} %get-tuple-element.28), channel_id=1, source_target_pairs={{0,16},{8,24},{16,0},{24,8},{1,17},{9,25},{17,1},{25,9},{2,18},{10... | collective-permute-start | bytes 49160 | tf_op jit(solution)/shard_map/ppermute | solution.py:348
  43.7 2.2 %collective-permute-done.12 = f32[16,256]{1,0:T(8,128)S(1)} collective-permute-done((f32[16,256]{1,0:T(8,128)S(1)}, f32[16,256]{1,0:T(8,128)S(1)}, u32[]{:S(2)}, u32[]{:S(2)}) %collective-permute-start.12) | collective-permute-done | bytes 16416 | tf_op jit(solution)/shard_map/ppermute | solution.py:348
  46.0 0.1 reshape.15
  46.1 0.6 %copy.10 = bf16[16,4,64]{2,0,1:T(8,128)(2,1)} copy(bf16[16,4,64]{2,1,0:T(4,128)(2,1)S(1)} %reshape.15) | data formatting | bytes 16384 | tf_op jit(solution)/shard_map/reshape | solution.py:408
  (7 shorter events, 0.1 us)
Async XLA Ops:
  0.0 9.8 %copy-start.1 = (s32[8]{0:T(128)S(1)}, s32[8]{0:T(128)}, u32[]{:S(2)}) copy-start(s32[8]{0:T(128)} %param.9) | copy-start | bytes 100
  0.0 10.0 %copy-start = (bf16[4,64,64]{2,1,0:T(8,128)(2,1)S(1)}, bf16[4,64,64]{2,1,0:T(8,128)(2,1)}, u32[]{:S(2)}) copy-start(bf16[4,64,64]{2,1,0:T(8,128)(2,1)} %param.8) | copy-start | bytes 98308
  5.3 6.6 %collective-permute-start = (f32[128,128]{1,0:T(8,128)S(1)}, f32[128,128]{1,0:T(8,128)S(1)}, u32[]{:S(2)}, u32[]{:S(2)}) collective-permute-start(f32[128,128]{1,0:T(8,128)S(1)} %get-tuple-element.18), channel_id=1, source_target_pairs={{0,7},{1,2},{2,1},{3,4},{4,3},{5,6},{6,5},{7,0},{8,15},{9,10},{10,... | collective-permute-start | bytes 196616 | tf_op jit(solution)/shard_map/ppermute | solution.py:363
  9.8 2.1 %collective-permute-start.1 = (f32[128,128]{1,0:T(8,128)S(1)}, f32[128,128]{1,0:T(8,128)S(1)}, u32[]{:S(2)}, u32[]{:S(2)}) collective-permute-start(f32[128,128]{1,0:T(8,128)S(1)} %get-tuple-element.19), channel_id=1, source_target_pairs={{0,1},{1,0},{2,3},{3,2},{4,5},{5,4},{6,7},{7,6},{8,9},{9,8},{10,11... | collective-permute-start | bytes 196616 | tf_op jit(solution)/shard_map/ppermute | solution.py:348
  11.9 5.9 %collective-permute-start.4 = (bf16[128,256]{1,0:T(8,128)(2,1)S(1)}, bf16[128,256]{1,0:T(8,128)(2,1)S(1)}, u32[]{:S(2)}, u32[]{:S(2)}) collective-permute-start(bf16[128,256]{1,0:T(8,128)(2,1)S(1)} %fusion.refs_1_), channel_id=1, source_target_pairs={{0,24},{8,16},{16,8},{24,0},{1,25},{9,17},{17,9},{25,1},{2,26},{10... | collective-permute-start | bytes 196616 | tf_op jit(solution)/shard_map/ppermute | solution.py:348
  15.2 4.3 %collective-permute-start.3 = (bf16[128,256]{1,0:T(8,128)(2,1)S(1)}, bf16[128,256]{1,0:T(8,128)(2,1)S(1)}, u32[]{:S(2)}, u32[]{:S(2)}) collective-permute-start(bf16[128,256]{1,0:T(8,128)(2,1)S(1)} %fusion.refs_1_), channel_id=1, source_target_pairs={{0,16},{8,24},{16,0},{24,8},{1,17},{9,25},{17,1},{25,9},{2,18},{10... | collective-permute-start | bytes 196616 | tf_op jit(solution)/shard_map/ppermute | solution.py:348
  15.8 4.3 %collective-permute-start.2 = (bf16[128,256]{1,0:T(8,128)(2,1)S(1)}, bf16[128,256]{1,0:T(8,128)(2,1)S(1)}, u32[]{:S(2)}, u32[]{:S(2)}) collective-permute-start(bf16[128,256]{1,0:T(8,128)(2,1)S(1)} %fusion.refs_1_), channel_id=1, source_target_pairs={{0,8},{8,0},{16,24},{24,16},{1,9},{9,1},{17,25},{25,17},{2,10},{10... | collective-permute-start | bytes 196616 | tf_op jit(solution)/shard_map/ppermute | solution.py:348
  20.9 1.3 %collective-permute-start.5 = (f32[128,128]{1,0:T(8,128)S(1)}, f32[128,128]{1,0:T(8,128)S(1)}, u32[]{:S(2)}, u32[]{:S(2)}) collective-permute-start(f32[128,128]{1,0:T(8,128)S(1)} %get-tuple-element.21), channel_id=1, source_target_pairs={{0,1},{1,0},{2,3},{3,2},{4,5},{5,4},{6,7},{7,6},{8,9},{9,8},{10,11... | collective-permute-start | bytes 196616 | tf_op jit(solution)/shard_map/ppermute | solution.py:348
  21.0 1.4 %collective-permute-start.8 = (f32[96,128]{1,0:T(8,128)S(1)}, f32[96,128]{1,0:T(8,128)S(1)}, u32[]{:S(2)}, u32[]{:S(2)}) collective-permute-start(f32[96,128]{1,0:T(8,128)S(1)} %get-tuple-element.25), channel_id=1, source_target_pairs={{0,1},{1,0},{2,3},{3,2},{4,5},{5,4},{6,7},{7,6},{8,9},{9,8},{10,11... | collective-permute-start | bytes 147464 | tf_op jit(solution)/shard_map/ppermute | solution.py:348
  22.2 4.7 %collective-permute-start.6 = (f32[128,128]{1,0:T(8,128)S(1)}, f32[128,128]{1,0:T(8,128)S(1)}, u32[]{:S(2)}, u32[]{:S(2)}) collective-permute-start(f32[128,128]{1,0:T(8,128)S(1)} %add.45), channel_id=1, source_target_pairs={{0,2},{1,3},{2,0},{3,1},{4,6},{5,7},{6,4},{7,5},{8,10},{9,11},{10,... | collective-permute-start | bytes 196616 | tf_op jit(solution)/shard_map/ppermute | solution.py:348
  22.4 5.1 %collective-permute-start.9 = (f32[96,128]{1,0:T(8,128)S(1)}, f32[96,128]{1,0:T(8,128)S(1)}, u32[]{:S(2)}, u32[]{:S(2)}) collective-permute-start(f32[96,128]{1,0:T(8,128)S(1)} %add.47), channel_id=1, source_target_pairs={{0,2},{1,3},{2,0},{3,1},{4,6},{5,7},{6,4},{7,5},{8,10},{9,11},{10,... | collective-permute-start | bytes 147464 | tf_op jit(solution)/shard_map/ppermute | solution.py:348
  27.0 6.0 %collective-permute-start.7 = (f32[128,128]{1,0:T(8,128)S(1)}, f32[128,128]{1,0:T(8,128)S(1)}, u32[]{:S(2)}, u32[]{:S(2)}) collective-permute-start(f32[128,128]{1,0:T(8,128)S(1)} %add.46.near), channel_id=1, source_target_pairs={{0,4},{1,5},{2,6},{3,7},{4,0},{5,1},{6,2},{7,3},{8,12},{9,13},{10,... | collective-permute-start | bytes 196616 | tf_op jit(solution)/shard_map/ppermute | solution.py:348
  27.5 7.5 %collective-permute-start.10 = (f32[96,128]{1,0:T(8,128)S(1)}, f32[96,128]{1,0:T(8,128)S(1)}, u32[]{:S(2)}, u32[]{:S(2)}) collective-permute-start(f32[96,128]{1,0:T(8,128)S(1)} %add.48.refs_2_), channel_id=1, source_target_pairs={{0,4},{1,5},{2,6},{3,7},{4,0},{5,1},{6,2},{7,3},{8,12},{9,13},{10,... | collective-permute-start | bytes 147464 | tf_op jit(solution)/shard_map/ppermute | solution.py:348
  37.2 1.3 %collective-permute-start.11 = (f32[224,128]{1,0:T(8,128)S(1)}, f32[224,128]{1,0:T(8,128)S(1)}, u32[]{:S(2)}, u32[]{:S(2)}) collective-permute-start(f32[224,128]{1,0:T(8,128)S(1)} %pair.1.refs_1_), channel_id=1, source_target_pairs={{0,1},{1,0},{2,3},{3,2},{4,5},{5,4},{6,7},{7,6},{8,9},{9,8},{10,11... | collective-permute-start | bytes 344072 | tf_op jit(solution)/shard_map/ppermute | solution.py:348
  42.2 3.8 %collective-permute-start.12 = (f32[16,256]{1,0:T(8,128)S(1)}, f32[16,256]{1,0:T(8,128)S(1)}, u32[]{:S(2)}, u32[]{:S(2)}) collective-permute-start(f32[16,256]{1,0:T(8,128)S(1)} %get-tuple-element.28), channel_id=1, source_target_pairs={{0,16},{8,24},{16,0},{24,8},{1,17},{9,25},{17,1},{25,9},{2,18},{10... | collective-permute-start | bytes 49160 | tf_op jit(solution)/shard_map/ppermute | solution.py:348

commit v6 on v5

--- a/solution.py
+++ b/solution.py
@@ -122,8 +122,8 @@
         layers.append(total[:, :lanes] + total[:, lanes:])
     own[...] = jnp.concatenate(layers[1:-1], axis=1)
     odd = side[0] == 1
-    to_core[...] = jnp.where(odd, layers[0], layers[-1])
-    to_chip[...] = jnp.where(odd, layers[-1], layers[0])
+    to_core[...] = jnp.where(odd, layers[0], layers[-1]).astype(BF16)
+    to_chip[...] = jnp.where(odd, layers[-1], layers[0]).astype(BF16)
 
 
 def restrict(probes, sources, side):
@@ -152,7 +152,11 @@
         restrict_kernel,
         in_specs=[pl.BlockSpec(memory_space=pltpu.SMEM)] + [outside] * 4,
         out_specs=[vmem] * 3,
-        out_shape=[pltpu.VMEM((all_rows, n), F32) for n in (lanes, 128, 128)],
+        out_shape=[
+            pltpu.VMEM((all_rows, lanes), F32),
+            pltpu.VMEM((all_rows, 128), BF16),
+            pltpu.VMEM((all_rows, 128), BF16),
+        ],
         scratch_shapes=[
             pltpu.VMEM((edges_x * coarse_y * all_rows, fine_z), F32),
             pltpu.VMEM((all_rows * series, fine_z), BF16),
@@ -358,9 +362,9 @@
     side = place % 2
 
     own, to_core, to_chip = restrict(probes, sources, side[None].astype(jnp.int32))
-    from_core = swap(to_core, "space", 1)
+    from_core = swap(to_core, "space", 1).astype(F32)
     across = [(i, (i + 1 if i % 2 else i - 1) % space) for i in range(space)]
-    from_chip = lax.ppermute(to_chip, "space", across)
+    from_chip = lax.ppermute(to_chip, "space", across).astype(F32)
     from_chip = jnp.where((place == 0) | (place == space - 1), 0.0, from_chip)
     from_below = jnp.where(side == 0, from_chip, from_core)
     from_above = jnp.where(side == 0, from_core, from_chip)

time: 46.8 us -> 46.2 us (0.987)
  transfers between devices with their start and end apart: 13 -> 13, of which waited for: 10 -> 9; matrix products, arithmetic and copies ran while one was open for 1% -> 1% of each run, Pallas kernels for 4% -> 4%
where the time goes in v6:
time: 46.2 us; the launch traced here: 46 us
  starting transfers between devices  15.4 us (33%)
  waiting for transfers between devices  15.3 us (33%)
  Pallas kernels  14 us (30%)
  local copies, waits for them, and re-layouts  0.95 us (2%)
    ppermute x12, waiting for transfers between devices, swap(): lax.ppermute(x, axis, [(i, i ^ mask) for i in range(lax.axis_size(axis))])  14 us
    ppermute x12, starting transfers between devices, swap(): lax.ppermute(x, axis, [(i, i ^ mask) for i in range(lax.axis_size(axis))])  10.8 us
    pallas_call x3, Pallas kernels, local_call(): pl.pallas_call(kernel, in_specs=[smem] * len(scalars) + [vmem] * len(args...  7.85 us
    pallas_call x1, Pallas kernels, restrict(): pl.pallas_call(restrict_kernel, in_specs=[pl.BlockSpec(memory_space=pltpu...  5.24 us
    ppermute x1, starting transfers between devices, body(): from_chip = lax.ppermute(to_chip, 'space', across).astype(F32)  4.55 us
    ppermute x1, waiting for transfers between devices, body(): from_chip = lax.ppermute(to_chip, 'space', across).astype(F32)  1.28 us
  transfers between devices with their start and end apart: 13, of which 9 were waited for; matrix products, arithmetic and copies ran while one was open for 1% of the time, Pallas kernels for 4%

profile of v6, /device:TPU:0, one launch (start us, length us, event | category | flops | bytes accessed | tf_op | source)
XLA Modules:
  0.0 46.0 jit_solution(10474225969484098079)
XLA Ops:
  0.0 0.0 copy-start.1
  0.0 0.0 copy-start
  0.0 5.2 %restrict.1 = (f32[128,256]{1,0:T(8,128)S(1)}, bf16[128,128]{1,0:T(8,128)(2,1)S(1)}, bf16[128,128]{1,0:T(8,128)(2,1)S(1)}) custom-call(s32[1]{0:T(128)} %bitcast.side, bf16[32768,128]{1,0:T(8,128)(2,1)} %bitcast.9, bf16[2,256,128]{2,1,0:T(8,128)(2,1)} %bitcast.10, bf16[32,256]{1,0:T(8,128)(2,1)} %constant.74.table_xy, bf16[512,256]{1,0:T(8,128)(2,1)} %constant.79.table_z), custom_call_target="tpu_custom_call" | custom-call | tf_op jit(solution)/shard_map/restrict/pallas_call | solution.py:151
  5.3 4.6 %collective-permute-start = (bf16[128,128]{1,0:T(8,128)(2,1)S(1)}, bf16[128,128]{1,0:T(8,128)(2,1)S(1)}, u32[]{:S(2)}, u32[]{:S(2)}) collective-permute-start(bf16[128,128]{1,0:T(8,128)(2,1)S(1)} %get-tuple-element.18), channel_id=1, source_target_pairs={{0,7},{1,2},{2,1},{3,4},{4,3},{5,6},{6,5},{7,0},{8,15},{9,10},{10,... | collective-permute-start | bytes 98312 | tf_op jit(solution)/shard_map/ppermute | solution.py:367
  9.8 0.0 collective-permute-start.1
  9.8 0.0 copy-done.1
  9.8 0.1 dynamic_slice.6
  9.9 0.1 pad_add_fusion.1
  10.0 0.1 fusion.1
  10.1 0.0 copy-done
  10.1 0.1 copy.7
  10.1 0.1 reshape.14.refs_5_
  10.2 1.3 %collective-permute-done = bf16[128,128]{1,0:T(8,128)(2,1)S(1)} collective-permute-done((bf16[128,128]{1,0:T(8,128)(2,1)S(1)}, bf16[128,128]{1,0:T(8,128)(2,1)S(1)}, u32[]{:S(2)}, u32[]{:S(2)}) %collective-permute-start) | collective-permute-done | bytes 32800 | tf_op jit(solution)/shard_map/ppermute | solution.py:367
  11.5 0.0 collective-permute-done.1
  11.6 2.9 %collective-permute-start.4 = (bf16[128,256]{1,0:T(8,128)(2,1)S(1)}, bf16[128,256]{1,0:T(8,128)(2,1)S(1)}, u32[]{:S(2)}, u32[]{:S(2)}) collective-permute-start(bf16[128,256]{1,0:T(8,128)(2,1)S(1)} %fusion.refs_1_), channel_id=1, source_target_pairs={{0,24},{8,16},{16,8},{24,0},{1,25},{9,17},{17,9},{25,1},{2,26},{10... | collective-permute-start | bytes 196616 | tf_op jit(solution)/shard_map/ppermute | solution.py:352
  14.5 0.5 %collective-permute-start.3 = (bf16[128,256]{1,0:T(8,128)(2,1)S(1)}, bf16[128,256]{1,0:T(8,128)(2,1)S(1)}, u32[]{:S(2)}, u32[]{:S(2)}) collective-permute-start(bf16[128,256]{1,0:T(8,128)(2,1)S(1)} %fusion.refs_1_), channel_id=1, source_target_pairs={{0,16},{8,24},{16,0},{24,8},{1,17},{9,25},{17,1},{25,9},{2,18},{10... | collective-permute-start | bytes 196616 | tf_op jit(solution)/shard_map/ppermute | solution.py:352
  15.0 0.1 collective-permute-start.2
  15.1 0.1 pad_add_fusion.2.refs_0_
  15.2 1.7 %collective-permute-done.4.refs_4_ = bf16[128,256]{1,0:T(8,128)(2,1)S(1)} collective-permute-done((bf16[128,256]{1,0:T(8,128)(2,1)S(1)}, bf16[128,256]{1,0:T(8,128)(2,1)S(1)}, u32[]{:S(2)}, u32[]{:S(2)}) %collective-permute-start.4) | collective-permute-done | bytes 65568 | tf_op jit(solution)/shard_map/ppermute | solution.py:352
  16.9 1.8 %collective-permute-done.3.refs_3_ = bf16[128,256]{1,0:T(8,128)(2,1)S(1)} collective-permute-done((bf16[128,256]{1,0:T(8,128)(2,1)S(1)}, bf16[128,256]{1,0:T(8,128)(2,1)S(1)}, u32[]{:S(2)}, u32[]{:S(2)}) %collective-permute-start.3) | collective-permute-done | bytes 65568 | tf_op jit(solution)/shard_map/ppermute | solution.py:352
  18.7 0.5 %collective-permute-done.2.refs_2_ = bf16[128,256]{1,0:T(8,128)(2,1)S(1)} collective-permute-done((bf16[128,256]{1,0:T(8,128)(2,1)S(1)}, bf16[128,256]{1,0:T(8,128)(2,1)S(1)}, u32[]{:S(2)}, u32[]{:S(2)}) %collective-permute-start.2) | collective-permute-done | bytes 65568 | tf_op jit(solution)/shard_map/ppermute | solution.py:352
  19.2 0.9 %products.1 = (bf16[256,256]{1,0:T(8,128)(2,1)S(1)}, f32[128,128]{1,0:T(8,128)S(1)}, f32[128,128]{1,0:T(8,128)S(1)}, f32[96,128]{1,0:T(8,128)S(1)}, f32[96,128]{1,0:T(8,128)S(1)}) custom-call(s32[5]{0:T(128)S(1)} %pad_add_fusion.2.refs_0_, bf16[128,256]{1,0:T(8,128)(2,1)S(1)} %fusion.refs_1_, bf16[128,256]{1,0:T(8,128)(2,1)S(1)} %collective-permute-done.2.refs_2_, ...), custom_call_target="tpu_custom_call" | custom-call | tf_op jit(solution)/shard_map/products/pallas_call | solution.py:219
  20.1 0.1 collective-permute-start.5
  20.2 0.5 %collective-permute-start.8 = (f32[96,128]{1,0:T(8,128)S(1)}, f32[96,128]{1,0:T(8,128)S(1)}, u32[]{:S(2)}, u32[]{:S(2)}) collective-permute-start(f32[96,128]{1,0:T(8,128)S(1)} %get-tuple-element.25), channel_id=1, source_target_pairs={{0,1},{1,0},{2,3},{3,2},{4,5},{5,4},{6,7},{7,6},{8,9},{9,8},{10,11... | collective-permute-start | bytes 147464 | tf_op jit(solution)/shard_map/ppermute | solution.py:352
  20.7 0.7 %collective-permute-done.5 = f32[128,128]{1,0:T(8,128)S(1)} collective-permute-done((f32[128,128]{1,0:T(8,128)S(1)}, f32[128,128]{1,0:T(8,128)S(1)}, u32[]{:S(2)}, u32[]{:S(2)}) %collective-permute-start.5) | collective-permute-done | bytes 65568 | tf_op jit(solution)/shard_map/ppermute | solution.py:352
  21.5 0.1 collective-permute-start.6
  21.5 0.0 collective-permute-done.8
  21.6 2.0 %collective-permute-start.9 = (f32[96,128]{1,0:T(8,128)S(1)}, f32[96,128]{1,0:T(8,128)S(1)}, u32[]{:S(2)}, u32[]{:S(2)}) collective-permute-start(f32[96,128]{1,0:T(8,128)S(1)} %add.47), channel_id=1, source_target_pairs={{0,2},{1,3},{2,0},{3,1},{4,6},{5,7},{6,4},{7,5},{8,10},{9,11},{10,... | collective-permute-start | bytes 147464 | tf_op jit(solution)/shard_map/ppermute | solution.py:352
  23.6 2.6 %collective-permute-done.6 = f32[128,128]{1,0:T(8,128)S(1)} collective-permute-done((f32[128,128]{1,0:T(8,128)S(1)}, f32[128,128]{1,0:T(8,128)S(1)}, u32[]{:S(2)}, u32[]{:S(2)}) %collective-permute-start.6) | collective-permute-done | bytes 65568 | tf_op jit(solution)/shard_map/ppermute | solution.py:352
  26.2 0.8 %collective-permute-start.7 = (f32[128,128]{1,0:T(8,128)S(1)}, f32[128,128]{1,0:T(8,128)S(1)}, u32[]{:S(2)}, u32[]{:S(2)}) collective-permute-start(f32[128,128]{1,0:T(8,128)S(1)} %add.46.near), channel_id=1, source_target_pairs={{0,4},{1,5},{2,6},{3,7},{4,0},{5,1},{6,2},{7,3},{8,12},{9,13},{10,... | collective-permute-start | bytes 196616 | tf_op jit(solution)/shard_map/ppermute | solution.py:352
  27.0 0.0 collective-permute-done.9
  27.0 2.3 %collective-permute-start.10 = (f32[96,128]{1,0:T(8,128)S(1)}, f32[96,128]{1,0:T(8,128)S(1)}, u32[]{:S(2)}, u32[]{:S(2)}) collective-permute-start(f32[96,128]{1,0:T(8,128)S(1)} %add.48.refs_2_), channel_id=1, source_target_pairs={{0,4},{1,5},{2,6},{3,7},{4,0},{5,1},{6,2},{7,3},{8,12},{9,13},{10,... | collective-permute-start | bytes 147464 | tf_op jit(solution)/shard_map/ppermute | solution.py:352
  29.3 3.1 %collective-permute-done.7.got = f32[128,128]{1,0:T(8,128)S(1)} collective-permute-done((f32[128,128]{1,0:T(8,128)S(1)}, f32[128,128]{1,0:T(8,128)S(1)}, u32[]{:S(2)}, u32[]{:S(2)}) %collective-permute-start.7) | collective-permute-done | bytes 65568 | tf_op jit(solution)/shard_map/ppermute | solution.py:352
  32.4 2.0 %leaf.1 = (f32[128,128]{1,0:T(8,128)S(1)}, bf16[128,64]{1,0:T(8,128)(2,1)S(1)}) custom-call(f32[128,128]{1,0:T(8,128)S(1)} %add.46.near, f32[128,128]{1,0:T(8,128)S(1)} %collective-permute-done.7.got), custom_call_target="tpu_custom_call" | custom-call | flops 16777216 | bytes 131072 | tf_op jit(solution)/shard_map/leaf/pallas_call | solution.py:339
  34.4 0.0 collective-permute-done.10.refs_3_
  34.4 2.1 %pair.1.refs_1_ = f32[224,128]{1,0:T(8,128)S(1)} custom-call(f32[128,128]{1,0:T(8,128)S(1)} %get-tuple-element.22.refs_0_, bf16[128,64]{1,0:T(8,128)(2,1)S(1)} %get-tuple-element.23.refs_1_, f32[96,128]{1,0:T(8,128)S(1)} %add.48.refs_2_, f32[96,128]{1,0:T(8,128)S(1)} %collective-permute-done.10.refs_3_), custom_call_target="tpu_custom_call" | custom-call | flops 16777216 | bytes 131072 | tf_op jit(solution)/shard_map/pair/pallas_call | solution.py:339
  36.6 0.0 collective-permute-start.11
  36.6 0.1 pad_add_fusion.refs_0_
  36.6 1.3 %collective-permute-done.11.refs_2_ = f32[224,128]{1,0:T(8,128)S(1)} collective-permute-done((f32[224,128]{1,0:T(8,128)S(1)}, f32[224,128]{1,0:T(8,128)S(1)}, u32[]{:S(2)}, u32[]{:S(2)}) %collective-permute-start.11) | collective-permute-done | bytes 114720 | tf_op jit(solution)/shard_map/ppermute | solution.py:352
  37.9 3.7 %root.1 = (f32[16,256]{1,0:T(8,128)S(1)}, f32[16,256]{1,0:T(8,128)S(1)}) custom-call(s32[3]{0:T(128)S(1)} %pad_add_fusion.refs_0_, f32[224,128]{1,0:T(8,128)S(1)} %pair.1.refs_1_, f32[224,128]{1,0:T(8,128)S(1)} %collective-permute-done.11.refs_2_, bf16[256,256]{1,0:T(8,128)(2,1)S(1)} %get-tuple-element.26.refs_3_), custom_call_target="tpu_custom_call" | custom-call | flops 16777216 | bytes 131072 | tf_op jit(solution)/shard_map/root/pallas_call | solution.py:339
  41.6 1.5 %collective-permute-start.12 = (f32[16,256]{1,0:T(8,128)S(1)}, f32[16,256]{1,0:T(8,128)S(1)}, u32[]{:S(2)}, u32[]{:S(2)}) collective-permute-start(f32[16,256]{1,0:T(8,128)S(1)} %get-tuple-element.28), channel_id=1, source_target_pairs={{0,16},{8,24},{16,0},{24,8},{1,17},{9,25},{17,1},{25,9},{2,18},{10... | collective-permute-start | bytes 49160 | tf_op jit(solution)/shard_map/ppermute | solution.py:352
  43.1 2.2 %collective-permute-done.12 = f32[16,256]{1,0:T(8,128)S(1)} collective-permute-done((f32[16,256]{1,0:T(8,128)S(1)}, f32[16,256]{1,0:T(8,128)S(1)}, u32[]{:S(2)}, u32[]{:S(2)}) %collective-permute-start.12) | collective-permute-done | bytes 16416 | tf_op jit(solution)/shard_map/ppermute | solution.py:352
  45.3 0.1 reshape.15
  45.4 0.6 %copy.10 = bf16[16,4,64]{2,0,1:T(8,128)(2,1)} copy(bf16[16,4,64]{2,1,0:T(4,128)(2,1)S(1)} %reshape.15) | data formatting | bytes 16384 | tf_op jit(solution)/shard_map/reshape | solution.py:412
  (7 shorter events, 0.1 us)
Async XLA Ops:
  0.0 9.8 %copy-start.1 = (s32[8]{0:T(128)S(1)}, s32[8]{0:T(128)}, u32[]{:S(2)}) copy-start(s32[8]{0:T(128)} %param.9) | copy-start | bytes 100
  0.0 10.1 %copy-start = (bf16[4,64,64]{2,1,0:T(8,128)(2,1)S(1)}, bf16[4,64,64]{2,1,0:T(8,128)(2,1)}, u32[]{:S(2)}) copy-start(bf16[4,64,64]{2,1,0:T(8,128)(2,1)} %param.8) | copy-start | bytes 98308
  5.3 6.3 %collective-permute-start = (bf16[128,128]{1,0:T(8,128)(2,1)S(1)}, bf16[128,128]{1,0:T(8,128)(2,1)S(1)}, u32[]{:S(2)}, u32[]{:S(2)}) collective-permute-start(bf16[128,128]{1,0:T(8,128)(2,1)S(1)} %get-tuple-element.18), channel_id=1, source_target_pairs={{0,7},{1,2},{2,1},{3,4},{4,3},{5,6},{6,5},{7,0},{8,15},{9,10},{10,... | collective-permute-start | bytes 98312 | tf_op jit(solution)/shard_map/ppermute | solution.py:367
  9.8 1.7 %collective-permute-start.1 = (bf16[128,128]{1,0:T(8,128)(2,1)S(1)}, bf16[128,128]{1,0:T(8,128)(2,1)S(1)}, u32[]{:S(2)}, u32[]{:S(2)}) collective-permute-start(bf16[128,128]{1,0:T(8,128)(2,1)S(1)} %get-tuple-element.19), channel_id=1, source_target_pairs={{0,1},{1,0},{2,3},{3,2},{4,5},{5,4},{6,7},{7,6},{8,9},{9,8},{10,11... | collective-permute-start | bytes 98312 | tf_op jit(solution)/shard_map/ppermute | solution.py:352
  11.6 5.3 %collective-permute-start.4 = (bf16[128,256]{1,0:T(8,128)(2,1)S(1)}, bf16[128,256]{1,0:T(8,128)(2,1)S(1)}, u32[]{:S(2)}, u32[]{:S(2)}) collective-permute-start(bf16[128,256]{1,0:T(8,128)(2,1)S(1)} %fusion.refs_1_), channel_id=1, source_target_pairs={{0,24},{8,16},{16,8},{24,0},{1,25},{9,17},{17,9},{25,1},{2,26},{10... | collective-permute-start | bytes 196616 | tf_op jit(solution)/shard_map/ppermute | solution.py:352
  14.5 4.3 %collective-permute-start.3 = (bf16[128,256]{1,0:T(8,128)(2,1)S(1)}, bf16[128,256]{1,0:T(8,128)(2,1)S(1)}, u32[]{:S(2)}, u32[]{:S(2)}) collective-permute-start(bf16[128,256]{1,0:T(8,128)(2,1)S(1)} %fusion.refs_1_), channel_id=1, source_target_pairs={{0,16},{8,24},{16,0},{24,8},{1,17},{9,25},{17,1},{25,9},{2,18},{10... | collective-permute-start | bytes 196616 | tf_op jit(solution)/shard_map/ppermute | solution.py:352
  15.0 4.3 %collective-permute-start.2 = (bf16[128,256]{1,0:T(8,128)(2,1)S(1)}, bf16[128,256]{1,0:T(8,128)(2,1)S(1)}, u32[]{:S(2)}, u32[]{:S(2)}) collective-permute-start(bf16[128,256]{1,0:T(8,128)(2,1)S(1)} %fusion.refs_1_), channel_id=1, source_target_pairs={{0,8},{8,0},{16,24},{24,16},{1,9},{9,1},{17,25},{25,17},{2,10},{10... | collective-permute-start | bytes 196616 | tf_op jit(solution)/shard_map/ppermute | solution.py:352
  20.1 1.3 %collective-permute-start.5 = (f32[128,128]{1,0:T(8,128)S(1)}, f32[128,128]{1,0:T(8,128)S(1)}, u32[]{:S(2)}, u32[]{:S(2)}) collective-permute-start(f32[128,128]{1,0:T(8,128)S(1)} %get-tuple-element.21), channel_id=1, source_target_pairs={{0,1},{1,0},{2,3},{3,2},{4,5},{5,4},{6,7},{7,6},{8,9},{9,8},{10,11... | collective-permute-start | bytes 196616 | tf_op jit(solution)/shard_map/ppermute | solution.py:352
  20.2 1.4 %collective-permute-start.8 = (f32[96,128]{1,0:T(8,128)S(1)}, f32[96,128]{1,0:T(8,128)S(1)}, u32[]{:S(2)}, u32[]{:S(2)}) collective-permute-start(f32[96,128]{1,0:T(8,128)S(1)} %get-tuple-element.25), channel_id=1, source_target_pairs={{0,1},{1,0},{2,3},{3,2},{4,5},{5,4},{6,7},{7,6},{8,9},{9,8},{10,11... | collective-permute-start | bytes 147464 | tf_op jit(solution)/shard_map/ppermute | solution.py:352
  21.5 4.7 %collective-permute-start.6 = (f32[128,128]{1,0:T(8,128)S(1)}, f32[128,128]{1,0:T(8,128)S(1)}, u32[]{:S(2)}, u32[]{:S(2)}) collective-permute-start(f32[128,128]{1,0:T(8,128)S(1)} %add.45), channel_id=1, source_target_pairs={{0,2},{1,3},{2,0},{3,1},{4,6},{5,7},{6,4},{7,5},{8,10},{9,11},{10,... | collective-permute-start | bytes 196616 | tf_op jit(solution)/shard_map/ppermute | solution.py:352
  21.6 5.4 %collective-permute-start.9 = (f32[96,128]{1,0:T(8,128)S(1)}, f32[96,128]{1,0:T(8,128)S(1)}, u32[]{:S(2)}, u32[]{:S(2)}) collective-permute-start(f32[96,128]{1,0:T(8,128)S(1)} %add.47), channel_id=1, source_target_pairs={{0,2},{1,3},{2,0},{3,1},{4,6},{5,7},{6,4},{7,5},{8,10},{9,11},{10,... | collective-permute-start | bytes 147464 | tf_op jit(solution)/shard_map/ppermute | solution.py:352
  26.2 6.2 %collective-permute-start.7 = (f32[128,128]{1,0:T(8,128)S(1)}, f32[128,128]{1,0:T(8,128)S(1)}, u32[]{:S(2)}, u32[]{:S(2)}) collective-permute-start(f32[128,128]{1,0:T(8,128)S(1)} %add.46.near), channel_id=1, source_target_pairs={{0,4},{1,5},{2,6},{3,7},{4,0},{5,1},{6,2},{7,3},{8,12},{9,13},{10,... | collective-permute-start | bytes 196616 | tf_op jit(solution)/shard_map/ppermute | solution.py:352
  27.0 7.4 %collective-permute-start.10 = (f32[96,128]{1,0:T(8,128)S(1)}, f32[96,128]{1,0:T(8,128)S(1)}, u32[]{:S(2)}, u32[]{:S(2)}) collective-permute-start(f32[96,128]{1,0:T(8,128)S(1)} %add.48.refs_2_), channel_id=1, source_target_pairs={{0,4},{1,5},{2,6},{3,7},{4,0},{5,1},{6,2},{7,3},{8,12},{9,13},{10,... | collective-permute-start | bytes 147464 | tf_op jit(solution)/shard_map/ppermute | solution.py:352
  36.6 1.3 %collective-permute-start.11 = (f32[224,128]{1,0:T(8,128)S(1)}, f32[224,128]{1,0:T(8,128)S(1)}, u32[]{:S(2)}, u32[]{:S(2)}) collective-permute-start(f32[224,128]{1,0:T(8,128)S(1)} %pair.1.refs_1_), channel_id=1, source_target_pairs={{0,1},{1,0},{2,3},{3,2},{4,5},{5,4},{6,7},{7,6},{8,9},{9,8},{10,11... | collective-permute-start | bytes 344072 | tf_op jit(solution)/shard_map/ppermute | solution.py:352
  41.6 3.8 %collective-permute-start.12 = (f32[16,256]{1,0:T(8,128)S(1)}, f32[16,256]{1,0:T(8,128)S(1)}, u32[]{:S(2)}, u32[]{:S(2)}) collective-permute-start(f32[16,256]{1,0:T(8,128)S(1)} %get-tuple-element.28), channel_id=1, source_target_pairs={{0,16},{8,24},{16,0},{24,8},{1,17},{9,25},{17,1},{25,9},{2,18},{10... | collective-permute-start | bytes 49160 | tf_op jit(solution)/shard_map/ppermute | solution.py:352

commit v7 on v6

--- a/solution.py
+++ b/solution.py
@@ -88,6 +88,14 @@
     small[0].wait()
     small[1].wait()
     fields[...] = raw[...].astype(F32)
+    late = []
+
+    def keep_rows(rank, both):
+        both = both[:edges] + both[edges:]
+        for k in range(2):
+            at = (rank + k) * edges
+            rows[at : at + edges, :] = both[:, k * fine_z : (k + 1) * fine_z]
+
     for i in range(chunks):
         g = i * groups // chunks
         arrival(i).wait()
@@ -108,10 +116,10 @@
             both = jnp.concatenate(
                 [jnp.concatenate(high[k] + low[k], axis=0) for k in range(2)], axis=1
             )
-            both = dot(weights_xy[...], both)
-            both = both[:edges] + both[edges:]
-            for k, rank in enumerate((first, second)):
-                rows[rank * edges : (rank + 1) * edges, :] = both[:, k * fine_z : (k + 1) * fine_z]
+            late.append((first, dot(weights_xy[...], both)))
+            if len(late) > 1:
+                keep_rows(*late.pop(0))
+    keep_rows(*late.pop(0))
     small[2].wait()
     per = weights_z.shape[0] // fine_z
     lanes = weights_z.shape[1] // 2

time: 46.2 us -> 46.2 us (level)
  no operation moved by 1% of the time
where the time goes in v7:
time: 46.2 us; the launch traced here: 46 us
  starting transfers between devices  15.4 us (33%)
  waiting for transfers between devices  15.3 us (33%)
  Pallas kernels  14 us (30%)
  local copies, waits for them, and re-layouts  0.95 us (2%)
    ppermute x12, waiting for transfers between devices, swap(): lax.ppermute(x, axis, [(i, i ^ mask) for i in range(lax.axis_size(axis))])  14 us
    ppermute x12, starting transfers between devices, swap(): lax.ppermute(x, axis, [(i, i ^ mask) for i in range(lax.axis_size(axis))])  10.8 us
    pallas_call x3, Pallas kernels, local_call(): pl.pallas_call(kernel, in_specs=[smem] * len(scalars) + [vmem] * len(args...  7.85 us
    pallas_call x1, Pallas kernels, restrict(): pl.pallas_call(restrict_kernel, in_specs=[pl.BlockSpec(memory_space=pltpu...  5.24 us
    ppermute x1, starting transfers between devices, body(): from_chip = lax.ppermute(to_chip, 'space', across).astype(F32)  4.55 us
    ppermute x1, waiting for transfers between devices, body(): from_chip = lax.ppermute(to_chip, 'space', across).astype(F32)  1.28 us
  transfers between devices with their start and end apart: 13, of which 9 were waited for; matrix products, arithmetic and copies ran while one was open for 1% of the time, Pallas kernels for 4%

profile of v7, /device:TPU:0, one launch (start us, length us, event | category | flops | bytes accessed | tf_op | source)
XLA Modules:
  0.0 46.0 jit_solution(17146603667986864022)
XLA Ops:
  0.0 0.0 copy-start.1
  0.0 0.0 copy-start
  0.0 5.2 %restrict.1 = (f32[128,256]{1,0:T(8,128)S(1)}, bf16[128,128]{1,0:T(8,128)(2,1)S(1)}, bf16[128,128]{1,0:T(8,128)(2,1)S(1)}) custom-call(s32[1]{0:T(128)} %bitcast.side, bf16[32768,128]{1,0:T(8,128)(2,1)} %bitcast.9, bf16[2,256,128]{2,1,0:T(8,128)(2,1)} %bitcast.10, bf16[32,256]{1,0:T(8,128)(2,1)} %constant.74.table_xy, bf16[512,256]{1,0:T(8,128)(2,1)} %constant.79.table_z), custom_call_target="tpu_custom_call" | custom-call | tf_op jit(solution)/shard_map/restrict/pallas_call | solution.py:159
  5.3 4.6 %collective-permute-start = (bf16[128,128]{1,0:T(8,128)(2,1)S(1)}, bf16[128,128]{1,0:T(8,128)(2,1)S(1)}, u32[]{:S(2)}, u32[]{:S(2)}) collective-permute-start(bf16[128,128]{1,0:T(8,128)(2,1)S(1)} %get-tuple-element.18), channel_id=1, source_target_pairs={{0,7},{1,2},{2,1},{3,4},{4,3},{5,6},{6,5},{7,0},{8,15},{9,10},{10,... | collective-permute-start | bytes 98312 | tf_op jit(solution)/shard_map/ppermute | solution.py:375
  9.8 0.0 collective-permute-start.1
  9.8 0.0 copy-done.1
  9.8 0.1 dynamic_slice.6
  9.9 0.1 pad_add_fusion.1
  10.0 0.1 fusion.1
  10.1 0.0 copy-done
  10.1 0.1 copy.7
  10.1 0.1 reshape.14.refs_5_
  10.2 1.3 %collective-permute-done = bf16[128,128]{1,0:T(8,128)(2,1)S(1)} collective-permute-done((bf16[128,128]{1,0:T(8,128)(2,1)S(1)}, bf16[128,128]{1,0:T(8,128)(2,1)S(1)}, u32[]{:S(2)}, u32[]{:S(2)}) %collective-permute-start) | collective-permute-done | bytes 32800 | tf_op jit(solution)/shard_map/ppermute | solution.py:375
  11.5 0.0 collective-permute-done.1
  11.6 2.9 %collective-permute-start.4 = (bf16[128,256]{1,0:T(8,128)(2,1)S(1)}, bf16[128,256]{1,0:T(8,128)(2,1)S(1)}, u32[]{:S(2)}, u32[]{:S(2)}) collective-permute-start(bf16[128,256]{1,0:T(8,128)(2,1)S(1)} %fusion.refs_1_), channel_id=1, source_target_pairs={{0,24},{8,16},{16,8},{24,0},{1,25},{9,17},{17,9},{25,1},{2,26},{10... | collective-permute-start | bytes 196616 | tf_op jit(solution)/shard_map/ppermute | solution.py:360
  14.5 0.5 %collective-permute-start.3 = (bf16[128,256]{1,0:T(8,128)(2,1)S(1)}, bf16[128,256]{1,0:T(8,128)(2,1)S(1)}, u32[]{:S(2)}, u32[]{:S(2)}) collective-permute-start(bf16[128,256]{1,0:T(8,128)(2,1)S(1)} %fusion.refs_1_), channel_id=1, source_target_pairs={{0,16},{8,24},{16,0},{24,8},{1,17},{9,25},{17,1},{25,9},{2,18},{10... | collective-permute-start | bytes 196616 | tf_op jit(solution)/shard_map/ppermute | solution.py:360
  15.0 0.1 collective-permute-start.2
  15.1 0.1 pad_add_fusion.2.refs_0_
  15.2 1.7 %collective-permute-done.4.refs_4_ = bf16[128,256]{1,0:T(8,128)(2,1)S(1)} collective-permute-done((bf16[128,256]{1,0:T(8,128)(2,1)S(1)}, bf16[128,256]{1,0:T(8,128)(2,1)S(1)}, u32[]{:S(2)}, u32[]{:S(2)}) %collective-permute-start.4) | collective-permute-done | bytes 65568 | tf_op jit(solution)/shard_map/ppermute | solution.py:360
  16.9 1.8 %collective-permute-done.3.refs_3_ = bf16[128,256]{1,0:T(8,128)(2,1)S(1)} collective-permute-done((bf16[128,256]{1,0:T(8,128)(2,1)S(1)}, bf16[128,256]{1,0:T(8,128)(2,1)S(1)}, u32[]{:S(2)}, u32[]{:S(2)}) %collective-permute-start.3) | collective-permute-done | bytes 65568 | tf_op jit(solution)/shard_map/ppermute | solution.py:360
  18.7 0.5 %collective-permute-done.2.refs_2_ = bf16[128,256]{1,0:T(8,128)(2,1)S(1)} collective-permute-done((bf16[128,256]{1,0:T(8,128)(2,1)S(1)}, bf16[128,256]{1,0:T(8,128)(2,1)S(1)}, u32[]{:S(2)}, u32[]{:S(2)}) %collective-permute-start.2) | collective-permute-done | bytes 65568 | tf_op jit(solution)/shard_map/ppermute | solution.py:360
  19.2 0.9 %products.1 = (bf16[256,256]{1,0:T(8,128)(2,1)S(1)}, f32[128,128]{1,0:T(8,128)S(1)}, f32[128,128]{1,0:T(8,128)S(1)}, f32[96,128]{1,0:T(8,128)S(1)}, f32[96,128]{1,0:T(8,128)S(1)}) custom-call(s32[5]{0:T(128)S(1)} %pad_add_fusion.2.refs_0_, bf16[128,256]{1,0:T(8,128)(2,1)S(1)} %fusion.refs_1_, bf16[128,256]{1,0:T(8,128)(2,1)S(1)} %collective-permute-done.2.refs_2_, ...), custom_call_target="tpu_custom_call" | custom-call | tf_op jit(solution)/shard_map/products/pallas_call | solution.py:227
  20.1 0.1 collective-permute-start.5
  20.2 0.5 %collective-permute-start.8 = (f32[96,128]{1,0:T(8,128)S(1)}, f32[96,128]{1,0:T(8,128)S(1)}, u32[]{:S(2)}, u32[]{:S(2)}) collective-permute-start(f32[96,128]{1,0:T(8,128)S(1)} %get-tuple-element.25), channel_id=1, source_target_pairs={{0,1},{1,0},{2,3},{3,2},{4,5},{5,4},{6,7},{7,6},{8,9},{9,8},{10,11... | collective-permute-start | bytes 147464 | tf_op jit(solution)/shard_map/ppermute | solution.py:360
  20.7 0.7 %collective-permute-done.5 = f32[128,128]{1,0:T(8,128)S(1)} collective-permute-done((f32[128,128]{1,0:T(8,128)S(1)}, f32[128,128]{1,0:T(8,128)S(1)}, u32[]{:S(2)}, u32[]{:S(2)}) %collective-permute-start.5) | collective-permute-done | bytes 65568 | tf_op jit(solution)/shard_map/ppermute | solution.py:360
  21.5 0.1 collective-permute-start.6
  21.5 0.0 collective-permute-done.8
  21.6 2.0 %collective-permute-start.9 = (f32[96,128]{1,0:T(8,128)S(1)}, f32[96,128]{1,0:T(8,128)S(1)}, u32[]{:S(2)}, u32[]{:S(2)}) collective-permute-start(f32[96,128]{1,0:T(8,128)S(1)} %add.47), channel_id=1, source_target_pairs={{0,2},{1,3},{2,0},{3,1},{4,6},{5,7},{6,4},{7,5},{8,10},{9,11},{10,... | collective-permute-start | bytes 147464 | tf_op jit(solution)/shard_map/ppermute | solution.py:360
  23.6 2.6 %collective-permute-done.6 = f32[128,128]{1,0:T(8,128)S(1)} collective-permute-done((f32[128,128]{1,0:T(8,128)S(1)}, f32[128,128]{1,0:T(8,128)S(1)}, u32[]{:S(2)}, u32[]{:S(2)}) %collective-permute-start.6) | collective-permute-done | bytes 65568 | tf_op jit(solution)/shard_map/ppermute | solution.py:360
  26.2 0.8 %collective-permute-start.7 = (f32[128,128]{1,0:T(8,128)S(1)}, f32[128,128]{1,0:T(8,128)S(1)}, u32[]{:S(2)}, u32[]{:S(2)}) collective-permute-start(f32[128,128]{1,0:T(8,128)S(1)} %add.46.near), channel_id=1, source_target_pairs={{0,4},{1,5},{2,6},{3,7},{4,0},{5,1},{6,2},{7,3},{8,12},{9,13},{10,... | collective-permute-start | bytes 196616 | tf_op jit(solution)/shard_map/ppermute | solution.py:360
  27.0 0.0 collective-permute-done.9
  27.0 2.3 %collective-permute-start.10 = (f32[96,128]{1,0:T(8,128)S(1)}, f32[96,128]{1,0:T(8,128)S(1)}, u32[]{:S(2)}, u32[]{:S(2)}) collective-permute-start(f32[96,128]{1,0:T(8,128)S(1)} %add.48.refs_2_), channel_id=1, source_target_pairs={{0,4},{1,5},{2,6},{3,7},{4,0},{5,1},{6,2},{7,3},{8,12},{9,13},{10,... | collective-permute-start | bytes 147464 | tf_op jit(solution)/shard_map/ppermute | solution.py:360
  29.3 3.1 %collective-permute-done.7.got = f32[128,128]{1,0:T(8,128)S(1)} collective-permute-done((f32[128,128]{1,0:T(8,128)S(1)}, f32[128,128]{1,0:T(8,128)S(1)}, u32[]{:S(2)}, u32[]{:S(2)}) %collective-permute-start.7) | collective-permute-done | bytes 65568 | tf_op jit(solution)/shard_map/ppermute | solution.py:360
  32.4 2.0 %leaf.1 = (f32[128,128]{1,0:T(8,128)S(1)}, bf16[128,64]{1,0:T(8,128)(2,1)S(1)}) custom-call(f32[128,128]{1,0:T(8,128)S(1)} %add.46.near, f32[128,128]{1,0:T(8,128)S(1)} %collective-permute-done.7.got), custom_call_target="tpu_custom_call" | custom-call | flops 16777216 | bytes 131072 | tf_op jit(solution)/shard_map/leaf/pallas_call | solution.py:347
  34.4 0.0 collective-permute-done.10.refs_3_
  34.4 2.1 %pair.1.refs_1_ = f32[224,128]{1,0:T(8,128)S(1)} custom-call(f32[128,128]{1,0:T(8,128)S(1)} %get-tuple-element.22.refs_0_, bf16[128,64]{1,0:T(8,128)(2,1)S(1)} %get-tuple-element.23.refs_1_, f32[96,128]{1,0:T(8,128)S(1)} %add.48.refs_2_, f32[96,128]{1,0:T(8,128)S(1)} %collective-permute-done.10.refs_3_), custom_call_target="tpu_custom_call" | custom-call | flops 16777216 | bytes 131072 | tf_op jit(solution)/shard_map/pair/pallas_call | solution.py:347
  36.6 0.0 collective-permute-start.11
  36.6 0.1 pad_add_fusion.refs_0_
  36.6 1.3 %collective-permute-done.11.refs_2_ = f32[224,128]{1,0:T(8,128)S(1)} collective-permute-done((f32[224,128]{1,0:T(8,128)S(1)}, f32[224,128]{1,0:T(8,128)S(1)}, u32[]{:S(2)}, u32[]{:S(2)}) %collective-permute-start.11) | collective-permute-done | bytes 114720 | tf_op jit(solution)/shard_map/ppermute | solution.py:360
  37.9 3.7 %root.1 = (f32[16,256]{1,0:T(8,128)S(1)}, f32[16,256]{1,0:T(8,128)S(1)}) custom-call(s32[3]{0:T(128)S(1)} %pad_add_fusion.refs_0_, f32[224,128]{1,0:T(8,128)S(1)} %pair.1.refs_1_, f32[224,128]{1,0:T(8,128)S(1)} %collective-permute-done.11.refs_2_, bf16[256,256]{1,0:T(8,128)(2,1)S(1)} %get-tuple-element.26.refs_3_), custom_call_target="tpu_custom_call" | custom-call | flops 16777216 | bytes 131072 | tf_op jit(solution)/shard_map/root/pallas_call | solution.py:347
  41.6 1.5 %collective-permute-start.12 = (f32[16,256]{1,0:T(8,128)S(1)}, f32[16,256]{1,0:T(8,128)S(1)}, u32[]{:S(2)}, u32[]{:S(2)}) collective-permute-start(f32[16,256]{1,0:T(8,128)S(1)} %get-tuple-element.28), channel_id=1, source_target_pairs={{0,16},{8,24},{16,0},{24,8},{1,17},{9,25},{17,1},{25,9},{2,18},{10... | collective-permute-start | bytes 49160 | tf_op jit(solution)/shard_map/ppermute | solution.py:360
  43.1 2.2 %collective-permute-done.12 = f32[16,256]{1,0:T(8,128)S(1)} collective-permute-done((f32[16,256]{1,0:T(8,128)S(1)}, f32[16,256]{1,0:T(8,128)S(1)}, u32[]{:S(2)}, u32[]{:S(2)}) %collective-permute-start.12) | collective-permute-done | bytes 16416 | tf_op jit(solution)/shard_map/ppermute | solution.py:360
  45.3 0.1 reshape.15
  45.4 0.6 %copy.10 = bf16[16,4,64]{2,0,1:T(8,128)(2,1)} copy(bf16[16,4,64]{2,1,0:T(4,128)(2,1)S(1)} %reshape.15) | data formatting | bytes 16384 | tf_op jit(solution)/shard_map/reshape | solution.py:420
  (7 shorter events, 0.1 us)
Async XLA Ops:
  0.0 9.8 %copy-start.1 = (s32[8]{0:T(128)S(1)}, s32[8]{0:T(128)}, u32[]{:S(2)}) copy-start(s32[8]{0:T(128)} %param.9) | copy-start | bytes 100
  0.0 10.1 %copy-start = (bf16[4,64,64]{2,1,0:T(8,128)(2,1)S(1)}, bf16[4,64,64]{2,1,0:T(8,128)(2,1)}, u32[]{:S(2)}) copy-start(bf16[4,64,64]{2,1,0:T(8,128)(2,1)} %param.8) | copy-start | bytes 98308
  5.3 6.3 %collective-permute-start = (bf16[128,128]{1,0:T(8,128)(2,1)S(1)}, bf16[128,128]{1,0:T(8,128)(2,1)S(1)}, u32[]{:S(2)}, u32[]{:S(2)}) collective-permute-start(bf16[128,128]{1,0:T(8,128)(2,1)S(1)} %get-tuple-element.18), channel_id=1, source_target_pairs={{0,7},{1,2},{2,1},{3,4},{4,3},{5,6},{6,5},{7,0},{8,15},{9,10},{10,... | collective-permute-start | bytes 98312 | tf_op jit(solution)/shard_map/ppermute | solution.py:375
  9.8 1.7 %collective-permute-start.1 = (bf16[128,128]{1,0:T(8,128)(2,1)S(1)}, bf16[128,128]{1,0:T(8,128)(2,1)S(1)}, u32[]{:S(2)}, u32[]{:S(2)}) collective-permute-start(bf16[128,128]{1,0:T(8,128)(2,1)S(1)} %get-tuple-element.19), channel_id=1, source_target_pairs={{0,1},{1,0},{2,3},{3,2},{4,5},{5,4},{6,7},{7,6},{8,9},{9,8},{10,11... | collective-permute-start | bytes 98312 | tf_op jit(solution)/shard_map/ppermute | solution.py:360
  11.6 5.3 %collective-permute-start.4 = (bf16[128,256]{1,0:T(8,128)(2,1)S(1)}, bf16[128,256]{1,0:T(8,128)(2,1)S(1)}, u32[]{:S(2)}, u32[]{:S(2)}) collective-permute-start(bf16[128,256]{1,0:T(8,128)(2,1)S(1)} %fusion.refs_1_), channel_id=1, source_target_pairs={{0,24},{8,16},{16,8},{24,0},{1,25},{9,17},{17,9},{25,1},{2,26},{10... | collective-permute-start | bytes 196616 | tf_op jit(solution)/shard_map/ppermute | solution.py:360
  14.5 4.3 %collective-permute-start.3 = (bf16[128,256]{1,0:T(8,128)(2,1)S(1)}, bf16[128,256]{1,0:T(8,128)(2,1)S(1)}, u32[]{:S(2)}, u32[]{:S(2)}) collective-permute-start(bf16[128,256]{1,0:T(8,128)(2,1)S(1)} %fusion.refs_1_), channel_id=1, source_target_pairs={{0,16},{8,24},{16,0},{24,8},{1,17},{9,25},{17,1},{25,9},{2,18},{10... | collective-permute-start | bytes 196616 | tf_op jit(solution)/shard_map/ppermute | solution.py:360
  15.0 4.3 %collective-permute-start.2 = (bf16[128,256]{1,0:T(8,128)(2,1)S(1)}, bf16[128,256]{1,0:T(8,128)(2,1)S(1)}, u32[]{:S(2)}, u32[]{:S(2)}) collective-permute-start(bf16[128,256]{1,0:T(8,128)(2,1)S(1)} %fusion.refs_1_), channel_id=1, source_target_pairs={{0,8},{8,0},{16,24},{24,16},{1,9},{9,1},{17,25},{25,17},{2,10},{10... | collective-permute-start | bytes 196616 | tf_op jit(solution)/shard_map/ppermute | solution.py:360
  20.1 1.3 %collective-permute-start.5 = (f32[128,128]{1,0:T(8,128)S(1)}, f32[128,128]{1,0:T(8,128)S(1)}, u32[]{:S(2)}, u32[]{:S(2)}) collective-permute-start(f32[128,128]{1,0:T(8,128)S(1)} %get-tuple-element.21), channel_id=1, source_target_pairs={{0,1},{1,0},{2,3},{3,2},{4,5},{5,4},{6,7},{7,6},{8,9},{9,8},{10,11... | collective-permute-start | bytes 196616 | tf_op jit(solution)/shard_map/ppermute | solution.py:360
  20.2 1.4 %collective-permute-start.8 = (f32[96,128]{1,0:T(8,128)S(1)}, f32[96,128]{1,0:T(8,128)S(1)}, u32[]{:S(2)}, u32[]{:S(2)}) collective-permute-start(f32[96,128]{1,0:T(8,128)S(1)} %get-tuple-element.25), channel_id=1, source_target_pairs={{0,1},{1,0},{2,3},{3,2},{4,5},{5,4},{6,7},{7,6},{8,9},{9,8},{10,11... | collective-permute-start | bytes 147464 | tf_op jit(solution)/shard_map/ppermute | solution.py:360
  21.5 4.7 %collective-permute-start.6 = (f32[128,128]{1,0:T(8,128)S(1)}, f32[128,128]{1,0:T(8,128)S(1)}, u32[]{:S(2)}, u32[]{:S(2)}) collective-permute-start(f32[128,128]{1,0:T(8,128)S(1)} %add.45), channel_id=1, source_target_pairs={{0,2},{1,3},{2,0},{3,1},{4,6},{5,7},{6,4},{7,5},{8,10},{9,11},{10,... | collective-permute-start | bytes 196616 | tf_op jit(solution)/shard_map/ppermute | solution.py:360
  21.6 5.4 %collective-permute-start.9 = (f32[96,128]{1,0:T(8,128)S(1)}, f32[96,128]{1,0:T(8,128)S(1)}, u32[]{:S(2)}, u32[]{:S(2)}) collective-permute-start(f32[96,128]{1,0:T(8,128)S(1)} %add.47), channel_id=1, source_target_pairs={{0,2},{1,3},{2,0},{3,1},{4,6},{5,7},{6,4},{7,5},{8,10},{9,11},{10,... | collective-permute-start | bytes 147464 | tf_op jit(solution)/shard_map/ppermute | solution.py:360
  26.2 6.2 %collective-permute-start.7 = (f32[128,128]{1,0:T(8,128)S(1)}, f32[128,128]{1,0:T(8,128)S(1)}, u32[]{:S(2)}, u32[]{:S(2)}) collective-permute-start(f32[128,128]{1,0:T(8,128)S(1)} %add.46.near), channel_id=1, source_target_pairs={{0,4},{1,5},{2,6},{3,7},{4,0},{5,1},{6,2},{7,3},{8,12},{9,13},{10,... | collective-permute-start | bytes 196616 | tf_op jit(solution)/shard_map/ppermute | solution.py:360
  27.0 7.4 %collective-permute-start.10 = (f32[96,128]{1,0:T(8,128)S(1)}, f32[96,128]{1,0:T(8,128)S(1)}, u32[]{:S(2)}, u32[]{:S(2)}) collective-permute-start(f32[96,128]{1,0:T(8,128)S(1)} %add.48.refs_2_), channel_id=1, source_target_pairs={{0,4},{1,5},{2,6},{3,7},{4,0},{5,1},{6,2},{7,3},{8,12},{9,13},{10,... | collective-permute-start | bytes 147464 | tf_op jit(solution)/shard_map/ppermute | solution.py:360
  36.6 1.3 %collective-permute-start.11 = (f32[224,128]{1,0:T(8,128)S(1)}, f32[224,128]{1,0:T(8,128)S(1)}, u32[]{:S(2)}, u32[]{:S(2)}) collective-permute-start(f32[224,128]{1,0:T(8,128)S(1)} %pair.1.refs_1_), channel_id=1, source_target_pairs={{0,1},{1,0},{2,3},{3,2},{4,5},{5,4},{6,7},{7,6},{8,9},{9,8},{10,11... | collective-permute-start | bytes 344072 | tf_op jit(solution)/shard_map/ppermute | solution.py:360
  41.6 3.8 %collective-permute-start.12 = (f32[16,256]{1,0:T(8,128)S(1)}, f32[16,256]{1,0:T(8,128)S(1)}, u32[]{:S(2)}, u32[]{:S(2)}) collective-permute-start(f32[16,256]{1,0:T(8,128)S(1)} %get-tuple-element.28), channel_id=1, source_target_pairs={{0,16},{8,24},{16,0},{24,8},{1,17},{9,25},{17,1},{25,9},{2,18},{10... | collective-permute-start | bytes 49160 | tf_op jit(solution)/shard_map/ppermute | solution.py:360
